TPU v7x, 32 devices: a whole 2x2x4 slice. The times are simulated.
32 devices in a mesh: dp: 2 (over core), expert: 16 (over z, y, x).
Axes of the slice: x: 2, y: 2, z: 4, core: 2. Of those that a mesh axis runs over, the one named last changes fastest.
Arguments:
- tokens: bfloat16 [2048, 3584], P('expert', 'dp'), may hold values from -6 to 6
- out_grad: bfloat16 [2048, 3584], P('expert', 'dp'), may hold values from -6 to 6
- gate_up_weight: bfloat16 [16, 3584, 2048], P('expert', 'dp'), may hold values from -0.09375 to 0.09375
- down_weight: bfloat16 [16, 1024, 3584], P('expert', None, 'dp'), may hold values from -0.1875 to 0.1875
- routes: int32 [2048, 2], P('expert'), may hold values from 0 to 15, all different within a row; in each aligned block of 128 rows (0 to 127, 128 to 255, ...) at most 32 rows name the same one
- route_weight: float32 [2048, 2], P('expert'), may hold values from 0.1 to 1
- swapped: int32 [4], replicated, may hold values from 0 to 7, as said below
Outputs:
- layer_out: bfloat16 [2048, 3584], P('expert', 'dp')
- token_grad: bfloat16 [2048, 3584], P('expert', 'dp')
- down_grad: bfloat16 [16, 1024, 3584], P('expert', None, 'dp')
Inputs may be any that keep to these rules, and one draw needn't show every extreme that they name: `routes`: among the rows of each block of 128 consecutive tokens, no expert is named more than 32 times, a bound that some block reaches; a token names different experts. `swapped`: 4 different device numbers; device 0 and device 8 - 1 are always among them.
All inputs are finite; a program needn't handle non-finite values.
Results may differ from a plain program's by a relative error of at most 0.023.
Values may be sent and summed in bfloat16 or wider, within the bound.
No kernel may reach another device: no remote copies, remote signals or barrier semaphores. Data moves between devices by JAX's collectives and lax.ppermute only.
A program may use at most 64 MiB of HBM per device.

v0:
```python
import jax
import jax.numpy as jnp
from jax import lax
from jax.sharding import PartitionSpec as P


def shifted(block, axis, distance):
    devices = range(lax.axis_size(axis))
    route = [((i - distance) % len(devices), i) for i in devices]
    return lax.ppermute(block, axis, route)


def gate_grads(gate_val, up_val, hidden_grad):
    sig = jax.nn.sigmoid(gate_val)
    act = gate_val * sig
    gate_grad = hidden_grad * up_val * sig * (1.0 + gate_val * (1.0 - sig))
    up_grad = hidden_grad * act
    return (gate_grad, up_grad)


def on_device(tokens, out_grad, gate_up_weight, down_weight, routes, route_weight, swapped):
    experts = lax.axis_size("expert")
    half = experts // 2
    token_count = tokens.shape[0]
    width_block = tokens.shape[1]
    top_count = routes.shape[1]
    hidden_width = down_weight.shape[1]
    capacity = max(2, 2 * token_count * top_count // experts)
    row_count = token_count * top_count
    buffer_rows = experts * capacity
    device_id = lax.axis_index("expert")
    moved = jnp.any(swapped[:, None] == jnp.arange(half, dtype=jnp.int32)[None, :], axis=0)
    self_moved = moved[device_id % half]
    flat = routes.reshape(-1)
    onehot = (flat[:, None] == jnp.arange(experts, dtype=jnp.int32)[None, :]).astype(jnp.int32)
    slot = jnp.sum(jnp.cumsum(onehot, axis=0) * onehot, axis=1) - 1
    spot = flat * capacity + slot
    row_grad = (route_weight[:, :, None] * out_grad[:, None, :].astype(jnp.float32)).astype(
        jnp.bfloat16
    )
    row_grad = row_grad.reshape(row_count, width_block)
    token_rows = jnp.repeat(tokens, top_count, axis=0)
    send_tokens = jnp.zeros((buffer_rows, width_block), jnp.bfloat16).at[spot].set(token_rows)
    send_grads = jnp.zeros((buffer_rows, width_block), jnp.bfloat16).at[spot].set(row_grad)
    recv_tokens, recv_grads = (
        lax.all_to_all(
            send_tokens.reshape(experts, capacity, width_block),
            "expert",
            split_axis=0,
            concat_axis=0,
            tiled=True,
        ),
        lax.all_to_all(
            send_grads.reshape(experts, capacity, width_block),
            "expert",
            split_axis=0,
            concat_axis=0,
            tiled=True,
        ),
    )
    recv_tokens = recv_tokens.reshape(buffer_rows, width_block)
    recv_grads = recv_grads.reshape(buffer_rows, width_block)
    local_gate_up = gate_up_weight[0]
    local_down = down_weight[0]
    gate_up_part = jnp.dot(recv_tokens, local_gate_up, preferred_element_type=jnp.float32)
    gate_up = lax.psum(gate_up_part.astype(jnp.bfloat16), "dp").astype(jnp.float32)
    gate_val = gate_up[:, :hidden_width]
    up_val = gate_up[:, hidden_width:]
    hidden = (jax.nn.silu(gate_val) * up_val).astype(jnp.bfloat16)
    row_out = jnp.dot(hidden, local_down, preferred_element_type=jnp.float32).astype(jnp.bfloat16)
    row_out = row_out.reshape(experts, capacity, width_block)
    back_out = lax.all_to_all(row_out, "expert", split_axis=0, concat_axis=0, tiled=True)
    hidden_part = lax.dot_general(
        recv_grads, local_down, (((1,), (1,)), ((), ())), preferred_element_type=jnp.float32
    )
    hidden_grad = lax.psum(hidden_part.astype(jnp.bfloat16), "dp").astype(jnp.float32)
    gate_grad, up_grad = gate_grads(gate_val, up_val, hidden_grad)
    gate_up_grad = jnp.concatenate([gate_grad, up_grad], axis=1).astype(jnp.bfloat16)
    row_dx = lax.dot_general(
        gate_up_grad, local_gate_up, (((1,), (1,)), ((), ())), preferred_element_type=jnp.float32
    ).astype(jnp.bfloat16)
    row_dx = row_dx.reshape(experts, capacity, width_block)
    expert_grad = lax.dot_general(
        hidden, recv_grads, (((0,), (0,)), ((), ())), preferred_element_type=jnp.float32
    ).astype(jnp.bfloat16)
    moved_grad = shifted(expert_grad, "expert", half)
    down_grad = jnp.where(self_moved, moved_grad, expert_grad)[None]
    back_dx = lax.all_to_all(row_dx, "expert", split_axis=0, concat_axis=0, tiled=True)
    out_rows = back_out.reshape(buffer_rows, width_block)[spot].reshape(
        token_count, top_count, width_block
    )
    dx_rows = back_dx.reshape(buffer_rows, width_block)[spot].reshape(
        token_count, top_count, width_block
    )
    layer_out = jnp.sum(route_weight[:, :, None] * out_rows.astype(jnp.float32), axis=1).astype(
        jnp.bfloat16
    )
    token_grad = jnp.sum(dx_rows.astype(jnp.float32), axis=1).astype(jnp.bfloat16)
    return (layer_out, token_grad, down_grad)


def solution(mesh):
    return jax.shard_map(
        on_device,
        mesh=mesh,
        in_specs=(
            P("expert", "dp"),
            P("expert", "dp"),
            P("expert", "dp", None),
            P("expert", None, "dp"),
            P("expert", None),
            P("expert", None),
            P(),
        ),
        out_specs=(P("expert", "dp"), P("expert", "dp"), P("expert", None, "dp")),
        check_vma=False,
    )
```

profile of v0, /device:TPU:0, one launch (start us, length us, event | category | flops | bytes accessed | tf_op | source)
XLA Modules:
  0.0 415.8 jit_solution(1098616244020266082)
XLA Ops:
  7.2 0.7 broadcast_multiply_fusion
  7.8 0.8 copy.19
  10.1 1.5 broadcast_in_dim.4
  12.0 3.4 scatter_custom_fusion
  15.4 8.5 %all-to-all-start = ((bf16[16,32,1792]{2,1,0:T(8,128)(2,1)}), bf16[16,32,1792]{2,1,0:T(8,128)(2,1)}, u32[]{:S(2)}, u32[]{:S(2)}) async-start(bf16[16,32,1792]{2,1,0:T(8,128)(2,1)} %bitcast.3), calls=%async_computation | async-start | bytes 3670016 | tf_op jit(solution)/shard_map/all_to_all | solution.py:46
  23.9 1.7 mul.78
  25.6 2.6 mul.79
  28.4 3.5 scatter_custom_fusion.1
  31.9 30.6 %all-to-all-done = bf16[16,32,1792]{2,1,0:T(8,128)(2,1)} async-done(((bf16[16,32,1792]{2,1,0:T(8,128)(2,1)}), bf16[16,32,1792]{2,1,0:T(8,128)(2,1)}, u32[]{:S(2)}, u32[]{:S(2)}) %all-to-all-start) | async-done | bytes 1835040 | tf_op jit(solution)/shard_map/all_to_all | solution.py:46
  62.5 8.8 %all-to-all-start.2 = ((bf16[16,32,1792]{2,1,0:T(8,128)(2,1)}), bf16[16,32,1792]{2,1,0:T(8,128)(2,1)S(1)}, u32[]{:S(2)}, u32[]{:S(2)}) async-start(bf16[16,32,1792]{2,1,0:T(8,128)(2,1)} %bitcast.9), calls=%async_computation.2 | async-start | bytes 3670016 | tf_op jit(solution)/shard_map/all_to_all | solution.py:53
  71.6 8.9 %fusion.11 = bf16[512,2048]{1,0:T(8,128)(2,1)} fusion(bf16[512,1792]{1,0:T(8,128)(2,1)} %bitcast.4, bf16[1,1792,2048]{2,1,0:T(8,128)(2,1)} %param.9), kind=kOutput, calls=%fused_computation.15 | convolution fusion | flops 3759144960 | bytes 11272192 | tf_op jit(solution)/shard_map/dot_general | solution.py:65
  80.5 28.9 %all-to-all-done.2 = bf16[16,32,1792]{2,1,0:T(8,128)(2,1)S(1)} async-done(((bf16[16,32,1792]{2,1,0:T(8,128)(2,1)}), bf16[16,32,1792]{2,1,0:T(8,128)(2,1)S(1)}, u32[]{:S(2)}, u32[]{:S(2)}) %all-to-all-start.2) | async-done | bytes 1835040 | tf_op jit(solution)/shard_map/all_to_all | solution.py:53
  109.5 5.8 %fusion.25 = bf16[512,1024]{1,0:T(8,128)(2,1)} fusion(bf16[512,1792]{1,0:T(8,128)(2,1)S(1)} %bitcast.53, bf16[1,1024,1792]{2,1,0:T(8,128)(2,1)} %param.10), kind=kOutput, calls=%fused_computation.31 | convolution fusion | flops 1879572480 | bytes 6553600 | tf_op jit(solution)/shard_map/dot_general | solution.py:73
  115.3 26.3 %all-reduce.3.cloned.1.call-done = (bf16[512,2048]{1,0:T(8,128)(2,1)}, bf16[512,1024]{1,0:T(8,128)(2,1)}) async-done(((bf16[512,2048]{1,0:T(8,128)(2,1)}, bf16[512,1024]{1,0:T(8,128)(2,1)}), (bf16[512,2048]{1,0:T(8,128)(2,1)}, bf16[512,1024]{1,0:T(8,128)(2,1)})) %all-reduce.3.cloned.1.call-update) | async-done | bytes 3145744 | tf_op jit(solution)/shard_map/psum | solution.py:66
  141.6 2.2 convert_element_type.51
  143.8 2.8 fusion.19
  146.6 3.3 fusion.8
  149.9 6.8 %all-to-all-start.1 = ((bf16[16,32,1792]{2,1,0:T(8,128)(2,1)}), bf16[16,32,1792]{2,1,0:T(8,128)(2,1)S(1)}, u32[]{:S(2)}, u32[]{:S(2)}) async-start(bf16[16,32,1792]{2,1,0:T(8,128)(2,1)} %bitcast.55), calls=%async_computation.1 | async-start | bytes 3670016 | tf_op jit(solution)/shard_map/all_to_all | solution.py:72
  156.7 9.0 %fusion.14 = bf16[512,1792]{1,0:T(8,128)(2,1)} fusion(bf16[1,1792,2048]{2,1,0:T(8,128)(2,1)} %param.9, bf16[512,1024]{1,0:T(8,128)(2,1)} %get-tuple-element.6, bf16[512,1024]{1,0:T(8,128)(2,1)} %get-tuple-element.5), kind=kOutput, calls=%fused_computation.16 | convolution fusion | flops 3763208192 | bytes 11272192 | tf_op jit(solution)/shard_map/dot_general | solution.py:79
  165.7 29.8 %all-to-all-done.1 = bf16[16,32,1792]{2,1,0:T(8,128)(2,1)S(1)} async-done(((bf16[16,32,1792]{2,1,0:T(8,128)(2,1)}), bf16[16,32,1792]{2,1,0:T(8,128)(2,1)S(1)}, u32[]{:S(2)}, u32[]{:S(2)}) %all-to-all-start.1) | async-done | bytes 1835040 | tf_op jit(solution)/shard_map/all_to_all | solution.py:72
  195.5 9.3 %all-to-all-start.3 = ((bf16[16,32,1792]{2,1,0:T(8,128)(2,1)}), bf16[16,32,1792]{2,1,0:T(8,128)(2,1)}, u32[]{:S(2)}, u32[]{:S(2)}) async-start(bf16[16,32,1792]{2,1,0:T(8,128)(2,1)} %bitcast.52), calls=%async_computation.3 | async-start | bytes 3670016 | tf_op jit(solution)/shard_map/all_to_all | solution.py:88
  204.8 5.5 %convolution_convert_fusion = bf16[1024,1792]{1,0:T(8,128)(2,1)} fusion(bf16[512,1024]{1,0:T(8,128)(2,1)S(1)} %get-tuple-element.7, bf16[512,1792]{1,0:T(8,128)(2,1)} %bitcast.54), kind=kOutput, calls=%fused_computation.8 | convolution fusion | flops 1880883200 | bytes 6553600 | tf_op jit(solution)/shard_map/dot_general | solution.py:83
  210.3 2.8 collective-permute-start
  213.8 1.3 gather_fusion
  215.2 0.9 reshape.108
  216.1 105.6 %all-to-all-done.3 = bf16[16,32,1792]{2,1,0:T(8,128)(2,1)} async-done(((bf16[16,32,1792]{2,1,0:T(8,128)(2,1)}), bf16[16,32,1792]{2,1,0:T(8,128)(2,1)}, u32[]{:S(2)}, u32[]{:S(2)}) %all-to-all-start.3) | async-done | bytes 1835040 | tf_op jit(solution)/shard_map/all_to_all | solution.py:88
  321.7 3.9 gather_fusion.1
  325.6 1.3 reshape.107
  326.9 4.2 %reduce_sum.32 = bf16[128,1792]{1,0:T(8,128)(2,1)} reduce(bf16[128,2,1792]{2,1,0:T(2,128)(2,1)} %reshape.107, bf16[]{:T(256)} %constant.16.clone.1), dimensions={1}, to_apply=%region_8.9 | reduce | flops 229376 | bytes 1376258 | tf_op jit(solution)/shard_map/reduce_sum | solution.py:98
  331.0 3.3 multiply_reduce_fusion
  334.4 69.7 %collective-permute-done = bf16[1024,1792]{1,0:T(8,128)(2,1)} collective-permute-done((bf16[1024,1792]{1,0:T(8,128)(2,1)}, bf16[1024,1792]{1,0:T(8,128)(2,1)}, u32[]{:S(2)}, u32[]{:S(2)}) %collective-permute-start) | collective-permute-done | bytes 3670048 | tf_op jit(solution)/shard_map/ppermute | solution.py:10
  404.1 4.9 %select_bitcast_fusion = bf16[1,1024,1792]{2,1,0:T(8,128)(2,1)} fusion(bf16[1024,1792]{1,0:T(8,128)(2,1)} %collective-permute-done, bf16[1024,1792]{1,0:T(8,128)(2,1)} %convolution_convert_fusion, pred[]{:T(512)} %bitcast.13), kind=kLoop, calls=%fused_computation.13 | loop fusion | flops 1835008 | bytes 11010049 | tf_op jit(solution)/shard_map/broadcast_in_dim | solution.py:87
  (32 shorter events, 3.1 us)
Async XLA Ops:
  15.4 8.5 %copy-start.2 = (bf16[128,1792]{1,0:T(8,128)(2,1)S(1)}, bf16[128,1792]{1,0:T(8,128)(2,1)}, u32[]{:S(2)}) copy-start(bf16[128,1792]{1,0:T(8,128)(2,1)} %param.8) | copy-start | bytes 1376260
  15.4 47.1 %all-to-all-start = ((bf16[16,32,1792]{2,1,0:T(8,128)(2,1)}), bf16[16,32,1792]{2,1,0:T(8,128)(2,1)}, u32[]{:S(2)}, u32[]{:S(2)}) async-start(bf16[16,32,1792]{2,1,0:T(8,128)(2,1)} %bitcast.3), calls=%async_computation | async-start | bytes 3670016 | tf_op jit(solution)/shard_map/all_to_all | solution.py:46
  25.6 2.6 copy-start.3
  62.5 46.9 %all-to-all-start.2 = ((bf16[16,32,1792]{2,1,0:T(8,128)(2,1)}), bf16[16,32,1792]{2,1,0:T(8,128)(2,1)S(1)}, u32[]{:S(2)}, u32[]{:S(2)}) async-start(bf16[16,32,1792]{2,1,0:T(8,128)(2,1)} %bitcast.9), calls=%async_computation.2 | async-start | bytes 3670016 | tf_op jit(solution)/shard_map/all_to_all | solution.py:53
  71.4 70.2 %all-reduce.3.cloned.1.call-start = ((), (), s32[]{:S(2)}) async-start(), calls=%async_computation.4 | async-start | bytes 6291456 | tf_op jit(solution)/shard_map/psum | solution.py:66
  109.5 5.8 %copy-start = (bf16[16,32,1792]{2,1,0:T(8,128)(2,1)}, bf16[16,32,1792]{2,1,0:T(8,128)(2,1)S(1)}, u32[]{:S(2)}) copy-start(bf16[16,32,1792]{2,1,0:T(8,128)(2,1)S(1)} %all-to-all-done.2) | copy-start | bytes 5505028
  141.6 2.2 copy-start.1
  143.8 2.8 copy-start.4
  149.9 45.6 %all-to-all-start.1 = ((bf16[16,32,1792]{2,1,0:T(8,128)(2,1)}), bf16[16,32,1792]{2,1,0:T(8,128)(2,1)S(1)}, u32[]{:S(2)}, u32[]{:S(2)}) async-start(bf16[16,32,1792]{2,1,0:T(8,128)(2,1)} %bitcast.55), calls=%async_computation.1 | async-start | bytes 3670016 | tf_op jit(solution)/shard_map/all_to_all | solution.py:72
  195.5 126.2 %all-to-all-start.3 = ((bf16[16,32,1792]{2,1,0:T(8,128)(2,1)}), bf16[16,32,1792]{2,1,0:T(8,128)(2,1)}, u32[]{:S(2)}, u32[]{:S(2)}) async-start(bf16[16,32,1792]{2,1,0:T(8,128)(2,1)} %bitcast.52), calls=%async_computation.3 | async-start | bytes 3670016 | tf_op jit(solution)/shard_map/all_to_all | solution.py:88
  204.8 8.2 %copy-start.5 = (s32[4]{0:T(128)S(1)}, s32[4]{0:T(128)}, u32[]{:S(2)}) copy-start(s32[4]{0:T(128)} %param.13) | copy-start | bytes 52
  210.3 193.8 %collective-permute-start = (bf16[1024,1792]{1,0:T(8,128)(2,1)}, bf16[1024,1792]{1,0:T(8,128)(2,1)}, u32[]{:S(2)}, u32[]{:S(2)}) collective-permute-start(bf16[1024,1792]{1,0:T(8,128)(2,1)} %convolution_convert_fusion), channel_id=1, source_target_pairs={{8,0},{9,1},{10,2},{11,3},{12,4},{13,5},{14,6},{15,7},{0,8},{1,9},... | collective-permute-start | bytes 11010056 | tf_op jit(solution)/shard_map/ppermute | solution.py:10
Sparse Core Ops, SparseCore 0:
  115.4 26.1 all-reduce.2
where the time goes:
time: 417 us; the launch traced here: 416 us
  waiting for transfers between devices  291 us (70%)
  starting transfers between devices  36.5 us (9%)
  matrix products  32.4 us (8%)
  other arithmetic  22.5 us (5%)
  local copies, waits for them, and re-layouts  19.4 us (5%)
  between operations  14.2 us (3%)
    all_to_all x1, waiting for transfers between devices, on_device(): lax.all_to_all(row_dx, 'expert', split_axis=0, concat_axis=0, tiled=True)  106 us
    ppermute x1, waiting for transfers between devices, shifted(): return lax.ppermute(block, axis, route)  69.7 us
    all_to_all x1, waiting for transfers between devices, on_device(): lax.all_to_all(send_tokens.reshape(experts, capacity, width_block), 'expe...  30.6 us
    all_to_all x1, waiting for transfers between devices, on_device(): lax.all_to_all(row_out, 'expert', split_axis=0, concat_axis=0, tiled=True)  29.8 us
    all_to_all x1, waiting for transfers between devices, on_device(): lax.all_to_all(send_grads.reshape(experts, capacity, width_block), 'exper...  28.9 us
    psum x1, waiting for transfers between devices, on_device(): lax.psum(gate_up_part.astype(jnp.bfloat16), 'dp').astype(jnp.float32)  26.3 us
    all_to_all x1, starting transfers between devices, on_device(): lax.all_to_all(row_dx, 'expert', split_axis=0, concat_axis=0, tiled=True)  9.33 us
    dot_general x1, matrix products, on_device(): lax.dot_general(gate_up_grad, local_gate_up, (((1,), (1,)), ((), ())), pr...  8.98 us
  transfers between devices with their start and end apart: 6, of which 6 were waited for; matrix products, arithmetic and copies ran while one was open for 11% of the time, Pallas kernels for 0%

commit v1 on v0

v1 whole, which is shorter than its diff:
```python
import jax
import jax.numpy as jnp
from jax import lax
from jax.sharding import PartitionSpec as P

BF16 = jnp.bfloat16
F32 = jnp.float32


def crossed(block, axis, distance):
    size = lax.axis_size(axis)
    return lax.ppermute(block, axis, [(i, (i + distance) % size) for i in range(size)])


def summed_blocks(part):
    total = part.astype(F32)
    for distance in range(1, lax.axis_size("dp")):
        total = total + crossed(part, "dp", distance).astype(F32)
    return total


def halves_exchange(rows, half):
    groups = [[side * half + j for j in range(half)] for side in range(2)]
    return lax.all_to_all(
        rows, "expert", split_axis=0, concat_axis=0, tiled=True, axis_index_groups=groups
    )


def slots_of(routes, experts):
    ids = jnp.arange(experts, dtype=jnp.int32)
    member = jnp.any(routes[:, :, None] == ids, axis=1)
    count = routes.shape[0]
    before = jnp.arange(count)[:, None] > jnp.arange(count)[None, :]
    place = jnp.dot(before.astype(BF16), member.astype(BF16), preferred_element_type=F32)
    return jnp.where(member, place.astype(jnp.int32), -1)


def chooser(places, first, half, capacity):
    mine = lax.dynamic_slice_in_dim(places, first, half, axis=1)
    return (mine.T[:, None, :] == jnp.arange(capacity)[None, :, None]).astype(F32)


def on_device(tokens, out_grad, gate_up_weight, down_weight, routes, route_weight, swapped):
    experts = lax.axis_size("expert")
    half = experts // 2
    token_count, width = tokens.shape
    top_count = routes.shape[1]
    hidden_width = down_weight.shape[1]
    capacity = max(2, 2 * token_count * top_count // experts)
    n_dp = lax.axis_size("dp")
    me = lax.axis_index("expert")
    side = me // half
    moved = jnp.any(swapped == me % half)

    meta = jnp.concatenate([routes.astype(F32), route_weight], axis=1)
    meta_far = crossed(meta, "expert", half)
    tokens_far = crossed(tokens, "expert", half)
    grad_far = crossed(out_grad, "expert", half)
    routes_far = meta_far[:, :top_count].astype(jnp.int32)
    weight_far = meta_far[:, top_count:]

    places = slots_of(routes, experts)
    places_far = slots_of(routes_far, experts)
    rows = 2 * half * capacity

    def selector(first, swap):
        near = chooser(places, first, half, capacity)
        far = chooser(places_far, first, half, capacity)
        zero = jnp.zeros_like(near)
        both = [jnp.concatenate([near, zero], axis=2), jnp.concatenate([zero, far], axis=2)]
        if swap:
            both = both[::-1]
        return jnp.concatenate(both, axis=1).reshape(rows, 2 * token_count)

    def weights_at(first):
        ids = first + jnp.arange(half, dtype=jnp.int32)

        def table(r, w):
            return jnp.sum(jnp.where(r[:, :, None] == ids, w[:, :, None], 0.0), axis=1)

        return jnp.concatenate([table(routes, route_weight), table(routes_far, weight_far)], axis=0)

    def weighted(sel, first):
        w = weights_at(first).T[:, None, :]
        return (sel.reshape(half, 2 * capacity, 2 * token_count) * w).reshape(sel.shape)

    here = side * half
    there = half - here
    sel = selector(here, False)
    sel_w = weighted(sel, here)
    row_w = jnp.sum(sel_w, axis=1, keepdims=True)
    sel_there = selector(there, True)
    row_w_there = jnp.sum(weighted(sel_there, there), axis=1, keepdims=True)
    sel16 = sel.astype(BF16)

    def pick(s, data):
        return jnp.dot(s.astype(BF16), data, preferred_element_type=F32)

    def exchange(x):
        return halves_exchange(x.reshape(half, 2 * capacity, width), half).reshape(rows, width)

    tokens_both = jnp.concatenate([tokens, tokens_far], axis=0)
    grad_both = jnp.concatenate([out_grad, grad_far], axis=0)
    recv_tokens = exchange(pick(sel16, tokens_both).astype(BF16))
    recv_grads = exchange((pick(sel16, grad_both) * row_w).astype(BF16))

    local_gate_up = gate_up_weight[0]
    local_down = down_weight[0]
    gate_up_part = jnp.dot(recv_tokens, local_gate_up, preferred_element_type=F32).astype(BF16)
    gate_up = summed_blocks(gate_up_part)
    gate_val = gate_up[:, :hidden_width]
    up_val = gate_up[:, hidden_width:]
    sig = jax.nn.sigmoid(gate_val)
    act = gate_val * sig
    hidden = (act * up_val).astype(BF16)
    row_out = jnp.dot(hidden, local_down, preferred_element_type=F32).astype(BF16)
    back_out = exchange(row_out)

    hidden_part = lax.dot_general(
        recv_grads, local_down, (((1,), (1,)), ((), ())), preferred_element_type=F32
    ).astype(BF16)
    hidden_grad = summed_blocks(hidden_part)
    gate_grad = hidden_grad * up_val * sig * (1.0 + gate_val * (1.0 - sig))
    up_grad = hidden_grad * act
    gate_up_grad = jnp.concatenate([gate_grad, up_grad], axis=1).astype(BF16)
    row_dx = lax.dot_general(
        gate_up_grad, local_gate_up, (((1,), (1,)), ((), ())), preferred_element_type=F32
    ).astype(BF16)
    back_dx = exchange(row_dx)

    share = hidden_width // n_dp
    core = lax.axis_index("dp")
    mine = lax.dynamic_slice_in_dim(hidden, core * share, share, axis=1)
    far_share = crossed(mine, "expert", half)
    far_hidden = jnp.zeros_like(hidden)
    for distance in range(n_dp):
        piece = far_share if distance == 0 else crossed(far_share, "dp", distance)
        far_hidden = lax.dynamic_update_slice_in_dim(
            far_hidden, piece, ((core - distance) % n_dp) * share, axis=1
        )
    grads_there = exchange((pick(sel_there, grad_both) * row_w_there).astype(BF16))
    left = jnp.where(moved, far_hidden, hidden)
    right = jnp.where(moved, grads_there, recv_grads)
    down_grad = lax.dot_general(
        left, right, (((0,), (0,)), ((), ())), preferred_element_type=F32
    ).astype(BF16)[None]

    def give(s, data):
        return lax.dot_general(s, data, (((0,), (0,)), ((), ())), preferred_element_type=F32)

    w_hi = sel_w.astype(BF16)
    w_lo = (sel_w - w_hi.astype(F32)).astype(BF16)
    part_out = give(w_hi, back_out) + give(w_lo, back_out)
    part_dx = give(sel16, back_dx)

    def finish(part):
        far = crossed(part[token_count:].astype(BF16), "expert", half)
        return (part[:token_count] + far.astype(F32)).astype(BF16)

    return finish(part_out), finish(part_dx), down_grad


def solution(mesh):
    return jax.shard_map(
        on_device,
        mesh=mesh,
        in_specs=(
            P("expert", "dp"),
            P("expert", "dp"),
            P("expert", "dp", None),
            P("expert", None, "dp"),
            P("expert", None),
            P("expert", None),
            P(),
        ),
        out_specs=(P("expert", "dp"), P("expert", "dp"), P("expert", None, "dp")),
        check_vma=False,
    )
```

time: 417 us -> 250 us (0.60)
  waiting for transfers between devices: 291 us -> 152 us
  between operations: 14.2 us -> 0.93 us
  local copies, waits for them, and re-layouts: 19.4 us -> 9.65 us
  other arithmetic: 22.5 us -> 12.9 us
  matrix products: 32.4 us -> 38 us
    all_to_all x4 -> x5, waiting for transfers between devices: 195 us -> 37.8 us  [halves_exchange(): lax.all_to_all(rows, 'expert', split_axis=0, concat_axis=0, tiled=True, a...]
    ppermute x1 -> x9, waiting for transfers between devices: 69.7 us -> 114 us  [crossed(): lax.ppermute(block, axis, [(i, (i + distance) % size) for i in range(size)])]
    psum x1 -> x0, waiting for transfers between devices: 26.3 us -> none  [on_device(): lax.psum(gate_up_part.astype(jnp.bfloat16), 'dp').astype(jnp.float32)]
    dot_general x3 -> x11, matrix products: 17.7 us -> 28.7 us  [the longest x1 8.93 us: on_device(): jnp.dot(recv_tokens, local_gate_up, preferred_element_type=F32).astype(BF16)]
    all_to_all x4 -> x5, starting transfers between devices: 33.5 us -> 26.8 us  [halves_exchange(): lax.all_to_all(rows, 'expert', split_axis=0, concat_axis=0, tiled=True, a...]
    reduce_sum x3, other arithmetic: 7.6 us -> 0.94 us  [the longest x1 0.72 us: on_device(): row_w = jnp.sum(sel_w, axis=1, keepdims=True)]
    ppermute x1 -> x9, starting transfers between devices: 2.77 us -> 8.99 us  [crossed(): lax.ppermute(block, axis, [(i, (i + distance) % size) for i in range(size)])]
    gather x2 -> x0, local copies, waits for them, and re-layouts: 5.23 us -> none  [the longest x1 3.89 us: on_device(): back_dx.reshape(buffer_rows, width_block)[spot]]
  transfers between devices with their start and end apart: 6 -> 14, of which waited for: 6 -> 9; matrix products, arithmetic and copies ran while one was open for 11% -> 20% of each run, Pallas kernels for 0% -> 0%
where the time goes in v1:
time: 250 us; the launch traced here: 249 us
  waiting for transfers between devices  152 us (61%)
  matrix products  38 us (15%)
  starting transfers between devices  35.7 us (14%)
  other arithmetic  12.9 us (5%)
  local copies, waits for them, and re-layouts  9.65 us (4%)
    ppermute x9, waiting for transfers between devices, crossed(): lax.ppermute(block, axis, [(i, (i + distance) % size) for i in range(size)])  114 us
    all_to_all x5, waiting for transfers between devices, halves_exchange(): lax.all_to_all(rows, 'expert', split_axis=0, concat_axis=0, tiled=True, a...  37.8 us
    all_to_all x5, starting transfers between devices, halves_exchange(): lax.all_to_all(rows, 'expert', split_axis=0, concat_axis=0, tiled=True, a...  26.8 us
    ppermute x9, starting transfers between devices, crossed(): lax.ppermute(block, axis, [(i, (i + distance) % size) for i in range(size)])  8.99 us
    dot_general x1, matrix products, on_device(): jnp.dot(recv_tokens, local_gate_up, preferred_element_type=F32).astype(BF16)  8.93 us
    dot_general x3, matrix products, pick(): return jnp.dot(s.astype(BF16), data, preferred_element_type=F32)  7.32 us
    dot_general x1, matrix products, on_device(): jnp.dot(hidden, local_down, preferred_element_type=F32).astype(BF16)  5.37 us
    dot_general x1, matrix products, on_device(): lax.dot_general(gate_up_grad, local_gate_up, (((1,), (1,)), ((), ())), pr...  5.14 us
  transfers between devices with their start and end apart: 14, of which 9 were waited for; matrix products, arithmetic and copies ran while one was open for 20% of the time, Pallas kernels for 0%

profile of v1, /device:TPU:0, one launch (start us, length us, event | category | flops | bytes accessed | tf_op | source)
XLA Modules:
  0.0 249.4 jit_solution(18229359774076938737)
XLA Ops:
  2.0 4.0 %collective-permute-start = (f32[128,4]{0,1:T(4,128)S(1)}, f32[128,4]{0,1:T(4,128)S(1)}, u32[]{:S(2)}, u32[]{:S(2)}) collective-permute-start(f32[128,4]{0,1:T(4,128)S(1)} %pad_maximum_fusion), channel_id=1, source_target_pairs={{0,8},{1,9},{2,10},{3,11},{4,12},{5,13},{6,14},{7,15},{8,0},{9,1},... | collective-permute-start | bytes 6152 | tf_op jit(solution)/shard_map/ppermute | solution.py:12
  8.5 20.5 %collective-permute-done.1 = bf16[128,1792]{1,0:T(8,128)(2,1)S(1)} collective-permute-done((bf16[128,1792]{1,0:T(8,128)(2,1)}, bf16[128,1792]{1,0:T(8,128)(2,1)S(1)}, u32[]{:S(2)}, u32[]{:S(2)}) %collective-permute-start.1) | collective-permute-done | bytes 458784 | tf_op jit(solution)/shard_map/ppermute | solution.py:12
  29.0 2.9 %convolution_convert_fusion.1 = bf16[512,1792]{1,0:T(8,128)(2,1)} fusion(bf16[512,256]{1,0:T(8,128)(2,1)S(1)} %bitcast.67, bf16[128,1792]{1,0:T(8,128)(2,1)S(1)} %collective-permute-done.1, bf16[128,1792]{1,0:T(8,128)(2,1)} %param.7), kind=kOutput, calls=%fused_computation.14 | convolution fusion | flops 472514560 | bytes 3014656 | tf_op jit(solution)/shard_map/dot_general | solution.py:97
  31.9 3.9 %all-to-all-start = ((bf16[8,64,1792]{2,1,0:T(8,128)(2,1)}), bf16[8,64,1792]{2,1,0:T(8,128)(2,1)S(1)}, u32[]{:S(2)}, u32[]{:S(2)}) async-start(bf16[8,64,1792]{2,1,0:T(8,128)(2,1)} %bitcast.4), calls=%async_computation | async-start | bytes 3670016 | tf_op jit(solution)/shard_map/all_to_all | solution.py:24
  35.7 1.4 collective-permute-start.4
  37.9 1.3 mul.80
  39.3 25.4 %collective-permute-done.4 = bf16[128,1792]{1,0:T(8,128)(2,1)} collective-permute-done((bf16[128,1792]{1,0:T(8,128)(2,1)S(1)}, bf16[128,1792]{1,0:T(8,128)(2,1)}, u32[]{:S(2)}, u32[]{:S(2)}) %collective-permute-start.4) | collective-permute-done | bytes 458784 | tf_op jit(solution)/shard_map/ppermute | solution.py:12
  65.7 2.5 %multiply_convert_fusion.1 = bf16[512,1792]{1,0:T(8,128)(2,1)} fusion(bf16[512,256]{1,0:T(8,128)(2,1)S(1)} %bitcast.68, bf16[256,1792]{1,0:T(8,128)(2,1)S(1)} %constant_dynamic-update-slice_fusion, f32[512]{0:T(512)} %mul.80), kind=kOutput, calls=%fused_computation.11 | convolution fusion | flops 471597056 | bytes 3016704 | tf_op jit(solution)/shard_map/dot_general | solution.py:97
  68.3 1.3 copy-done.5
  69.5 9.7 %all-to-all-start.2 = ((bf16[8,64,1792]{2,1,0:T(8,128)(2,1)}), bf16[8,64,1792]{2,1,0:T(8,128)(2,1)S(1)}, u32[]{:S(2)}, u32[]{:S(2)}) async-start(bf16[8,64,1792]{2,1,0:T(8,128)(2,1)} %bitcast.11), calls=%async_computation.2 | async-start | bytes 3670016 | tf_op jit(solution)/shard_map/all_to_all | solution.py:24
  79.3 8.9 %fusion.12 = bf16[512,2048]{1,0:T(8,128)(2,1)} fusion(bf16[512,1792]{1,0:T(8,128)(2,1)} %bitcast.70, bf16[1,1792,2048]{2,1,0:T(8,128)(2,1)} %param.9), kind=kOutput, calls=%fused_computation.15 | convolution fusion | flops 3759144960 | bytes 11272192 | tf_op jit(solution)/shard_map/dot_general | solution.py:109
  88.5 1.9 multiply_convert_fusion
  90.5 11.4 %all-to-all-done.2 = bf16[8,64,1792]{2,1,0:T(8,128)(2,1)S(1)} async-done(((bf16[8,64,1792]{2,1,0:T(8,128)(2,1)}), bf16[8,64,1792]{2,1,0:T(8,128)(2,1)S(1)}, u32[]{:S(2)}, u32[]{:S(2)}) %all-to-all-start.2) | async-done | bytes 1835040 | tf_op jit(solution)/shard_map/all_to_all | solution.py:24
  101.9 4.3 %all-to-all-start.4 = ((bf16[8,64,1792]{2,1,0:T(8,128)(2,1)}), bf16[8,64,1792]{2,1,0:T(8,128)(2,1)}, u32[]{:S(2)}, u32[]{:S(2)}) async-start(bf16[8,64,1792]{2,1,0:T(8,128)(2,1)} %bitcast.19), calls=%async_computation.4 | async-start | bytes 3670016 | tf_op jit(solution)/shard_map/all_to_all | solution.py:24
  106.2 4.1 %fusion.23 = bf16[512,1024]{1,0:T(8,128)(2,1)S(1)} fusion(bf16[512,1792]{1,0:T(8,128)(2,1)S(1)} %bitcast.66, bf16[1,1024,1792]{2,1,0:T(8,128)(2,1)} %param.10), kind=kOutput, calls=%fused_computation.31 | convolution fusion | flops 1879572480 | bytes 6553600 | tf_op jit(solution)/shard_map/dot_general | solution.py:119
  110.5 3.2 %convert_add_fusion = f32[512,2048]{1,0:T(8,128)S(1)} fusion(bf16[512,2048]{1,0:T(8,128)(2,1)} %collective-permute-done.2, bf16[512,2048]{1,0:T(8,128)(2,1)} %fusion.12), kind=kLoop, calls=%fused_computation.4 | loop fusion | flops 3145728 | bytes 8388608 | tf_op jit(solution)/shard_map/add | solution.py:18
  113.7 1.3 multiply_convert_fusion.3
  115.6 5.1 %fusion.15 = bf16[512,1792]{1,0:T(8,128)(2,1)} fusion(bf16[1,1792,2048]{2,1,0:T(8,128)(2,1)S(1)} %bitcast.74, bf16[512,1024]{1,0:T(8,128)(2,1)S(1)} %get-tuple-element.10, bf16[512,1024]{1,0:T(8,128)(2,1)S(1)} %get-tuple-element.9), kind=kOutput, calls=%fused_computation.16 | convolution fusion | flops 3763208192 | bytes 11272192 | tf_op jit(solution)/shard_map/dot_general | solution.py:126
  120.8 8.4 %all-to-all-done.4 = bf16[8,64,1792]{2,1,0:T(8,128)(2,1)} async-done(((bf16[8,64,1792]{2,1,0:T(8,128)(2,1)}), bf16[8,64,1792]{2,1,0:T(8,128)(2,1)}, u32[]{:S(2)}, u32[]{:S(2)}) %all-to-all-start.4) | async-done | bytes 1835040 | tf_op jit(solution)/shard_map/all_to_all | solution.py:24
  129.2 4.1 %all-to-all-start.3 = ((bf16[8,64,1792]{2,1,0:T(8,128)(2,1)}), bf16[8,64,1792]{2,1,0:T(8,128)(2,1)S(1)}, u32[]{:S(2)}, u32[]{:S(2)}) async-start(bf16[8,64,1792]{2,1,0:T(8,128)(2,1)} %bitcast.71), calls=%async_computation.3 | async-start | bytes 3670016 | tf_op jit(solution)/shard_map/all_to_all | solution.py:24
  133.3 5.4 %fusion.9 = bf16[512,1792]{1,0:T(8,128)(2,1)} fusion(bf16[512,1024]{1,0:T(8,128)(2,1)S(1)} %get-tuple-element.11, bf16[1,1024,1792]{2,1,0:T(8,128)(2,1)} %param.10), kind=kOutput, calls=%fused_computation.13 | convolution fusion | flops 1879965696 | bytes 6553600 | tf_op jit(solution)/shard_map/dot_general | solution.py:116
  138.6 17.9 %all-to-all-done.3 = bf16[8,64,1792]{2,1,0:T(8,128)(2,1)S(1)} async-done(((bf16[8,64,1792]{2,1,0:T(8,128)(2,1)}), bf16[8,64,1792]{2,1,0:T(8,128)(2,1)S(1)}, u32[]{:S(2)}, u32[]{:S(2)}) %all-to-all-start.3) | async-done | bytes 1835040 | tf_op jit(solution)/shard_map/all_to_all | solution.py:24
  156.5 1.2 copy-done
  157.7 4.8 %all-to-all-start.1 = ((bf16[8,64,1792]{2,1,0:T(8,128)(2,1)}), bf16[8,64,1792]{2,1,0:T(8,128)(2,1)S(1)}, u32[]{:S(2)}, u32[]{:S(2)}) async-start(bf16[8,64,1792]{2,1,0:T(8,128)(2,1)} %bitcast.69), calls=%async_computation.1 | async-start | bytes 3670016 | tf_op jit(solution)/shard_map/all_to_all | solution.py:24
  164.0 29.6 %collective-permute-done.7 = bf16[512,512]{1,0:T(8,128)(2,1)} collective-permute-done((bf16[512,512]{1,0:T(8,128)(2,1)}, bf16[512,512]{1,0:T(8,128)(2,1)}, u32[]{:S(2)}, u32[]{:S(2)}) %collective-permute-start.7) | collective-permute-done | bytes 524320 | tf_op jit(solution)/shard_map/ppermute | solution.py:12
  193.6 2.9 %bitcast_select_fusion = bf16[512,1792]{1,0:T(8,128)(2,1)S(1)} fusion(bf16[8,64,1792]{2,1,0:T(8,128)(2,1)} %all-to-all-done.4, pred[]{:T(512)} %compare_reduce_fusion, bf16[8,64,1792]{2,1,0:T(8,128)(2,1)} %copy-done.2), kind=kLoop, calls=%fused_computation.30 | loop fusion | flops 917504 | bytes 5505025 | tf_op jit(solution)/shard_map/jit(_where)/select_n | solution.py:143
  196.6 1.1 constant_dynamic-update-slice_fusion.3
  197.8 4.8 %fusion.8 = bf16[1,1024,1792]{2,1,0:T(8,128)(2,1)} fusion(bf16[512,1792]{1,0:T(8,128)(2,1)S(1)} %bitcast_select_fusion, bf16[512,1024]{1,0:T(8,128)(2,1)S(1)} %constant_dynamic-update-slice_fusion.2, bf16[512,1024]{1,0:T(8,128)(2,1)S(1)} %get-tuple-element.11, pred[]{:T(512)} %compare_reduce_fusion), kind=kOutput, calls=%fused_computation.12 | convolution fusion | flops 1881407488 | bytes 7602177 | tf_op jit(solution)/shard_map/dot_general | solution.py:144
  203.3 1.2 copy-done.3
  204.5 3.4 %collective-permute-start.6 = (bf16[128,1792]{1,0:T(8,128)(2,1)S(1)}, bf16[128,1792]{1,0:T(8,128)(2,1)S(1)}, u32[]{:S(2)}, u32[]{:S(2)}) collective-permute-start(bf16[128,1792]{1,0:T(8,128)(2,1)S(1)} %slice.57), channel_id=1, source_target_pairs={{0,8},{1,9},{2,10},{3,11},{4,12},{5,13},{6,14},{7,15},{8,0},{9,1},... | collective-permute-start | bytes 1376264 | tf_op jit(solution)/shard_map/ppermute | solution.py:12
  209.4 29.5 %collective-permute-done.6 = bf16[128,1792]{1,0:T(8,128)(2,1)S(1)} collective-permute-done((bf16[128,1792]{1,0:T(8,128)(2,1)S(1)}, bf16[128,1792]{1,0:T(8,128)(2,1)S(1)}, u32[]{:S(2)}, u32[]{:S(2)}) %collective-permute-start.6) | collective-permute-done | bytes 458784 | tf_op jit(solution)/shard_map/ppermute | solution.py:12
  239.8 8.8 %collective-permute-done.3 = bf16[128,1792]{1,0:T(8,128)(2,1)S(1)} collective-permute-done((bf16[128,1792]{1,0:T(8,128)(2,1)S(1)}, bf16[128,1792]{1,0:T(8,128)(2,1)S(1)}, u32[]{:S(2)}, u32[]{:S(2)}) %collective-permute-start.3) | collective-permute-done | bytes 458784 | tf_op jit(solution)/shard_map/ppermute | solution.py:12
  (72 shorter events, 12.2 us)
Async XLA Ops:
  2.0 5.6 %collective-permute-start = (f32[128,4]{0,1:T(4,128)S(1)}, f32[128,4]{0,1:T(4,128)S(1)}, u32[]{:S(2)}, u32[]{:S(2)}) collective-permute-start(f32[128,4]{0,1:T(4,128)S(1)} %pad_maximum_fusion), channel_id=1, source_target_pairs={{0,8},{1,9},{2,10},{3,11},{4,12},{5,13},{6,14},{7,15},{8,0},{9,1},... | collective-permute-start | bytes 6152 | tf_op jit(solution)/shard_map/ppermute | solution.py:12
  6.0 22.9 %collective-permute-start.1 = (bf16[128,1792]{1,0:T(8,128)(2,1)}, bf16[128,1792]{1,0:T(8,128)(2,1)S(1)}, u32[]{:S(2)}, u32[]{:S(2)}) collective-permute-start(bf16[128,1792]{1,0:T(8,128)(2,1)} %param.7), channel_id=1, source_target_pairs={{0,8},{1,9},{2,10},{3,11},{4,12},{5,13},{6,14},{7,15},{8,0},{9,1},... | collective-permute-start | bytes 1376264 | tf_op jit(solution)/shard_map/ppermute | solution.py:12
  31.8 3.9 %copy-start.6 = (bf16[128,1792]{1,0:T(8,128)(2,1)S(1)}, bf16[128,1792]{1,0:T(8,128)(2,1)}, u32[]{:S(2)}) copy-start(bf16[128,1792]{1,0:T(8,128)(2,1)} %param.8) | copy-start | bytes 1376260
  31.8 5.3 %copy-start.9 = (s32[128,2]{0,1:T(2,128)S(1)}, s32[128,2]{0,1:T(2,128)}, u32[]{:S(2)}) copy-start(s32[128,2]{0,1:T(2,128)} %param.11) | copy-start | bytes 3076
  31.9 5.3 %copy-start.10 = (f32[128,2]{0,1:T(2,128)S(1)}, f32[128,2]{0,1:T(2,128)}, u32[]{:S(2)}) copy-start(f32[128,2]{0,1:T(2,128)} %param.12) | copy-start | bytes 3076
  31.9 36.4 %all-to-all-start = ((bf16[8,64,1792]{2,1,0:T(8,128)(2,1)}), bf16[8,64,1792]{2,1,0:T(8,128)(2,1)S(1)}, u32[]{:S(2)}, u32[]{:S(2)}) async-start(bf16[8,64,1792]{2,1,0:T(8,128)(2,1)} %bitcast.4), calls=%async_computation | async-start | bytes 3670016 | tf_op jit(solution)/shard_map/all_to_all | solution.py:24
  35.7 29.0 %collective-permute-start.4 = (bf16[128,1792]{1,0:T(8,128)(2,1)S(1)}, bf16[128,1792]{1,0:T(8,128)(2,1)}, u32[]{:S(2)}, u32[]{:S(2)}) collective-permute-start(bf16[128,1792]{1,0:T(8,128)(2,1)S(1)} %copy-done.6), channel_id=1, source_target_pairs={{0,8},{1,9},{2,10},{3,11},{4,12},{5,13},{6,14},{7,15},{8,0},{9,1},... | collective-permute-start | bytes 1376264 | tf_op jit(solution)/shard_map/ppermute | solution.py:12
  68.3 1.3 copy-start.5
  69.5 32.4 %all-to-all-start.2 = ((bf16[8,64,1792]{2,1,0:T(8,128)(2,1)}), bf16[8,64,1792]{2,1,0:T(8,128)(2,1)S(1)}, u32[]{:S(2)}, u32[]{:S(2)}) async-start(bf16[8,64,1792]{2,1,0:T(8,128)(2,1)} %bitcast.11), calls=%async_computation.2 | async-start | bytes 3670016 | tf_op jit(solution)/shard_map/all_to_all | solution.py:24
  79.3 9.0 %copy-start.8 = (s32[8,128]{1,0:T(8,128)S(1)}, s32[8,128]{1,0:T(8,128)}, u32[]{:S(2)}) copy-start(s32[8,128]{1,0:T(8,128)} %get-tuple-element.14) | copy-start | bytes 12292
  79.3 9.0 %copy-start.7 = (s32[8,128]{1,0:T(8,128)S(1)}, s32[8,128]{1,0:T(8,128)}, u32[]{:S(2)}) copy-start(s32[8,128]{1,0:T(8,128)} %get-tuple-element.19) | copy-start | bytes 12292
  88.2 22.2 %collective-permute-start.2 = (bf16[512,2048]{1,0:T(8,128)(2,1)}, bf16[512,2048]{1,0:T(8,128)(2,1)}, u32[]{:S(2)}, u32[]{:S(2)}) collective-permute-start(bf16[512,2048]{1,0:T(8,128)(2,1)} %fusion.12), channel_id=1, source_target_pairs={{0,16},{16,0},{1,17},{17,1},{2,18},{18,2},{3,19},{19,3},{4,20},{20... | collective-permute-start | bytes 6291464 | tf_op jit(solution)/shard_map/ppermute | solution.py:12
  101.9 8.5 %copy-start.2 = (bf16[8,64,1792]{2,1,0:T(8,128)(2,1)}, bf16[8,64,1792]{2,1,0:T(8,128)(2,1)S(1)}, u32[]{:S(2)}) copy-start(bf16[8,64,1792]{2,1,0:T(8,128)(2,1)S(1)} %all-to-all-done.2) | copy-start | bytes 5505028
  101.9 27.3 %all-to-all-start.4 = ((bf16[8,64,1792]{2,1,0:T(8,128)(2,1)}), bf16[8,64,1792]{2,1,0:T(8,128)(2,1)}, u32[]{:S(2)}, u32[]{:S(2)}) async-start(bf16[8,64,1792]{2,1,0:T(8,128)(2,1)} %bitcast.19), calls=%async_computation.4 | async-start | bytes 3670016 | tf_op jit(solution)/shard_map/all_to_all | solution.py:24
  110.4 3.3 %collective-permute-start.5 = (bf16[512,1024]{1,0:T(8,128)(2,1)S(1)}, bf16[512,1024]{1,0:T(8,128)(2,1)S(1)}, u32[]{:S(2)}, u32[]{:S(2)}) collective-permute-start(bf16[512,1024]{1,0:T(8,128)(2,1)S(1)} %fusion.23), channel_id=1, source_target_pairs={{0,16},{16,0},{1,17},{17,1},{2,18},{18,2},{3,19},{19,3},{4,20},{20... | collective-permute-start | bytes 3145736 | tf_op jit(solution)/shard_map/ppermute | solution.py:12
  110.5 4.6 %slice-start = ((s8[7340032]{0:T(1024)(128)(4,1)}), s8[4194304]{0:T(1024)(128)(4,1)S(1)}, s32[]{:S(2)}) async-start(s8[7340032]{0:T(1024)(128)(4,1)} %bitcast.73), calls=%async_computation.5 | async-start | bytes 8388608
  113.7 2.0 slice-start.1
  129.2 27.3 %all-to-all-start.3 = ((bf16[8,64,1792]{2,1,0:T(8,128)(2,1)}), bf16[8,64,1792]{2,1,0:T(8,128)(2,1)S(1)}, u32[]{:S(2)}, u32[]{:S(2)}) async-start(bf16[8,64,1792]{2,1,0:T(8,128)(2,1)} %bitcast.71), calls=%async_computation.3 | async-start | bytes 3670016 | tf_op jit(solution)/shard_map/all_to_all | solution.py:24
  156.5 1.3 copy-start
  156.5 6.9 %copy-start.11 = (s32[4]{0:T(128)S(1)}, s32[4]{0:T(128)}, u32[]{:S(2)}) copy-start(s32[4]{0:T(128)} %param.13) | copy-start | bytes 52
  157.7 50.1 %all-to-all-start.1 = ((bf16[8,64,1792]{2,1,0:T(8,128)(2,1)}), bf16[8,64,1792]{2,1,0:T(8,128)(2,1)S(1)}, u32[]{:S(2)}, u32[]{:S(2)}) async-start(bf16[8,64,1792]{2,1,0:T(8,128)(2,1)} %bitcast.69), calls=%async_computation.1 | async-start | bytes 3670016 | tf_op jit(solution)/shard_map/all_to_all | solution.py:24
  163.4 30.2 %collective-permute-start.7 = (bf16[512,512]{1,0:T(8,128)(2,1)}, bf16[512,512]{1,0:T(8,128)(2,1)}, u32[]{:S(2)}, u32[]{:S(2)}) collective-permute-start(bf16[512,512]{1,0:T(8,128)(2,1)} %constant_dynamic-slice_fusion), channel_id=1, source_target_pairs={{0,8},{1,9},{2,10},{3,11},{4,12},{5,13},{6,14},{7,15},{8,0},{9,1},... | collective-permute-start | bytes 1572872 | tf_op jit(solution)/shard_map/ppermute | solution.py:12
  193.6 4.1 %collective-permute-start.8 = (bf16[512,512]{1,0:T(8,128)(2,1)}, bf16[512,512]{1,0:T(8,128)(2,1)S(1)}, u32[]{:S(2)}, u32[]{:S(2)}) collective-permute-start(bf16[512,512]{1,0:T(8,128)(2,1)} %collective-permute-done.7), channel_id=1, source_target_pairs={{0,16},{16,0},{1,17},{17,1},{2,18},{18,2},{3,19},{19,3},{4,20},{20... | collective-permute-start | bytes 1572872 | tf_op jit(solution)/shard_map/ppermute | solution.py:12
  197.8 4.8 %copy-start.1 = (bf16[8,64,1792]{2,1,0:T(8,128)(2,1)S(1)}, bf16[8,64,1792]{2,1,0:T(8,128)(2,1)}, u32[]{:S(2)}) copy-start(bf16[8,64,1792]{2,1,0:T(8,128)(2,1)} %copy-done) | copy-start | bytes 5505028
  203.2 1.3 copy-start.3
  204.5 34.4 %collective-permute-start.6 = (bf16[128,1792]{1,0:T(8,128)(2,1)S(1)}, bf16[128,1792]{1,0:T(8,128)(2,1)S(1)}, u32[]{:S(2)}, u32[]{:S(2)}) collective-permute-start(bf16[128,1792]{1,0:T(8,128)(2,1)S(1)} %slice.57), channel_id=1, source_target_pairs={{0,8},{1,9},{2,10},{3,11},{4,12},{5,13},{6,14},{7,15},{8,0},{9,1},... | collective-permute-start | bytes 1376264 | tf_op jit(solution)/shard_map/ppermute | solution.py:12
  208.6 30.4 %copy-start.4 = (f32[256,1792]{1,0:T(8,128)S(1)}, f32[256,1792]{1,0:T(8,128)}, u32[]{:S(2)}) copy-start(f32[256,1792]{1,0:T(8,128)} %copy-done.3) | copy-start | bytes 5505028
  209.3 39.2 %collective-permute-start.3 = (bf16[128,1792]{1,0:T(8,128)(2,1)S(1)}, bf16[128,1792]{1,0:T(8,128)(2,1)S(1)}, u32[]{:S(2)}, u32[]{:S(2)}) collective-permute-start(bf16[128,1792]{1,0:T(8,128)(2,1)S(1)} %slice.58), channel_id=1, source_target_pairs={{0,8},{1,9},{2,10},{3,11},{4,12},{5,13},{6,14},{7,15},{8,0},{9,1},... | collective-permute-start | bytes 1376264 | tf_op jit(solution)/shard_map/ppermute | solution.py:12

commit v2 on v0

v2 whole, which is shorter than its diff:
```python
import jax
import jax.numpy as jnp
from jax import lax
from jax.experimental import pallas as pl
from jax.experimental.pallas import tpu as pltpu
from jax.sharding import PartitionSpec as P

BF16 = jnp.bfloat16
F32 = jnp.float32
LONG = 50_000_000_000
ANYWHERE = pl.BlockSpec(memory_space=pl.ANY)
IN_VMEM = pl.BlockSpec(memory_space=pltpu.VMEM)


def tile_of(size):
    return 256 if size % 256 == 0 else size


def wide_tile_of(size):
    return size // 2 if size % 256 == 0 else size


def run(body, out_shape, grid, in_specs, out_specs, operands, scratch=(), deps=(), aliases=None, flops=0):
    count = len(operands)
    out_shape = jax.tree.map(
        lambda x: pltpu.HBM(x.shape, x.dtype) if isinstance(x, jax.ShapeDtypeStruct) else x,
        out_shape,
        is_leaf=lambda x: not isinstance(x, (list, tuple)),
    )

    def whole(*refs):
        body(*refs[:count], *refs[count + len(deps) :])

    return pl.pallas_call(
        whole,
        out_shape=out_shape,
        grid=grid,
        in_specs=list(in_specs) + [ANYWHERE] * len(deps),
        out_specs=out_specs,
        scratch_shapes=list(scratch),
        input_output_aliases=aliases or {},
        cost_estimate=pl.CostEstimate(flops=flops, bytes_accessed=0, transcendentals=0),
        compiler_params=pltpu.CompilerParams(vmem_limit_bytes=52 * 1024 * 1024),
    )(*operands, *deps)


def tied(value, *deps, flops=0):
    shape = jax.ShapeDtypeStruct(value.shape, value.dtype)
    return run(lambda *refs: None, shape, (), [ANYWHERE], ANYWHERE, [value], (), deps, {0: 0}, flops)


def resident(weight):
    parts = 8
    step = weight.shape[1] // parts

    def body(w_ref, out, sems):
        copies = [
            pltpu.make_async_copy(
                w_ref.at[0, pl.ds(n * step, step)], out.at[0, pl.ds(n * step, step)], sems.at[n]
            )
            for n in range(parts)
        ]
        for copy in copies:
            copy.start()
        for copy in copies:
            copy.wait()

    return run(
        body,
        pltpu.VMEM(weight.shape, weight.dtype),
        (),
        [ANYWHERE],
        IN_VMEM,
        [weight],
        [pltpu.SemaphoreType.DMA((parts,))],
    )


def held(value, *deps):
    def body(value_ref, out, sem):
        copy = pltpu.make_async_copy(value_ref, out, sem)
        copy.start()
        copy.wait()

    shape = jax.ShapeDtypeStruct(value.shape, value.dtype)
    scratch = [pltpu.SemaphoreType.DMA]
    return run(body, shape, (), [ANYWHERE], ANYWHERE, [value], scratch, deps)


def fixed(shape):
    return pl.BlockSpec(shape, lambda *at: (0,) * len(shape))


def pick(parts, peers, deps=(), flops=0):
    rows = parts[0][0].shape[0]
    slots = rows // peers
    count, width = parts[0][1].shape
    tile = wide_tile_of(width)
    operands, specs = [], []
    for sel, data, weight in parts:
        operands += [sel, data]
        specs += [fixed(sel.shape), pl.BlockSpec((count, tile), lambda c: (0, c))]
        if weight is not None:
            operands.append(weight)
            specs.append(fixed(weight.shape))

    def body(*refs):
        out, refs = refs[-1], list(refs[:-1])
        for n, (_, _, weight) in enumerate(parts):
            got = jnp.dot(refs.pop(0)[...], refs.pop(0)[...], preferred_element_type=F32)
            if weight is not None:
                got = got * refs.pop(0)[...]
            out[:, n * slots : (n + 1) * slots, :] = got.astype(BF16).reshape(peers, slots, tile)

    return run(
        body,
        jax.ShapeDtypeStruct((peers, slots * len(parts), width), BF16),
        (width // tile,),
        specs,
        pl.BlockSpec((peers, slots * len(parts), tile), lambda c: (0, 0, c)),
        operands,
        deps=deps,
        flops=flops,
    )


def tile_at(tile, size):
    if tile == size:
        return slice(None)
    return pl.ds(pl.multiple_of(pl.program_id(0) * tile, tile), tile)


def gate_up_part(x, group, slots, weight, deps=()):
    peers, _, width = x.shape
    rows, columns = peers * slots, weight.shape[2]
    tile = tile_of(columns // 2) * 2

    def body(x_ref, w_ref, out):
        got = jnp.dot(x_ref[...].reshape(rows, width), w_ref[0, :, tile_at(tile, columns)], preferred_element_type=F32)
        out[...] = got.astype(BF16)

    return run(
        body,
        jax.ShapeDtypeStruct((rows, columns), BF16),
        (columns // tile,),
        [
            pl.BlockSpec((peers, slots, width), lambda c: (0, group, 0)),
            IN_VMEM,
        ],
        pl.BlockSpec((rows, tile), lambda c: (0, c)),
        [x, weight],
        deps=deps,
    )


def total(refs):
    result = refs[0][...].astype(F32)
    for ref in refs[1:]:
        result = result + ref[...].astype(F32)
    return result


def hidden_and_out(near, far, weight, core, n_dp, peers, tail, deps=()):
    n = len(near)
    rows = near[0].shape[0]
    _, inner, width = weight.shape
    slots = rows // peers
    share = inner // n_dp
    tile = wide_tile_of(width)
    block = pl.BlockSpec((peers, slots, tile), lambda c: (0, 0, c))

    def body(*refs):
        near_refs, far_refs = refs[:n], refs[n : 2 * n]
        core_ref, w_ref, tail_ref, hidden, mine, send, out = refs[2 * n :]

        @pl.when(pl.program_id(0) == 0)
        def _():
            for at, part_refs in ((0, near_refs), (rows, far_refs)):
                gate_up = total(part_refs)
                gate = gate_up[:, :inner]
                hidden[at : at + rows, :] = (
                    gate * jax.nn.sigmoid(gate) * gate_up[:, inner:]
                ).astype(BF16)
            first = pl.multiple_of(core_ref[0] * share, 128)
            mine[...] = hidden[:, pl.ds(first, share)]

        got = jnp.dot(
            hidden[...], w_ref[0, :, tile_at(tile, width)], preferred_element_type=F32
        ).astype(BF16)
        out[...] = got[:rows].reshape(peers, slots, tile)
        send[:, :slots, :] = got[rows:].reshape(peers, slots, tile)
        send[:, slots:, :] = tail_ref[...]

    return run(
        body,
        (
            jax.ShapeDtypeStruct((2 * rows, inner), BF16),
            jax.ShapeDtypeStruct((2 * rows, share), BF16),
            jax.ShapeDtypeStruct((peers, 2 * slots, width), BF16),
            jax.ShapeDtypeStruct((peers, slots, width), BF16),
        ),
        (width // tile,),
        [fixed(p.shape) for p in (*near, *far)]
        + [pl.BlockSpec(memory_space=pltpu.SMEM), IN_VMEM, block],
        (
            fixed((2 * rows, inner)),
            fixed((2 * rows, share)),
            pl.BlockSpec((peers, 2 * slots, tile), lambda c: (0, 0, c)),
            block,
        ),
        [*near, *far, core, weight, tail],
        deps=deps,
    )


def hidden_grad_part(x, slots, weight, deps=()):
    peers, _, width = x.shape
    rows, inner = peers * slots, weight.shape[1]
    tile = tile_of(inner)

    def body(x_ref, w_ref, out):
        data = [x_ref[:, at : at + slots, :].reshape(rows, width) for at in (0, slots)]
        got = lax.dot_general(
            jnp.concatenate(data, axis=0),
            w_ref[0, tile_at(tile, inner), :],
            (((1,), (1,)), ((), ())),
            preferred_element_type=F32,
        )
        out[...] = got.astype(BF16)

    return run(
        body,
        jax.ShapeDtypeStruct((2 * rows, inner), BF16),
        (inner // tile,),
        [fixed(x.shape), IN_VMEM],
        pl.BlockSpec((2 * rows, tile), lambda c: (0, c)),
        [x, weight],
        deps=deps,
    )


def rows_dx(grad_parts, near, far, weight, peers, ahead, tail, deps=()):
    n = len(near)
    rows = near[0].shape[0]
    inner = grad_parts[0].shape[1]
    width = weight.shape[1]
    slots = rows // peers
    tile = tile_of(width)
    block = pl.BlockSpec((peers, slots, tile), lambda c: (0, 0, c))
    blocks = pl.BlockSpec((peers, 2 * slots, tile), lambda c: (0, 0, c))

    def body(*refs):
        grad_refs, near_refs, far_refs = refs[:n], refs[n : 2 * n], refs[2 * n : 3 * n]
        w_ref, ahead_ref, tail_ref, far_out, near_out, both = refs[3 * n :]

        @pl.when(pl.program_id(0) == 0)
        def _():
            for at, part_refs in ((0, near_refs), (rows, far_refs)):
                hidden_grad = total([g.at[at : at + rows, :] for g in grad_refs])
                gate_up = total(part_refs)
                gate, up = gate_up[:, :inner], gate_up[:, inner:]
                sig = jax.nn.sigmoid(gate)
                gate_grad = hidden_grad * up * sig * (1.0 + gate * (1.0 - sig))
                both[at : at + rows, :inner] = gate_grad.astype(BF16)
                both[at : at + rows, inner:] = (hidden_grad * (gate * sig)).astype(BF16)

        got = lax.dot_general(
            both[...],
            w_ref[0, tile_at(tile, width), :],
            (((1,), (1,)), ((), ())),
            preferred_element_type=F32,
        ).astype(BF16)
        near_out[:, :slots, :] = ahead_ref[...]
        near_out[:, slots:, :] = got[:rows].reshape(peers, slots, tile)
        far_out[:, :slots, :] = got[rows:].reshape(peers, slots, tile)
        far_out[:, slots:, :] = tail_ref[...]

    return run(
        body,
        [jax.ShapeDtypeStruct((peers, 2 * slots, width), BF16)] * 2,
        (width // tile,),
        [fixed(p.shape) for p in (*grad_parts, *near, *far)] + [IN_VMEM, block, block],
        [blocks, blocks],
        [*grad_parts, *near, *far, weight, ahead, tail],
        [pltpu.VMEM((2 * rows, 2 * inner), BF16)],
        deps,
    )


def give(back, group, slots, matrices, more=None, deps=()):
    peers, _, width = back.shape
    count = matrices[0].shape[0]
    tile = wide_tile_of(width)
    column = pl.BlockSpec((count, tile), lambda c: (0, c))

    def body(back_ref, *refs):
        data = back_ref[...].reshape(peers * slots, tile)
        result = jnp.dot(refs[0][...], data, preferred_element_type=F32)
        for ref in refs[1 : len(matrices)]:
            result = result + jnp.dot(ref[...], data, preferred_element_type=F32)
        if more is not None:
            result = result + refs[len(matrices)][...].astype(F32)
        refs[-1][...] = result.astype(BF16)

    return run(
        body,
        jax.ShapeDtypeStruct((count, width), BF16),
        (width // tile,),
        [pl.BlockSpec((peers, slots, tile), lambda c: (0, group, c))]
        + [fixed(m.shape) for m in matrices]
        + ([column] if more is not None else []),
        column,
        [back] + list(matrices) + ([more] if more is not None else []),
        deps=deps,
    )


def finish(back, slots, weighted, plain, out_from, dx_from, deps=()):
    peers, _, width = back.shape
    count = plain.shape[0]
    tile = wide_tile_of(width)
    column = pl.BlockSpec((count, tile), lambda c: (0, c))

    def body(back_ref, high, low, plain_ref, out_ref, dx_ref, layer_out, token_grad):
        rows = [back_ref[:, at : at + slots, :].reshape(peers * slots, tile) for at in (0, slots)]
        result = jnp.dot(high[...], rows[0], preferred_element_type=F32)
        result = result + jnp.dot(low[...], rows[0], preferred_element_type=F32)
        layer_out[...] = (result + out_ref[...].astype(F32)).astype(BF16)
        result = jnp.dot(plain_ref[...], rows[1], preferred_element_type=F32)
        token_grad[...] = (result + dx_ref[...].astype(F32)).astype(BF16)

    return run(
        body,
        [jax.ShapeDtypeStruct((count, width), BF16)] * 2,
        (width // tile,),
        [pl.BlockSpec((peers, 2 * slots, tile), lambda c: (0, 0, c))]
        + [fixed(plain.shape)] * 3
        + [column] * 2,
        [column] * 2,
        [back, *weighted, plain, out_from, dx_from],
        deps=deps,
    )


def expert_grad(where, hidden, far_shares, own, there, slots, deps=()):
    n = len(far_shares)
    peers, _, width = own.shape
    rows = peers * slots
    inner = hidden.shape[1]
    share = inner // n
    tile = wide_tile_of(width)

    def body(where_ref, hidden_ref, *refs):
        share_refs = refs[:n]
        own_ref, there_0, there_1 = refs[n : n + 3]
        out, left = refs[-2:]
        moved = where_ref[1] != 0

        @pl.when(pl.program_id(1) == 0)
        def _():
            @pl.when(jnp.logical_not(moved))
            def _():
                left[...] = hidden_ref[...].astype(F32).T.astype(BF16)

            for d in range(n):
                @pl.when(jnp.logical_and(moved, pl.program_id(0) == d))
                def _():
                    left[...] = share_refs[d][...].astype(F32).T.astype(BF16)

        mine = [own_ref[:, at : at + slots, :].reshape(rows, tile) for at in (0, slots)]
        other = [there_0[...].reshape(rows, tile), there_1[...].reshape(rows, tile)]
        right = [jnp.where(moved, a, b) for a, b in zip(other, mine)]
        got = jnp.dot(left[...], jnp.concatenate(right, axis=0), preferred_element_type=F32)
        out[0] = got.astype(BF16)

    def place(d, where):
        return lax.rem(where[0] - d + n, n)

    return pl.pallas_call(
        body,
        out_shape=pltpu.HBM((1, inner, width), BF16),
        grid_spec=pltpu.PrefetchScalarGridSpec(
            num_scalar_prefetch=1,
            grid=(n, width // tile),
            in_specs=[pl.BlockSpec((2 * rows, share), lambda d, c, w: (0, place(d, w)))]
            + [pl.BlockSpec((2 * rows, share), lambda d, c, w: (0, 0))] * n
            + [pl.BlockSpec((peers, 2 * slots, tile), lambda d, c, w: (0, 0, c))]
            + [pl.BlockSpec((peers, slots, tile), lambda d, c, w: (0, 1, c))] * 2
            + [ANYWHERE] * len(deps),
            out_specs=pl.BlockSpec((1, share, tile), lambda d, c, w: (0, place(d, w), c)),
            scratch_shapes=[pltpu.VMEM((share, 2 * rows), BF16)],
        ),
        cost_estimate=pl.CostEstimate(flops=0, bytes_accessed=0, transcendentals=0),
        compiler_params=pltpu.CompilerParams(vmem_limit_bytes=52 * 1024 * 1024),
    )(where, hidden, *far_shares, own, *there, *deps)


def crossed(block, axis, distance):
    size = lax.axis_size(axis)
    return lax.ppermute(block, axis, [(i, (i + distance) % size) for i in range(size)])


def over_dp(part):
    parts = [part] + [crossed(part, "dp", d) for d in range(1, lax.axis_size("dp"))]
    if len(parts) > 2:
        parts = [sum(p.astype(F32) for p in parts)]
    return parts


def dispatch(routes, weights, firsts, peers, slots, sends, deps=(), flops=0):
    top_count, count = routes.shape
    rows = peers * slots
    ids = jnp.stack(firsts)
    data = [d for send in sends for _, d, _ in send]

    def body(ids_ref, routes_ref, weights_ref, *refs):
        data_refs, outs = list(refs[: len(data)]), list(refs[len(data) :])
        earlier = lax.broadcasted_iota(jnp.int32, (count, count), 0)
        later = lax.broadcasted_iota(jnp.int32, (count, count), 1)
        before = (earlier < later).astype(F32).astype(BF16)
        chosen = []
        for n in range(len(firsts)):
            expert = ids_ref[n] + lax.broadcasted_iota(jnp.int32, (peers, count), 0)
            member = jnp.zeros((peers, count), F32)
            table = jnp.zeros((peers, count), F32)
            for k in range(top_count):
                named = routes_ref[k : k + 1, :] == expert
                member = jnp.where(named, 1.0, member)
                table = jnp.where(named, weights_ref[k : k + 1, :], table)
            place = jnp.dot(member.astype(BF16), before, preferred_element_type=F32)
            place = jnp.where(member > 0.0, place, -1.0)
            slot = lax.broadcasted_iota(jnp.int32, (slots, count), 0).astype(F32)
            hits, weighted = [], []
            for e in range(peers):
                hit = slot == place[e : e + 1, :]
                hits.append(jnp.where(hit, 1.0, 0.0))
                weighted.append(jnp.where(hit, table[e : e + 1, :], 0.0))
            sel = jnp.concatenate(hits, axis=0)
            weighted = jnp.concatenate(weighted, axis=0)
            chosen.append((sel.astype(BF16), jnp.sum(weighted, axis=1, keepdims=True)))
            outs.pop(0)[...] = chosen[-1][0]
            outs.pop(0)[...] = chosen[-1][1]
            if n == 0:
                turned = weighted.T
                high = turned.astype(BF16)
                outs.pop(0)[...] = sel.T.astype(BF16)
                outs.pop(0)[...] = high
                outs.pop(0)[...] = (turned - high.astype(F32)).astype(BF16)
        for send in sends:
            out = outs.pop(0)
            for g, (n, _, weighted) in enumerate(send):
                sel, weight = chosen[n]
                got = jnp.dot(sel, data_refs.pop(0)[...], preferred_element_type=F32)
                if weighted:
                    got = got * weight
                got = got.astype(BF16).reshape(peers, slots, got.shape[1])
                out[:, g * slots : (g + 1) * slots, :] = got

    shapes = []
    for n in range(len(firsts)):
        shapes += [((rows, count), BF16), ((rows, 1), F32)]
        if n == 0:
            shapes += [((count, rows), BF16)] * 3
    for send in sends:
        shapes.append(((peers, slots * len(send), send[0][1].shape[1]), BF16))
    operands = [routes, weights] + data
    out = run(
        body,
        [jax.ShapeDtypeStruct(*shape) for shape in shapes],
        (1,),
        [pl.BlockSpec(memory_space=pltpu.SMEM)] + [fixed(x.shape) for x in operands],
        [fixed(shape) for shape, _ in shapes],
        [ids] + operands,
        deps=deps,
        flops=flops,
    )
    out = list(out)
    result = []
    for n in range(len(firsts)):
        size = 5 if n == 0 else 2
        result.append(out[:size])
        out = out[size:]
    return result, out


def on_device(tokens, out_grad, gate_up_weight, down_weight, routes, route_weight, swapped):
    experts = lax.axis_size("expert")
    half = experts // 2
    token_count = tokens.shape[0]
    top_count = routes.shape[1]
    n_dp = lax.axis_size("dp")
    slots = max(16, 2 * token_count * top_count // experts)
    me = lax.axis_index("expert")
    core = lax.axis_index("dp")
    moved = jnp.any(swapped == me % half)
    here = (me // half) * half
    there = half - here
    groups = [[s * half + j for j in range(half)] for s in range(2)]

    def cross(x):
        return crossed(x, "expert", half)

    def exchange(x):
        return lax.all_to_all(
            x, "expert", split_axis=0, concat_axis=0, tiled=True, axis_index_groups=groups
        )

    routes, route_weight = routes.T, route_weight.T
    tokens_far = cross(tokens)
    routes_far = cross(routes)
    weight_far = cross(route_weight)
    core_at = core.astype(jnp.int32).reshape(1)
    where = jnp.stack([core.astype(jnp.int32), moved.astype(jnp.int32)])

    (near, near_there), (send_1,) = dispatch(
        routes, route_weight, [here, there], half, slots, [[(0, tokens, False)]]
    )
    sel_n, row_n, back_sel_n, *back_wt_n = near
    first = exchange(send_1)
    gate_up_vmem = gate_up_weight
    down_vmem = down_weight

    grad_far = cross(held(out_grad, tokens_far))
    (far, far_there), (send_2,) = dispatch(
        routes_far,
        weight_far,
        [here, there],
        half,
        slots,
        [[(0, tokens_far, False)]],
        deps=(send_1,),
        flops=LONG,
    )
    sel_f, row_f, back_sel_f, *back_wt_f = far
    send_2 = tied(send_2, first)
    second = exchange(send_2)
    part_n = gate_up_part(first, 0, slots, gate_up_vmem, deps=(send_2,))
    parts_n = over_dp(part_n)
    grads_there_n = pick([(near_there[0], out_grad, near_there[1])], half, deps=(part_n,))

    send_3 = pick(
        [(sel_n, out_grad, row_n), (sel_f, grad_far, row_f)],
        half,
        deps=(grads_there_n,),
        flops=LONG,
    )
    send_3 = tied(send_3, second)
    third = exchange(send_3)
    part_f = gate_up_part(second, 0, slots, gate_up_vmem, deps=(send_3,))
    parts_f = over_dp(part_f)
    grads_there_f = pick([(far_there[0], grad_far, far_there[1])], half, deps=(part_f,))
    hidden, share, send_4, out_n = hidden_and_out(
        parts_n, parts_f, down_vmem, core_at, n_dp, half, grads_there_f
    )
    far_share = cross(share)
    send_4 = tied(send_4, third)
    fourth = exchange(send_4)

    grad_parts = over_dp(hidden_grad_part(third, slots, down_vmem, deps=(send_4,)))
    send_5, send_6 = rows_dx(
        grad_parts, parts_n, parts_f, gate_up_vmem, half, out_n, grads_there_n
    )
    send_5 = tied(send_5, fourth, far_share)
    fifth = exchange(send_5)
    far_shares = [far_share] + [crossed(far_share, "dp", d) for d in range(1, n_dp)]
    give_out = give(fourth, 0, slots, back_wt_f, deps=(send_5,))
    out_from = cross(give_out)

    send_6 = tied(send_6, fifth, out_from)
    sixth = exchange(send_6)
    give_dx = give(fifth, 0, slots, [back_sel_f], deps=(send_6,))
    dx_from = cross(give_dx)
    down_grad = expert_grad(
        where, hidden, far_shares, third, (fourth, fifth), slots, deps=(give_dx,)
    )
    layer_out, token_grad = finish(
        sixth, slots, back_wt_n, back_sel_n, out_from, dx_from, deps=(down_grad,)
    )
    return layer_out, token_grad, down_grad


def solution(mesh):
    return jax.shard_map(
        on_device,
        mesh=mesh,
        in_specs=(
            P("expert", "dp"),
            P("expert", "dp"),
            P("expert", "dp", None),
            P("expert", None, "dp"),
            P("expert", None),
            P("expert", None),
            P(),
        ),
        out_specs=(P("expert", "dp"), P("expert", "dp"), P("expert", None, "dp")),
        check_vma=False,
    )
```

time: 417 us -> 206 us (0.49)
  waiting for transfers between devices: 291 us -> 82.5 us
  Pallas kernels: 0 us -> 65.4 us
  matrix products: 32.4 us -> 0 us
  other arithmetic: 22.5 us -> 0.78 us
  between operations: 14.2 us -> 1.53 us
  local copies, waits for them, and re-layouts: 19.4 us -> 14.3 us
    all_to_all x4 -> x6, waiting for transfers between devices: 195 us -> 20.8 us  [exchange(): lax.all_to_all(x, 'expert', split_axis=0, concat_axis=0, tiled=True, axis...]
    pallas_call x0 -> x20, Pallas kernels: none -> 65.4 us  [the longest x19 57.4 us: run(): pl.pallas_call(whole, out_shape=out_shape, grid=grid, in_specs=list(in_sp...]
    dot_general x5 -> x0, matrix products: 32.4 us -> none  [the longest x1 8.98 us: on_device(): lax.dot_general(gate_up_grad, local_gate_up, (((1,), (1,)), ((), ())), pr...]
    psum x1 -> x0, waiting for transfers between devices: 26.3 us -> none  [on_device(): lax.psum(gate_up_part.astype(jnp.bfloat16), 'dp').astype(jnp.float32)]
    unnamed x14 -> x72, local copies, waits for them, and re-layouts: 0.92 us -> 14.3 us
    ppermute x1 -> x11, waiting for transfers between devices: 69.7 us -> 61.8 us  [crossed(): lax.ppermute(block, axis, [(i, (i + distance) % size) for i in range(size)])]
    reduce_sum x3 -> x0, other arithmetic: 7.6 us -> none  [the longest x1 4.18 us: on_device(): jnp.sum(dx_rows.astype(jnp.float32), axis=1).astype(jnp.bfloat16)]
    ppermute x1 -> x11, starting transfers between devices: 2.77 us -> 10 us  [crossed(): lax.ppermute(block, axis, [(i, (i + distance) % size) for i in range(size)])]
  transfers between devices with their start and end apart: 6 -> 17, of which waited for: 6 -> 10; matrix products, arithmetic and copies ran while one was open for 11% -> 0% of each run, Pallas kernels for 0% -> 31%
where the time goes in v2:
time: 206 us; the launch traced here: 205 us
  waiting for transfers between devices  82.5 us (40%)
  Pallas kernels  65.4 us (32%)
  starting transfers between devices  40.3 us (20%)
  local copies, waits for them, and re-layouts  14.3 us (7%)
    ppermute x11, waiting for transfers between devices, crossed(): lax.ppermute(block, axis, [(i, (i + distance) % size) for i in range(size)])  61.8 us
    pallas_call x19, Pallas kernels, run(): pl.pallas_call(whole, out_shape=out_shape, grid=grid, in_specs=list(in_sp...  57.4 us
    all_to_all x6, starting transfers between devices, exchange(): lax.all_to_all(x, 'expert', split_axis=0, concat_axis=0, tiled=True, axis...  30.3 us
    all_to_all x6, waiting for transfers between devices, exchange(): lax.all_to_all(x, 'expert', split_axis=0, concat_axis=0, tiled=True, axis...  20.8 us
    unnamed x72, local copies, waits for them, and re-layouts  14.3 us
    ppermute x11, starting transfers between devices, crossed(): lax.ppermute(block, axis, [(i, (i + distance) % size) for i in range(size)])  10 us
    pallas_call x1, Pallas kernels, expert_grad(): pl.pallas_call(body, out_shape=pltpu.HBM((1, inner, width), BF16), grid_s...  7.99 us
  transfers between devices with their start and end apart: 17, of which 10 were waited for; matrix products, arithmetic and copies ran while one was open for 0% of the time, Pallas kernels for 31%

profile of v2, /device:TPU:0, one launch (start us, length us, event | category | flops | bytes accessed | tf_op | source)
XLA Modules:
  0.0 204.9 jit_solution(13098432965159263876)
XLA Ops:
  0.6 4.1 %collective-permute-start.2 = (bf16[128,1792]{1,0:T(8,128)(2,1)}, bf16[128,1792]{1,0:T(8,128)(2,1)S(1)}, u32[]{:S(2)}, u32[]{:S(2)}) collective-permute-start(bf16[128,1792]{1,0:T(8,128)(2,1)} %refs_3_.1), channel_id=1, source_target_pairs={{0,8},{1,9},{2,10},{3,11},{4,12},{5,13},{6,14},{7,15},{8,0},{9,1},... | collective-permute-start | bytes 1376264 | tf_op jit(solution)/shard_map/ppermute | solution.py:400
  4.8 2.8 %collective-permute-start.1 = (f32[2,128]{1,0:T(2,128)}, f32[2,128]{1,0:T(2,128)S(1)}, u32[]{:S(2)}, u32[]{:S(2)}) collective-permute-start(f32[2,128]{1,0:T(2,128)} %bitcast.8), channel_id=1, source_target_pairs={{0,8},{1,9},{2,10},{3,11},{4,12},{5,13},{6,14},{7,15},{8,0},{9,1},... | collective-permute-start | bytes 3080 | tf_op jit(solution)/shard_map/ppermute | solution.py:400
  10.1 2.0 shard_map.94
  12.1 4.9 %all-to-all-start = ((bf16[8,32,1792]{2,1,0:T(8,128)(2,1)}), bf16[8,32,1792]{2,1,0:T(8,128)(2,1)S(1)}, u32[]{:S(2)}, u32[]{:S(2)}) async-start(bf16[8,32,1792]{2,1,0:T(8,128)(2,1)} %get-tuple-element.29.refs_4_), calls=%async_computation | async-start | bytes 1835008 | tf_op jit(solution)/shard_map/all_to_all | solution.py:504
  17.0 8.5 %collective-permute-done.2.refs_3_.refs_1_ = bf16[128,1792]{1,0:T(8,128)(2,1)S(1)} collective-permute-done((bf16[128,1792]{1,0:T(8,128)(2,1)}, bf16[128,1792]{1,0:T(8,128)(2,1)S(1)}, u32[]{:S(2)}, u32[]{:S(2)}) %collective-permute-start.2) | collective-permute-done | bytes 458784 | tf_op jit(solution)/shard_map/ppermute | solution.py:400
  26.4 2.0 shard_map.95
  28.4 8.5 %all-to-all-done.refs_1_.refs_0_ = bf16[8,32,1792]{2,1,0:T(8,128)(2,1)S(1)} async-done(((bf16[8,32,1792]{2,1,0:T(8,128)(2,1)}), bf16[8,32,1792]{2,1,0:T(8,128)(2,1)S(1)}, u32[]{:S(2)}, u32[]{:S(2)}) %all-to-all-start) | async-done | bytes 917536 | tf_op jit(solution)/shard_map/all_to_all | solution.py:504
  36.9 4.2 %all-to-all-start.1 = ((bf16[8,32,1792]{2,1,0:T(8,128)(2,1)}), bf16[8,32,1792]{2,1,0:T(8,128)(2,1)S(1)}, u32[]{:S(2)}, u32[]{:S(2)}) async-start(bf16[8,32,1792]{2,1,0:T(8,128)(2,1)} %shard_map.97.refs_2_), calls=%async_computation.1 | async-start | bytes 1835008 | tf_op jit(solution)/shard_map/all_to_all | solution.py:504
  41.1 6.7 %shard_map.98.refs_3_.refs_0_.refs_2_ = bf16[256,2048]{1,0:T(8,128)(2,1)} custom-call(bf16[8,32,1792]{2,1,0:T(8,128)(2,1)S(1)} %all-to-all-done.refs_1_.refs_0_, bf16[1,1792,2048]{2,1,0:T(8,128)(2,1)} %refs_6_.1, bf16[8,32,1792]{2,1,0:T(8,128)(2,1)S(1)} %copy-done.7), custom_call_target="tpu_custom_call" | custom-call | tf_op jit(solution)/shard_map/pallas_call | solution.py:34
  49.1 1.4 shard_map.99.refs_6_.refs_8_
  50.6 2.7 %shard_map.100.refs_0_ = bf16[8,64,1792]{2,1,0:T(8,128)(2,1)} custom-call(bf16[256,128]{1,0:T(8,128)(2,1)S(1)} %copy-done.30, bf16[128,1792]{1,0:T(8,128)(2,1)S(1)} %copy-done.12, f32[256,1]{1,0:T(8,128)S(1)} %copy-done.29, bf16[256,128]{1,0:T(8,128)(2,1)S(1)} %copy-done.32, bf16[128,1792]{1,0:T(8,128)(2,1)} %collective-permute-done.3.refs_4_.refs_1_, ...), custom_call_target="tpu_custom_call" | custom-call | flops 49999998976 | tf_op jit(solution)/shard_map/pallas_call | solution.py:34
  53.3 5.5 %all-to-all-done.1.refs_1_.refs_0_ = bf16[8,32,1792]{2,1,0:T(8,128)(2,1)S(1)} async-done(((bf16[8,32,1792]{2,1,0:T(8,128)(2,1)}), bf16[8,32,1792]{2,1,0:T(8,128)(2,1)S(1)}, u32[]{:S(2)}, u32[]{:S(2)}) %all-to-all-start.1) | async-done | bytes 917536 | tf_op jit(solution)/shard_map/all_to_all | solution.py:504
  59.7 3.7 %all-to-all-start.2 = ((bf16[8,64,1792]{2,1,0:T(8,128)(2,1)}), bf16[8,64,1792]{2,1,0:T(8,128)(2,1)S(1)}, u32[]{:S(2)}, u32[]{:S(2)}) async-start(bf16[8,64,1792]{2,1,0:T(8,128)(2,1)} %shard_map.101.refs_2_), calls=%async_computation.2 | async-start | bytes 3670016 | tf_op jit(solution)/shard_map/all_to_all | solution.py:504
  64.7 6.6 %shard_map.102.refs_3_.refs_2_.refs_4_ = bf16[256,2048]{1,0:T(8,128)(2,1)} custom-call(bf16[8,32,1792]{2,1,0:T(8,128)(2,1)S(1)} %copy-done.9, bf16[1,1792,2048]{2,1,0:T(8,128)(2,1)} %refs_6_.1, bf16[8,64,1792]{2,1,0:T(8,128)(2,1)} %shard_map.101.refs_2_), custom_call_target="tpu_custom_call" | custom-call | tf_op jit(solution)/shard_map/pallas_call | solution.py:34
  73.0 2.3 %shard_map.103.refs_6_ = bf16[8,32,1792]{2,1,0:T(8,128)(2,1)} custom-call(bf16[256,128]{1,0:T(8,128)(2,1)S(1)} %copy-done.25, bf16[128,1792]{1,0:T(8,128)(2,1)} %collective-permute-done.3.refs_4_.refs_1_, f32[256,1]{1,0:T(8,128)S(1)} %copy-done.17, bf16[256,2048]{1,0:T(8,128)(2,1)S(1)} %copy-done.6), custom_call_target="tpu_custom_call" | custom-call | tf_op jit(solution)/shard_map/pallas_call | solution.py:34
  76.5 8.1 %shard_map.104 = (bf16[512,1024]{1,0:T(8,128)(2,1)}, bf16[512,512]{1,0:T(8,128)(2,1)}, bf16[8,64,1792]{2,1,0:T(8,128)(2,1)}, bf16[8,32,1792]{2,1,0:T(8,128)(2,1)}) custom-call(bf16[256,2048]{1,0:T(8,128)(2,1)S(1)} %copy-done.5, bf16[256,2048]{1,0:T(8,128)(2,1)} %collective-permute-done.4.refs_1_.refs_3_, ...), custom_call_target="tpu_custom_call" | custom-call | tf_op jit(solution)/shard_map/pallas_call | solution.py:34
  84.6 2.3 %all-to-all-done.2.refs_1_.refs_0_.refs_2_ = bf16[8,64,1792]{2,1,0:T(8,128)(2,1)S(1)} async-done(((bf16[8,64,1792]{2,1,0:T(8,128)(2,1)}), bf16[8,64,1792]{2,1,0:T(8,128)(2,1)S(1)}, u32[]{:S(2)}, u32[]{:S(2)}) %all-to-all-start.2) | async-done | bytes 1835040 | tf_op jit(solution)/shard_map/all_to_all | solution.py:504
  88.1 5.4 %all-to-all-start.3 = ((bf16[8,64,1792]{2,1,0:T(8,128)(2,1)}), bf16[8,64,1792]{2,1,0:T(8,128)(2,1)S(1)}, u32[]{:S(2)}, u32[]{:S(2)}) async-start(bf16[8,64,1792]{2,1,0:T(8,128)(2,1)} %shard_map.105.refs_2_), calls=%async_computation.3 | async-start | bytes 3670016 | tf_op jit(solution)/shard_map/all_to_all | solution.py:504
  93.5 1.5 copy-done.3
  95.0 5.7 %shard_map.106.refs_0_ = bf16[512,1024]{1,0:T(8,128)(2,1)} custom-call(bf16[8,64,1792]{2,1,0:T(8,128)(2,1)S(1)} %copy-done.3, bf16[1,1024,1792]{2,1,0:T(8,128)(2,1)} %refs_1_.9, bf16[8,64,1792]{2,1,0:T(8,128)(2,1)} %shard_map.105.refs_2_), custom_call_target="tpu_custom_call" | custom-call | tf_op jit(solution)/shard_map/pallas_call | solution.py:34
  101.7 1.9 collective-permute-done.6.refs_1_
  104.6 12.8 %shard_map.107 = (bf16[8,64,1792]{2,1,0:T(8,128)(2,1)}, bf16[8,64,1792]{2,1,0:T(8,128)(2,1)}) custom-call(bf16[512,1024]{1,0:T(8,128)(2,1)} %shard_map.106.refs_0_, bf16[512,1024]{1,0:T(8,128)(2,1)} %copy-done.33, bf16[256,2048]{1,0:T(8,128)(2,1)} %shard_map.98.refs_3_.refs_0_.refs_2_, bf16[256,2048]{1,0:T(8,128)(2,1)} %collective-permute-done.4.refs_1_.refs_3_, ...), custom_call_target="tpu_custom_call" | custom-call | tf_op jit(solution)/shard_map/pallas_call | solution.py:34
  117.4 9.9 %collective-permute-done.7.refs_2_.refs_0_ = bf16[512,512]{1,0:T(8,128)(2,1)S(1)} collective-permute-done((bf16[512,512]{1,0:T(8,128)(2,1)S(1)}, bf16[512,512]{1,0:T(8,128)(2,1)S(1)}, u32[]{:S(2)}, u32[]{:S(2)}) %collective-permute-start.7) | collective-permute-done | bytes 524320 | tf_op jit(solution)/shard_map/ppermute | solution.py:400
  128.6 4.7 %all-to-all-start.4 = ((bf16[8,64,1792]{2,1,0:T(8,128)(2,1)}), bf16[8,64,1792]{2,1,0:T(8,128)(2,1)}, u32[]{:S(2)}, u32[]{:S(2)}) async-start(bf16[8,64,1792]{2,1,0:T(8,128)(2,1)} %shard_map.108.refs_3_), calls=%async_computation.4 | async-start | bytes 3670016 | tf_op jit(solution)/shard_map/all_to_all | solution.py:504
  136.2 25.5 %collective-permute-done.8.refs_2_.refs_4_ = bf16[128,1792]{1,0:T(8,128)(2,1)S(1)} collective-permute-done((bf16[128,1792]{1,0:T(8,128)(2,1)}, bf16[128,1792]{1,0:T(8,128)(2,1)S(1)}, u32[]{:S(2)}, u32[]{:S(2)}) %collective-permute-start.8) | collective-permute-done | bytes 458784 | tf_op jit(solution)/shard_map/ppermute | solution.py:400
  161.7 2.2 %all-to-all-done.4.refs_1_.refs_0_.refs_4_ = bf16[8,64,1792]{2,1,0:T(8,128)(2,1)} async-done(((bf16[8,64,1792]{2,1,0:T(8,128)(2,1)}), bf16[8,64,1792]{2,1,0:T(8,128)(2,1)}, u32[]{:S(2)}, u32[]{:S(2)}) %all-to-all-start.4) | async-done | bytes 1835040 | tf_op jit(solution)/shard_map/all_to_all | solution.py:504
  164.0 7.4 %all-to-all-start.5 = ((bf16[8,64,1792]{2,1,0:T(8,128)(2,1)}), bf16[8,64,1792]{2,1,0:T(8,128)(2,1)}, u32[]{:S(2)}, u32[]{:S(2)}) async-start(bf16[8,64,1792]{2,1,0:T(8,128)(2,1)} %shard_map.110.refs_2_), calls=%async_computation.5 | async-start | bytes 3670016 | tf_op jit(solution)/shard_map/all_to_all | solution.py:504
  171.4 2.2 %shard_map.111.refs_5_ = bf16[128,1792]{1,0:T(8,128)(2,1)} custom-call(bf16[8,64,1792]{2,1,0:T(8,128)(2,1)} %all-to-all-done.4.refs_1_.refs_0_.refs_4_, bf16[128,256]{1,0:T(8,128)(2,1)S(1)} %copy-done.22, bf16[8,64,1792]{2,1,0:T(8,128)(2,1)} %shard_map.110.refs_2_), custom_call_target="tpu_custom_call" | custom-call | tf_op jit(solution)/shard_map/pallas_call | solution.py:34
  176.0 8.0 %shard_map.112.refs_6_ = bf16[1,1024,1792]{2,1,0:T(8,128)(2,1)} custom-call(s32[2]{0:T(128)S(1)} %pad_add_fusion.1.where_ref, bf16[512,1024]{1,0:T(8,128)(2,1)} %get-tuple-element.48.hidden_ref, bf16[512,512]{1,0:T(8,128)(2,1)S(1)} %collective-permute-done.7.refs_2_.refs_0_, bf16[512,512]{1,0:T(8,128)(2,1)S(1)} %collective-permute-done.10.refs_1_, ...), custom_call_target="tpu_custom_call" | custom-call | tf_op jit(solution)/shard_map/pallas_call | solution.py:379
  184.0 15.9 %collective-permute-done.9.refs_5_ = bf16[128,1792]{1,0:T(8,128)(2,1)S(1)} collective-permute-done((bf16[128,1792]{1,0:T(8,128)(2,1)}, bf16[128,1792]{1,0:T(8,128)(2,1)S(1)}, u32[]{:S(2)}, u32[]{:S(2)}) %collective-permute-start.9) | collective-permute-done | bytes 458784 | tf_op jit(solution)/shard_map/ppermute | solution.py:400
  199.9 2.2 %all-to-all-done.5.refs_0_ = bf16[8,64,1792]{2,1,0:T(8,128)(2,1)} async-done(((bf16[8,64,1792]{2,1,0:T(8,128)(2,1)}), bf16[8,64,1792]{2,1,0:T(8,128)(2,1)}, u32[]{:S(2)}, u32[]{:S(2)}) %all-to-all-start.5) | async-done | bytes 1835040 | tf_op jit(solution)/shard_map/all_to_all | solution.py:504
  202.2 2.7 %shard_map.113 = (bf16[128,1792]{1,0:T(8,128)(2,1)}, bf16[128,1792]{1,0:T(8,128)(2,1)}) custom-call(bf16[8,64,1792]{2,1,0:T(8,128)(2,1)} %all-to-all-done.5.refs_0_, bf16[128,256]{1,0:T(8,128)(2,1)S(1)} %copy-done.20, bf16[128,256]{1,0:T(8,128)(2,1)S(1)} %copy-done.21, bf16[128,256]{1,0:T(8,128)(2,1)S(1)} %copy-done.19, ...), custom_call_target="tpu_custom_call" | custom-call | tf_op jit(solution)/shard_map/pallas_call | solution.py:34
  (97 shorter events, 18.9 us)
Async XLA Ops:
  0.6 24.8 %copy-start.12 = (bf16[128,1792]{1,0:T(8,128)(2,1)S(1)}, bf16[128,1792]{1,0:T(8,128)(2,1)}, u32[]{:S(2)}) copy-start(bf16[128,1792]{1,0:T(8,128)(2,1)} %refs_1_.7) | copy-start | bytes 1376260
  0.6 24.8 %collective-permute-start.2 = (bf16[128,1792]{1,0:T(8,128)(2,1)}, bf16[128,1792]{1,0:T(8,128)(2,1)S(1)}, u32[]{:S(2)}, u32[]{:S(2)}) collective-permute-start(bf16[128,1792]{1,0:T(8,128)(2,1)} %refs_3_.1), channel_id=1, source_target_pairs={{0,8},{1,9},{2,10},{3,11},{4,12},{5,13},{6,14},{7,15},{8,0},{9,1},... | collective-permute-start | bytes 1376264 | tf_op jit(solution)/shard_map/ppermute | solution.py:400
  4.7 21.6 %collective-permute-start = (s32[2,128]{1,0:T(2,128)}, s32[2,128]{1,0:T(2,128)S(1)}, u32[]{:S(2)}, u32[]{:S(2)}) collective-permute-start(s32[2,128]{1,0:T(2,128)} %bitcast.6), channel_id=1, source_target_pairs={{0,8},{1,9},{2,10},{3,11},{4,12},{5,13},{6,14},{7,15},{8,0},{9,1},... | collective-permute-start | bytes 3080 | tf_op jit(solution)/shard_map/ppermute | solution.py:400
  4.8 21.5 %collective-permute-start.1 = (f32[2,128]{1,0:T(2,128)}, f32[2,128]{1,0:T(2,128)S(1)}, u32[]{:S(2)}, u32[]{:S(2)}) collective-permute-start(f32[2,128]{1,0:T(2,128)} %bitcast.8), channel_id=1, source_target_pairs={{0,8},{1,9},{2,10},{3,11},{4,12},{5,13},{6,14},{7,15},{8,0},{9,1},... | collective-permute-start | bytes 3080 | tf_op jit(solution)/shard_map/ppermute | solution.py:400
  12.1 14.2 %copy-start.14 = (bf16[8,32,1792]{2,1,0:T(8,128)(2,1)S(1)}, bf16[8,32,1792]{2,1,0:T(8,128)(2,1)}, u32[]{:S(2)}) copy-start(bf16[8,32,1792]{2,1,0:T(8,128)(2,1)} %get-tuple-element.29.refs_4_) | copy-start | bytes 2752516
  12.1 24.8 %all-to-all-start = ((bf16[8,32,1792]{2,1,0:T(8,128)(2,1)}), bf16[8,32,1792]{2,1,0:T(8,128)(2,1)S(1)}, u32[]{:S(2)}, u32[]{:S(2)}) async-start(bf16[8,32,1792]{2,1,0:T(8,128)(2,1)} %get-tuple-element.29.refs_4_), calls=%async_computation | async-start | bytes 1835008 | tf_op jit(solution)/shard_map/all_to_all | solution.py:504
  26.3 24.3 %collective-permute-start.3 = (bf16[128,1792]{1,0:T(8,128)(2,1)}, bf16[128,1792]{1,0:T(8,128)(2,1)}, u32[]{:S(2)}, u32[]{:S(2)}) collective-permute-start(bf16[128,1792]{1,0:T(8,128)(2,1)} %shard_map.96), channel_id=1, source_target_pairs={{0,8},{1,9},{2,10},{3,11},{4,12},{5,13},{6,14},{7,15},{8,0},{9,1},... | collective-permute-start | bytes 1376264 | tf_op jit(solution)/shard_map/ppermute | solution.py:400
  36.9 21.9 %all-to-all-start.1 = ((bf16[8,32,1792]{2,1,0:T(8,128)(2,1)}), bf16[8,32,1792]{2,1,0:T(8,128)(2,1)S(1)}, u32[]{:S(2)}, u32[]{:S(2)}) async-start(bf16[8,32,1792]{2,1,0:T(8,128)(2,1)} %shard_map.97.refs_2_), calls=%async_computation.1 | async-start | bytes 1835008 | tf_op jit(solution)/shard_map/all_to_all | solution.py:504
  41.1 6.8 %copy-start.18 = (f32[256,1]{1,0:T(8,128)S(1)}, f32[256,1]{1,0:T(8,128)}, u32[]{:S(2)}) copy-start(f32[256,1]{1,0:T(8,128)} %get-tuple-element.33.refs_2_) | copy-start | bytes 3076
  41.1 9.4 %copy-start.29 = (f32[256,1]{1,0:T(8,128)S(1)}, f32[256,1]{1,0:T(8,128)}, u32[]{:S(2)}) copy-start(f32[256,1]{1,0:T(8,128)} %get-tuple-element.28.refs_2_) | copy-start | bytes 3076
  41.1 9.4 %copy-start.30 = (bf16[256,128]{1,0:T(8,128)(2,1)S(1)}, bf16[256,128]{1,0:T(8,128)(2,1)}, u32[]{:S(2)}) copy-start(bf16[256,128]{1,0:T(8,128)(2,1)} %get-tuple-element.27.refs_0_) | copy-start | bytes 196612
  41.1 9.4 %copy-start.31 = (f32[256,1]{1,0:T(8,128)S(1)}, f32[256,1]{1,0:T(8,128)}, u32[]{:S(2)}) copy-start(f32[256,1]{1,0:T(8,128)} %get-tuple-element.31.refs_5_) | copy-start | bytes 3076
  41.1 9.4 %copy-start.32 = (bf16[256,128]{1,0:T(8,128)(2,1)S(1)}, bf16[256,128]{1,0:T(8,128)(2,1)}, u32[]{:S(2)}) copy-start(bf16[256,128]{1,0:T(8,128)(2,1)} %get-tuple-element.30.refs_3_) | copy-start | bytes 196612
  59.7 27.1 %all-to-all-start.2 = ((bf16[8,64,1792]{2,1,0:T(8,128)(2,1)}), bf16[8,64,1792]{2,1,0:T(8,128)(2,1)S(1)}, u32[]{:S(2)}, u32[]{:S(2)}) async-start(bf16[8,64,1792]{2,1,0:T(8,128)(2,1)} %shard_map.101.refs_2_), calls=%async_computation.2 | async-start | bytes 3670016 | tf_op jit(solution)/shard_map/all_to_all | solution.py:504
  63.5 11.9 %collective-permute-start.4 = (bf16[256,2048]{1,0:T(8,128)(2,1)S(1)}, bf16[256,2048]{1,0:T(8,128)(2,1)}, u32[]{:S(2)}, u32[]{:S(2)}) collective-permute-start(bf16[256,2048]{1,0:T(8,128)(2,1)S(1)} %copy-done.5), channel_id=1, source_target_pairs={{0,16},{16,0},{1,17},{17,1},{2,18},{18,2},{3,19},{19,3},{4,20},{20... | collective-permute-start | bytes 3145736 | tf_op jit(solution)/shard_map/ppermute | solution.py:400
  64.7 7.1 %copy-start.17 = (f32[256,1]{1,0:T(8,128)S(1)}, f32[256,1]{1,0:T(8,128)}, u32[]{:S(2)}) copy-start(f32[256,1]{1,0:T(8,128)} %get-tuple-element.36.refs_2_) | copy-start | bytes 3076
  64.7 7.1 %copy-start.25 = (bf16[256,128]{1,0:T(8,128)(2,1)S(1)}, bf16[256,128]{1,0:T(8,128)(2,1)}, u32[]{:S(2)}) copy-start(bf16[256,128]{1,0:T(8,128)(2,1)} %get-tuple-element.35.refs_0_) | copy-start | bytes 196612
  71.3 4.0 %collective-permute-start.5 = (bf16[256,2048]{1,0:T(8,128)(2,1)}, bf16[256,2048]{1,0:T(8,128)(2,1)}, u32[]{:S(2)}, u32[]{:S(2)}) collective-permute-start(bf16[256,2048]{1,0:T(8,128)(2,1)} %shard_map.102.refs_3_.refs_2_.refs_4_), channel_id=1, source_target_pairs={{0,16},{16,0},{1,17},{17,1},{2,18},{18,2},{3,19},{19,3},{4,20},{20... | collective-permute-start | bytes 3145736 | tf_op jit(solution)/shard_map/ppermute | solution.py:400
  88.1 39.2 %all-to-all-start.3 = ((bf16[8,64,1792]{2,1,0:T(8,128)(2,1)}), bf16[8,64,1792]{2,1,0:T(8,128)(2,1)S(1)}, u32[]{:S(2)}, u32[]{:S(2)}) async-start(bf16[8,64,1792]{2,1,0:T(8,128)(2,1)} %shard_map.105.refs_2_), calls=%async_computation.3 | async-start | bytes 3670016 | tf_op jit(solution)/shard_map/all_to_all | solution.py:504
  95.0 9.6 %copy-start.11 = (bf16[8,32,1792]{2,1,0:T(8,128)(2,1)S(1)}, bf16[8,32,1792]{2,1,0:T(8,128)(2,1)}, u32[]{:S(2)}) copy-start(bf16[8,32,1792]{2,1,0:T(8,128)(2,1)} %shard_map.99.refs_6_.refs_8_) | copy-start | bytes 2752516
  95.0 9.6 %copy-start.15 = (bf16[8,32,1792]{2,1,0:T(8,128)(2,1)S(1)}, bf16[8,32,1792]{2,1,0:T(8,128)(2,1)}, u32[]{:S(2)}) copy-start(bf16[8,32,1792]{2,1,0:T(8,128)(2,1)} %get-tuple-element.38.refs_7_) | copy-start | bytes 2752516
  100.8 2.9 %collective-permute-start.6 = (bf16[512,1024]{1,0:T(8,128)(2,1)}, bf16[512,1024]{1,0:T(8,128)(2,1)S(1)}, u32[]{:S(2)}, u32[]{:S(2)}) collective-permute-start(bf16[512,1024]{1,0:T(8,128)(2,1)} %shard_map.106.refs_0_), channel_id=1, source_target_pairs={{0,16},{16,0},{1,17},{17,1},{2,18},{18,2},{3,19},{19,3},{4,20},{20... | collective-permute-start | bytes 3145736 | tf_op jit(solution)/shard_map/ppermute | solution.py:400
  100.8 26.5 %collective-permute-start.7 = (bf16[512,512]{1,0:T(8,128)(2,1)S(1)}, bf16[512,512]{1,0:T(8,128)(2,1)S(1)}, u32[]{:S(2)}, u32[]{:S(2)}) collective-permute-start(bf16[512,512]{1,0:T(8,128)(2,1)S(1)} %copy-done.34), channel_id=1, source_target_pairs={{0,8},{1,9},{2,10},{3,11},{4,12},{5,13},{6,14},{7,15},{8,0},{9,1},... | collective-permute-start | bytes 1572872 | tf_op jit(solution)/shard_map/ppermute | solution.py:400
  128.6 35.4 %all-to-all-start.4 = ((bf16[8,64,1792]{2,1,0:T(8,128)(2,1)}), bf16[8,64,1792]{2,1,0:T(8,128)(2,1)}, u32[]{:S(2)}, u32[]{:S(2)}) async-start(bf16[8,64,1792]{2,1,0:T(8,128)(2,1)} %shard_map.108.refs_3_), calls=%async_computation.4 | async-start | bytes 3670016 | tf_op jit(solution)/shard_map/all_to_all | solution.py:504
  134.8 26.9 %collective-permute-start.8 = (bf16[128,1792]{1,0:T(8,128)(2,1)}, bf16[128,1792]{1,0:T(8,128)(2,1)S(1)}, u32[]{:S(2)}, u32[]{:S(2)}) collective-permute-start(bf16[128,1792]{1,0:T(8,128)(2,1)} %shard_map.109), channel_id=1, source_target_pairs={{0,8},{1,9},{2,10},{3,11},{4,12},{5,13},{6,14},{7,15},{8,0},{9,1},... | collective-permute-start | bytes 1376264 | tf_op jit(solution)/shard_map/ppermute | solution.py:400
  164.0 7.4 %copy-start.22 = (bf16[128,256]{1,0:T(8,128)(2,1)S(1)}, bf16[128,256]{1,0:T(8,128)(2,1)}, u32[]{:S(2)}) copy-start(bf16[128,256]{1,0:T(8,128)(2,1)} %get-tuple-element.47.refs_1_) | copy-start | bytes 196612
  164.0 38.2 %all-to-all-start.5 = ((bf16[8,64,1792]{2,1,0:T(8,128)(2,1)}), bf16[8,64,1792]{2,1,0:T(8,128)(2,1)}, u32[]{:S(2)}, u32[]{:S(2)}) async-start(bf16[8,64,1792]{2,1,0:T(8,128)(2,1)} %shard_map.110.refs_2_), calls=%async_computation.5 | async-start | bytes 3670016 | tf_op jit(solution)/shard_map/all_to_all | solution.py:504
  171.4 3.6 %collective-permute-start.10 = (bf16[512,512]{1,0:T(8,128)(2,1)S(1)}, bf16[512,512]{1,0:T(8,128)(2,1)S(1)}, u32[]{:S(2)}, u32[]{:S(2)}) collective-permute-start(bf16[512,512]{1,0:T(8,128)(2,1)S(1)} %collective-permute-done.7.refs_2_.refs_0_), channel_id=1, source_target_pairs={{0,16},{16,0},{1,17},{17,1},{2,18},{18,2},{3,19},{19,3},{4,20},{20... | collective-permute-start | bytes 1572872 | tf_op jit(solution)/shard_map/ppermute | solution.py:400
  173.6 26.3 %collective-permute-start.9 = (bf16[128,1792]{1,0:T(8,128)(2,1)}, bf16[128,1792]{1,0:T(8,128)(2,1)S(1)}, u32[]{:S(2)}, u32[]{:S(2)}) collective-permute-start(bf16[128,1792]{1,0:T(8,128)(2,1)} %shard_map.111.refs_5_), channel_id=1, source_target_pairs={{0,8},{1,9},{2,10},{3,11},{4,12},{5,13},{6,14},{7,15},{8,0},{9,1},... | collective-permute-start | bytes 1376264 | tf_op jit(solution)/shard_map/ppermute | solution.py:400
  176.0 26.1 %copy-start.19 = (bf16[128,256]{1,0:T(8,128)(2,1)S(1)}, bf16[128,256]{1,0:T(8,128)(2,1)}, u32[]{:S(2)}) copy-start(bf16[128,256]{1,0:T(8,128)(2,1)} %get-tuple-element.46.refs_3_) | copy-start | bytes 196612
  176.0 26.1 %copy-start.20 = (bf16[128,256]{1,0:T(8,128)(2,1)S(1)}, bf16[128,256]{1,0:T(8,128)(2,1)}, u32[]{:S(2)}) copy-start(bf16[128,256]{1,0:T(8,128)(2,1)} %get-tuple-element.44.refs_1_) | copy-start | bytes 196612
  176.0 26.1 %copy-start.21 = (bf16[128,256]{1,0:T(8,128)(2,1)S(1)}, bf16[128,256]{1,0:T(8,128)(2,1)}, u32[]{:S(2)}) copy-start(bf16[128,256]{1,0:T(8,128)(2,1)} %get-tuple-element.45.refs_2_) | copy-start | bytes 196612
  (21 other events, 51.1 us)

commit v3 on v2

v3 whole, which is shorter than its diff:
```python
import jax
import jax.numpy as jnp
from jax import lax
from jax.experimental import pallas as pl
from jax.experimental.pallas import tpu as pltpu
from jax.sharding import PartitionSpec as P

BF16 = jnp.bfloat16
F32 = jnp.float32
LONG = 50_000_000_000
ANYWHERE = pl.BlockSpec(memory_space=pl.ANY)
IN_VMEM = pl.BlockSpec(memory_space=pltpu.VMEM)


def tile_of(size):
    return 256 if size % 256 == 0 else size


def wide_tile_of(size):
    return size // 2 if size % 256 == 0 else size


def run(body, out_shape, grid, in_specs, out_specs, operands, scratch=(), deps=(), aliases=None, flops=0):
    count = len(operands)
    out_shape = jax.tree.map(
        lambda x: pltpu.HBM(x.shape, x.dtype) if isinstance(x, jax.ShapeDtypeStruct) else x,
        out_shape,
        is_leaf=lambda x: not isinstance(x, (list, tuple)),
    )

    def whole(*refs):
        body(*refs[:count], *refs[count + len(deps) :])

    return pl.pallas_call(
        whole,
        out_shape=out_shape,
        grid=grid,
        in_specs=list(in_specs) + [ANYWHERE] * len(deps),
        out_specs=out_specs,
        scratch_shapes=list(scratch),
        input_output_aliases=aliases or {},
        cost_estimate=pl.CostEstimate(flops=flops, bytes_accessed=0, transcendentals=0),
        compiler_params=pltpu.CompilerParams(vmem_limit_bytes=52 * 1024 * 1024),
    )(*operands, *deps)


def tied(value, *deps, flops=0):
    shape = jax.ShapeDtypeStruct(value.shape, value.dtype)
    return run(lambda *refs: None, shape, (), [ANYWHERE], ANYWHERE, [value], (), deps, {0: 0}, flops)


def held(value, *deps):
    def body(value_ref, out):
        out[...] = value_ref[...]

    rows, width = value.shape
    block = pl.BlockSpec((rows, wide_tile_of(width)), lambda c: (0, c))
    shape = jax.ShapeDtypeStruct(value.shape, value.dtype)
    return run(body, shape, (width // wide_tile_of(width),), [block], block, [value], (), deps)


def fixed(shape):
    return pl.BlockSpec(shape, lambda *at: (0,) * len(shape))


def streamed(shape, tile, dim):
    pieces = shape[dim] // tile
    piece = tuple(tile if d == dim else shape[d] for d in (1, 2))
    return [pltpu.VMEM((pieces,) + piece, BF16), pltpu.SemaphoreType.DMA((pieces,))]


def piece_of(w_ref, held, sems, dim):
    pieces, tile = held.shape[0], held.shape[dim]

    def copy(n):
        at = pl.ds(n * tile, tile)
        source = w_ref.at[0, at, :] if dim == 1 else w_ref.at[0, :, at]
        return pltpu.make_async_copy(source, held.at[n], sems.at[n])

    @pl.when(pl.program_id(0) == 0)
    def _():
        for n in range(pieces):
            copy(n).start()

    def arrived():
        for n in range(pieces):

            @pl.when(pl.program_id(0) == n)
            def _():
                copy(n).wait()

        return held[pl.program_id(0)]

    return arrived


def gate_up_part(x, group, slots, weight, deps=()):
    peers, _, width = x.shape
    rows, columns = peers * slots, weight.shape[2]
    tile = tile_of(columns // 2) * 2

    def body(x_ref, w_ref, out, *scratch):
        piece = piece_of(w_ref, *scratch, 2)
        got = jnp.dot(x_ref[...].reshape(rows, width), piece(), preferred_element_type=F32)
        out[...] = got.astype(BF16)

    return run(
        body,
        jax.ShapeDtypeStruct((rows, columns), BF16),
        (columns // tile,),
        [
            pl.BlockSpec((peers, slots, width), lambda c: (0, group, 0)),
            ANYWHERE,
        ],
        pl.BlockSpec((rows, tile), lambda c: (0, c)),
        [x, weight],
        streamed(weight.shape, tile, 2),
        deps=deps,
    )


def total(refs):
    result = refs[0][...].astype(F32)
    for ref in refs[1:]:
        result = result + ref[...].astype(F32)
    return result


def hidden_and_out(near, far, weight, core, n_dp, peers, deps=()):
    n = len(near)
    rows = near[0].shape[0]
    _, inner, width = weight.shape
    slots = rows // peers
    share = inner // n_dp
    tile = wide_tile_of(width)

    def body(*refs):
        near_refs, far_refs = refs[:n], refs[n : 2 * n]
        core_ref, w_ref, hidden, mine, send, *scratch = refs[2 * n :]
        piece = piece_of(w_ref, *scratch, 2)

        @pl.when(pl.program_id(0) == 0)
        def _():
            for at, part_refs in ((0, near_refs), (rows, far_refs)):
                gate_up = total(part_refs)
                gate = gate_up[:, :inner]
                hidden[at : at + rows, :] = (
                    gate * jax.nn.sigmoid(gate) * gate_up[:, inner:]
                ).astype(BF16)
            first = pl.multiple_of(core_ref[0] * share, 128)
            mine[...] = hidden[:, pl.ds(first, share)]

        got = jnp.dot(hidden[...], piece(), preferred_element_type=F32).astype(BF16)
        send[:, :slots, :] = got[rows:].reshape(peers, slots, tile)
        send[:, slots:, :] = got[:rows].reshape(peers, slots, tile)

    return run(
        body,
        (
            jax.ShapeDtypeStruct((2 * rows, inner), BF16),
            jax.ShapeDtypeStruct((2 * rows, share), BF16),
            jax.ShapeDtypeStruct((peers, 2 * slots, width), BF16),
        ),
        (width // tile,),
        [fixed(p.shape) for p in (*near, *far)]
        + [pl.BlockSpec(memory_space=pltpu.SMEM), ANYWHERE],
        (
            fixed((2 * rows, inner)),
            fixed((2 * rows, share)),
            pl.BlockSpec((peers, 2 * slots, tile), lambda c: (0, 0, c)),
        ),
        [*near, *far, core, weight],
        streamed(weight.shape, tile, 2),
        deps=deps,
    )


def place_rows(pieces, place, slots, out, first):
    peers = len(pieces)
    for d, piece in enumerate(pieces):
        for b in range(2):
            at = pl.multiple_of(first + (b * peers + (place ^ d)) * slots, slots)
            out[pl.ds(at, slots), :] = piece[b * slots : (b + 1) * slots, :]


def hidden_grad_part(scalars, near, far, slots, weight, deps=(), flops=0):
    peers = len(near)
    width = near[0].shape[1]
    inner = weight.shape[1]
    rows = 2 * peers * slots
    tile = tile_of(inner)

    def body(scalar_ref, *refs):
        near_refs, far_refs = refs[:peers], refs[peers : 2 * peers]
        w_ref, out, x, *scratch = refs[2 * peers :]
        piece = piece_of(w_ref, *scratch, 1)

        @pl.when(pl.program_id(0) == 0)
        def _():
            place_rows(near_refs, scalar_ref[3], slots, x, 0)
            place_rows(far_refs, scalar_ref[3], slots, x, rows)

        got = lax.dot_general(
            x[...], piece(), (((1,), (1,)), ((), ())), preferred_element_type=F32
        )
        out[...] = got.astype(BF16)

    return run(
        body,
        [
            jax.ShapeDtypeStruct((2 * rows, inner), BF16),
            jax.ShapeDtypeStruct((2 * rows, width), BF16),
        ],
        (inner // tile,),
        [pl.BlockSpec(memory_space=pltpu.SMEM)]
        + [fixed((2 * slots, width))] * (2 * peers)
        + [ANYWHERE],
        [pl.BlockSpec((2 * rows, tile), lambda c: (0, c)), fixed((2 * rows, width))],
        [scalars, *near, *far, weight],
        streamed(weight.shape, tile, 1),
        deps,
        flops=flops,
    )


def rows_dx(grad_parts, near, far, weight, peers, deps=()):
    n = len(near)
    rows = near[0].shape[0]
    inner = grad_parts[0].shape[1]
    width = weight.shape[1]
    slots = rows // peers
    tile = tile_of(width)
    blocks = pl.BlockSpec((peers, 2 * slots, tile), lambda c: (0, 0, c))

    def body(*refs):
        grad_refs, near_refs, far_refs = refs[:n], refs[n : 2 * n], refs[2 * n : 3 * n]
        w_ref, out, both, *scratch = refs[3 * n :]
        piece = piece_of(w_ref, *scratch, 1)

        @pl.when(pl.program_id(0) == 0)
        def _():
            for at, part_refs in ((0, near_refs), (rows, far_refs)):
                hidden_grad = total([g.at[at : at + rows, :] for g in grad_refs])
                gate_up = total(part_refs)
                gate, up = gate_up[:, :inner], gate_up[:, inner:]
                sig = jax.nn.sigmoid(gate)
                gate_grad = hidden_grad * up * sig * (1.0 + gate * (1.0 - sig))
                both[at : at + rows, :inner] = gate_grad.astype(BF16)
                both[at : at + rows, inner:] = (hidden_grad * (gate * sig)).astype(BF16)

        got = lax.dot_general(
            both[...],
            piece(),
            (((1,), (1,)), ((), ())),
            preferred_element_type=F32,
        ).astype(BF16)
        out[:, :slots, :] = got[rows:].reshape(peers, slots, tile)
        out[:, slots:, :] = got[:rows].reshape(peers, slots, tile)

    return run(
        body,
        jax.ShapeDtypeStruct((peers, 2 * slots, width), BF16),
        (width // tile,),
        [fixed(p.shape) for p in (*grad_parts, *near, *far)] + [ANYWHERE],
        blocks,
        [*grad_parts, *near, *far, weight],
        [pltpu.VMEM((2 * rows, 2 * inner), BF16)] + streamed(weight.shape, tile, 1),
        deps,
    )


def give(back, group, slots, matrices, more=None, deps=()):
    peers, _, width = back.shape
    count = matrices[0].shape[0]
    tile = wide_tile_of(width)
    column = pl.BlockSpec((count, tile), lambda c: (0, c))

    def body(back_ref, *refs):
        data = back_ref[...].reshape(peers * slots, tile)
        result = jnp.dot(refs[0][...], data, preferred_element_type=F32)
        for ref in refs[1 : len(matrices)]:
            result = result + jnp.dot(ref[...], data, preferred_element_type=F32)
        if more is not None:
            result = result + refs[len(matrices)][...].astype(F32)
        refs[-1][...] = result.astype(BF16)

    return run(
        body,
        jax.ShapeDtypeStruct((count, width), BF16),
        (width // tile,),
        [pl.BlockSpec((peers, slots, tile), lambda c: (0, group, c))]
        + [fixed(m.shape) for m in matrices]
        + ([column] if more is not None else []),
        column,
        [back] + list(matrices) + ([more] if more is not None else []),
        deps=deps,
    )


def finish(back_out, back_dx, slots, weighted, plain, out_from, dx_from, deps=()):
    peers, _, width = back_out.shape
    count = plain.shape[0]
    tile = wide_tile_of(width)
    column = pl.BlockSpec((count, tile), lambda c: (0, c))

    def body(back_ref, back_dx_ref, high, low, plain_ref, out_ref, dx_ref, layer_out, token_grad):
        rows = back_ref[...].reshape(peers * slots, tile)
        result = jnp.dot(high[...], rows, preferred_element_type=F32)
        result = result + jnp.dot(low[...], rows, preferred_element_type=F32)
        layer_out[...] = (result + out_ref[...].astype(F32)).astype(BF16)
        rows = back_dx_ref[...].reshape(peers * slots, tile)
        result = jnp.dot(plain_ref[...], rows, preferred_element_type=F32)
        token_grad[...] = (result + dx_ref[...].astype(F32)).astype(BF16)

    return run(
        body,
        [jax.ShapeDtypeStruct((count, width), BF16)] * 2,
        (width // tile,),
        [pl.BlockSpec((peers, slots, tile), lambda c: (0, 1, c))] * 2
        + [fixed(plain.shape)] * 3
        + [column] * 2,
        [column] * 2,
        [back_out, back_dx, *weighted, plain, out_from, dx_from],
        deps=deps,
    )


def expert_grad(where, hidden, far_shares, own, there, slots, deps=(), flops=0):
    n, peers = len(far_shares), len(there)
    rows, width = own.shape
    share = hidden.shape[1] // n
    tile = wide_tile_of(width)

    def body(where_ref, hidden_ref, *refs):
        share_refs, own_ref = refs[:n], refs[n]
        there_refs = refs[n + 1 : n + 1 + peers]
        out, left, right = refs[-3:]
        moved = where_ref[1] != 0
        at = pl.program_id(1)

        @pl.when(pl.program_id(0) == 0)
        def _():
            @pl.when(jnp.logical_not(moved))
            def _():
                left[at] = hidden_ref[...].astype(F32).T.astype(BF16)

            for d in range(n):
                @pl.when(jnp.logical_and(moved, at == d))
                def _():
                    left[at] = share_refs[d][...].astype(F32).T.astype(BF16)

        @pl.when(jnp.logical_and(moved, at == 0))
        def _():
            place_rows([r.at[2 * slots :, :] for r in there_refs], where_ref[2], slots, right, 0)
            place_rows(there_refs, where_ref[2], slots, right, rows // 2)

        @pl.when(jnp.logical_and(jnp.logical_not(moved), at == 0))
        def _():
            right[...] = own_ref[...]

        out[0] = jnp.dot(left[at], right[...], preferred_element_type=F32).astype(BF16)

    def place(d, where):
        return lax.rem(where[0] - d + n, n)

    return pl.pallas_call(
        body,
        out_shape=pltpu.HBM((1, hidden.shape[1], width), BF16),
        grid_spec=pltpu.PrefetchScalarGridSpec(
            num_scalar_prefetch=1,
            grid=(width // tile, n),
            in_specs=[pl.BlockSpec((rows, share), lambda c, d, w: (0, place(d, w)))]
            + [pl.BlockSpec((rows, share), lambda c, d, w: (0, 0))] * n
            + [pl.BlockSpec((rows, tile), lambda c, d, w: (0, c))]
            + [pl.BlockSpec((4 * slots, tile), lambda c, d, w: (0, c))] * peers
            + [ANYWHERE] * len(deps),
            out_specs=pl.BlockSpec((1, share, tile), lambda c, d, w: (0, place(d, w), c)),
            scratch_shapes=[pltpu.VMEM((n, share, rows), BF16), pltpu.VMEM((rows, tile), BF16)],
        ),
        cost_estimate=pl.CostEstimate(flops=flops, bytes_accessed=0, transcendentals=0),
        compiler_params=pltpu.CompilerParams(vmem_limit_bytes=52 * 1024 * 1024),
    )(where, hidden, *far_shares, own, *there, *deps)


def crossed(block, axis, distance):
    size = lax.axis_size(axis)
    return lax.ppermute(block, axis, [(i, (i + distance) % size) for i in range(size)])


def over_dp(part):
    parts = [part] + [crossed(part, "dp", d) for d in range(1, lax.axis_size("dp"))]
    if len(parts) > 2:
        parts = [sum(p.astype(F32) for p in parts)]
    return parts


def chosen(routes, weights, expert, slots):
    count = routes[0].shape[1]
    earlier = lax.broadcasted_iota(jnp.int32, (count, count), 0)
    later = lax.broadcasted_iota(jnp.int32, (count, count), 1)
    before = (earlier < later).astype(F32).astype(BF16)
    peers = expert.shape[0]
    expert = expert.astype(F32)
    member = jnp.zeros((peers, count), F32)
    table = jnp.zeros((peers, count), F32)
    for route, weight in zip(routes, weights):
        named = route == expert
        member = jnp.where(named, 1.0, member)
        table = jnp.where(named, weight, table)
    place = jnp.dot(member.astype(BF16), before, preferred_element_type=F32)
    place = jnp.where(member > 0.0, place, -1.0)
    slot = lax.broadcasted_iota(jnp.int32, (slots, count), 0).astype(F32)
    hits = [slot == place[e : e + 1, :] for e in range(peers)]
    sel = jnp.concatenate([jnp.where(hit, 1.0, 0.0) for hit in hits], axis=0)
    weighted = [jnp.where(hit, table[e : e + 1, :], 0.0) for e, hit in enumerate(hits)]
    return sel, jnp.concatenate(weighted, axis=0)


def dispatch_tokens(table, first, peers, slots, tokens, deps=(), flops=0):
    count, width = tokens.shape
    top_count = table.shape[0] // 2
    rows = peers * slots

    def body(first_ref, table_ref, tokens_ref, send, plain, high, low):
        names = [table_ref[k : k + 1, :] for k in range(2 * top_count)]
        expert = first_ref[0] + lax.broadcasted_iota(jnp.int32, (peers, count), 0)
        sel, weighted = chosen(names[:top_count], names[top_count:], expert, slots)
        got = jnp.dot(sel.astype(BF16), tokens_ref[...], preferred_element_type=F32)
        send[...] = got.astype(BF16).reshape(peers, slots, width)
        plain[...] = sel.T.astype(BF16)
        turned = weighted.T
        top = turned.astype(BF16)
        high[...] = top
        low[...] = (turned - top.astype(F32)).astype(BF16)

    shapes = [((peers, slots, width), BF16)] + [((count, rows), BF16)] * 3
    return run(
        body,
        [jax.ShapeDtypeStruct(*shape) for shape in shapes],
        (1,),
        [pl.BlockSpec(memory_space=pltpu.SMEM), fixed(table.shape), fixed(tokens.shape)],
        [fixed(shape) for shape, _ in shapes],
        [first, table, tokens],
        deps=deps,
        flops=flops,
    )


def dispatch_grads(scalars, table, table_next, own, beside, peers, slots, into=None, deps=(), flops=0):
    top_count = table.shape[0] // 2
    count, width = own.shape

    def body(scalar_ref, table_ref, next_ref, own_ref, beside_ref, *refs):
        *outs, data, names = refs[len(into or ()) :]
        for swap in (0, 1):

            @pl.when(scalar_ref[2] == swap)
            def _():
                for m in range(2):
                    data[m] = (own_ref, beside_ref)[m ^ swap][...]
                    names[m] = (table_ref, next_ref)[m ^ swap][...]

        place = lax.broadcasted_iota(jnp.int32, (peers, count), 0) ^ scalar_ref[3]
        for b in range(2):
            route = [names[b, k : k + 1, :] for k in range(top_count)]
            weight = [names[b, top_count + k : top_count + k + 1, :] for k in range(top_count)]
            for trade in (0, 1):
                sel, weighted = chosen(route, weight, scalar_ref[trade] + place, slots)
                got = jnp.dot(sel.astype(BF16), data[b], preferred_element_type=F32)
                got = (got * jnp.sum(weighted, axis=1, keepdims=True)).astype(BF16)
                for d in range(peers):
                    out = outs[trade * peers + d]
                    out[b * slots : (b + 1) * slots, :] = got[d * slots : (d + 1) * slots, :]

    operands = [scalars, table, table_next, own, beside]
    specs = [pl.BlockSpec(memory_space=pltpu.SMEM)] + [fixed(x.shape) for x in operands[1:]]
    part = 0 if into is None else 1
    aliases = {len(operands) + d: peers + d for d in range(peers * part)}
    out = run(
        body,
        [jax.ShapeDtypeStruct((2 * slots, width), BF16)] * peers
        + [jax.ShapeDtypeStruct((4 * slots, width), BF16)] * peers,
        (1,),
        specs + [ANYWHERE] * (peers * part),
        [fixed((2 * slots, width))] * peers
        + [pl.BlockSpec((2 * slots, width), lambda c: (part, 0))] * peers,
        operands + list(into or ()),
        [pltpu.VMEM((2, count, width), BF16), pltpu.VMEM((2, 2 * top_count, count), F32)],
        deps,
        aliases,
        flops,
    )
    return out[:peers], out[peers:]


def on_device(tokens, out_grad, gate_up_weight, down_weight, routes, route_weight, swapped):
    experts = lax.axis_size("expert")
    n_dp = lax.axis_size("dp")
    half, plane = experts // 2, experts // 4
    token_count = tokens.shape[0]
    top_count = routes.shape[1]
    slots = max(16, 2 * token_count * top_count // experts)
    me = lax.axis_index("expert").astype(jnp.int32)
    core = lax.axis_index("dp").astype(jnp.int32)
    moved = jnp.any(swapped == me % half).astype(jnp.int32)
    here = (me // half) * half
    layer = (me // plane) * plane
    halves = [[s * half + j for j in range(half)] for s in range(2)]

    def cross(x):
        return crossed(x, "expert", half)

    def beside(x):
        return lax.ppermute(x, "expert", [(i, i ^ plane) for i in range(experts)])

    def exchange(x):
        return lax.all_to_all(
            x, "expert", split_axis=0, concat_axis=0, tiled=True, axis_index_groups=halves
        )

    def over_plane(pieces):
        return [pieces[0]] + [
            lax.ppermute(pieces[d], "expert", [(i, i ^ d) for i in range(experts)])
            for d in range(1, plane)
        ]

    tokens_far = cross(tokens)
    table = jnp.concatenate([routes.T.astype(F32), route_weight.T], axis=0)
    table_far = cross(table)
    table_beside = beside(table)
    table_corner = lax.ppermute(
        table, "expert", [(i, (i ^ plane) ^ half) for i in range(experts)]
    )
    grad_beside = beside(out_grad)
    first_at = here.reshape(1)
    scalars = jnp.stack([layer, (layer + half) % experts, (me // plane) % 2, me % plane])
    where = jnp.stack([core, moved, me % plane])

    send_1, back_sel_n, *back_wt_n = dispatch_tokens(table, first_at, half, slots, tokens)
    first = exchange(send_1)
    send_near, trade_near = dispatch_grads(
        scalars, table, table_beside, out_grad, grad_beside, plane, slots, deps=(send_1, table_corner)
    )
    grads_near = over_plane(send_near)
    grad_copy = held(out_grad, tokens_far, send_near[0])
    grad_far = cross(grad_copy)
    send_2, back_sel_f, *back_wt_f = dispatch_tokens(
        table_far, first_at, half, slots, tokens_far, deps=(grad_copy,), flops=LONG
    )
    send_2 = tied(send_2, first)
    second = exchange(send_2)
    part_n = gate_up_part(first, 0, slots, gate_up_weight, deps=(send_2,))
    parts_n = over_dp(part_n)
    grad_far = tied(grad_far, part_n, flops=LONG)
    far_beside = beside(grad_far)
    part_f = gate_up_part(second, 0, slots, gate_up_weight, deps=(part_n,))
    parts_f = over_dp(part_f)

    send_far, trade = dispatch_grads(
        scalars,
        table_far,
        table_corner,
        grad_far,
        far_beside,
        plane,
        slots,
        into=trade_near,
        deps=(part_f, *grads_near[1:]),
        flops=LONG,
    )
    grads_far = over_plane(send_far)
    hidden, share, send_4 = hidden_and_out(
        parts_n, parts_f, down_weight, core.reshape(1), n_dp, half, deps=(send_far[0],)
    )
    far_share = cross(share)
    send_4 = tied(send_4, second)
    fourth = exchange(send_4)

    grad_part, grads = hidden_grad_part(
        scalars, grads_near, grads_far, slots, down_weight, deps=(send_4,), flops=LONG
    )
    grad_parts = over_dp(grad_part)
    far_share = tied(far_share, flops=LONG)
    send_5 = rows_dx(grad_parts, parts_n, parts_f, gate_up_weight, half, deps=(far_share,))
    send_5 = tied(send_5, fourth)
    fifth = exchange(send_5)
    far_shares = [far_share] + [crossed(far_share, "dp", d) for d in range(1, n_dp)]
    give_out = give(fourth, 0, slots, back_wt_f, deps=(send_5,))
    out_from = cross(give_out)

    give_dx = give(fifth, 0, slots, [back_sel_f], deps=(out_from,))
    dx_from = cross(give_dx)
    down_grad = expert_grad(
        where, hidden, far_shares, grads, over_plane(trade), slots, deps=(give_dx,)
    )
    layer_out, token_grad = finish(
        fourth, fifth, slots, back_wt_n, back_sel_n, out_from, dx_from, deps=(down_grad,)
    )
    return layer_out, token_grad, down_grad


def solution(mesh):
    return jax.shard_map(
        on_device,
        mesh=mesh,
        in_specs=(
            P("expert", "dp"),
            P("expert", "dp"),
            P("expert", "dp", None),
            P("expert", None, "dp"),
            P("expert", None),
            P("expert", None),
            P(),
        ),
        out_specs=(P("expert", "dp"), P("expert", "dp"), P("expert", None, "dp")),
        check_vma=False,
    )
```

time: 206 us -> 187 us (0.908)
  waiting for transfers between devices: 82.5 us -> 68 us
  Pallas kernels: 65.4 us -> 58.2 us
  starting transfers between devices: 40.3 us -> 47.2 us
  local copies, waits for them, and re-layouts: 14.3 us -> 8.72 us
    ppermute x11 -> x10, waiting for transfers between devices: 61.8 us -> 42.7 us  [crossed(): lax.ppermute(block, axis, [(i, (i + distance) % size) for i in range(size)])]
    ppermute x0 -> x13, waiting for transfers between devices: none -> 17.8 us  [the longest x1 9.25 us: on_device(): lax.ppermute(table, 'expert', [(i, i ^ plane ^ half) for i in range(exper...]
    ppermute x0 -> x13, starting transfers between devices: none -> 14.6 us  [the longest x9 10.6 us: over_plane(): lax.ppermute(pieces[d], 'expert', [(i, i ^ d) for i in range(experts)])]
    all_to_all x6 -> x4, waiting for transfers between devices: 20.8 us -> 7.46 us  [exchange(): lax.all_to_all(x, 'expert', split_axis=0, concat_axis=0, tiled=True, axis...]
    all_to_all x6 -> x4, starting transfers between devices: 30.3 us -> 18.2 us  [exchange(): lax.all_to_all(x, 'expert', split_axis=0, concat_axis=0, tiled=True, axis...]
    pallas_call x19 -> x18, Pallas kernels: 57.4 us -> 50.7 us  [run(): pl.pallas_call(whole, out_shape=out_shape, grid=grid, in_specs=list(in_sp...]
    unnamed x72 -> x60, local copies, waits for them, and re-layouts: 14.3 us -> 8.72 us
    ppermute x11 -> x10, starting transfers between devices: 10 us -> 14.4 us  [crossed(): lax.ppermute(block, axis, [(i, (i + distance) % size) for i in range(size)])]
  transfers between devices with their start and end apart: 17 -> 27, of which waited for: 10 -> 11; matrix products, arithmetic and copies ran while one was open for 0% -> 1% of each run, Pallas kernels for 31% -> 30%
where the time goes in v3:
time: 187 us; the launch traced here: 186 us
  waiting for transfers between devices  68 us (36%)
  Pallas kernels  58.2 us (31%)
  starting transfers between devices  47.2 us (25%)
  local copies, waits for them, and re-layouts  8.72 us (5%)
  other arithmetic  2.15 us (1%)
    pallas_call x18, Pallas kernels, run(): pl.pallas_call(whole, out_shape=out_shape, grid=grid, in_specs=list(in_sp...  50.7 us
    ppermute x10, waiting for transfers between devices, crossed(): lax.ppermute(block, axis, [(i, (i + distance) % size) for i in range(size)])  42.7 us
    all_to_all x4, starting transfers between devices, exchange(): lax.all_to_all(x, 'expert', split_axis=0, concat_axis=0, tiled=True, axis...  18.2 us
    ppermute x10, starting transfers between devices, crossed(): lax.ppermute(block, axis, [(i, (i + distance) % size) for i in range(size)])  14.4 us
    ppermute x9, starting transfers between devices, over_plane(): lax.ppermute(pieces[d], 'expert', [(i, i ^ d) for i in range(experts)])  10.6 us
    ppermute x1, waiting for transfers between devices, on_device(): lax.ppermute(table, 'expert', [(i, i ^ plane ^ half) for i in range(exper...  9.25 us
    unnamed x60, local copies, waits for them, and re-layouts  8.72 us
    ppermute x9, waiting for transfers between devices, over_plane(): lax.ppermute(pieces[d], 'expert', [(i, i ^ d) for i in range(experts)])  7.89 us
  transfers between devices with their start and end apart: 27, of which 11 were waited for; matrix products, arithmetic and copies ran while one was open for 1% of the time, Pallas kernels for 30%

profile of v3, /device:TPU:0, one launch (start us, length us, event | category | flops | bytes accessed | tf_op | source)
XLA Modules:
  0.0 185.8 jit_solution(4127938850404023516)
XLA Ops:
  0.6 3.1 %collective-permute-start.3 = (bf16[128,1792]{1,0:T(8,128)(2,1)}, bf16[128,1792]{1,0:T(8,128)(2,1)S(1)}, u32[]{:S(2)}, u32[]{:S(2)}) collective-permute-start(bf16[128,1792]{1,0:T(8,128)(2,1)} %refs_0_.1), channel_id=1, source_target_pairs={{0,4},{1,5},{2,6},{3,7},{4,0},{5,1},{6,2},{7,3},{8,12},{9,13},{10,... | collective-permute-start | bytes 1376264 | tf_op jit(solution)/shard_map/ppermute | solution.py:514
  3.7 2.6 %collective-permute-start.1 = (bf16[128,1792]{1,0:T(8,128)(2,1)}, bf16[128,1792]{1,0:T(8,128)(2,1)S(1)}, u32[]{:S(2)}, u32[]{:S(2)}) collective-permute-start(bf16[128,1792]{1,0:T(8,128)(2,1)} %refs_2_.1), channel_id=1, source_target_pairs={{0,8},{1,9},{2,10},{3,11},{4,12},{5,13},{6,14},{7,15},{8,0},{9,1},... | collective-permute-start | bytes 1376264 | tf_op jit(solution)/shard_map/ppermute | solution.py:387
  8.6 3.5 %collective-permute-start = (f32[4,128]{1,0:T(4,128)S(1)}, f32[4,128]{1,0:T(4,128)S(1)}, u32[]{:S(2)}, u32[]{:S(2)}) collective-permute-start(f32[4,128]{1,0:T(4,128)S(1)} %pad_maximum_fusion.refs_1_), channel_id=1, source_target_pairs={{0,8},{1,9},{2,10},{3,11},{4,12},{5,13},{6,14},{7,15},{8,0},{9,1},... | collective-permute-start | bytes 6152 | tf_op jit(solution)/shard_map/ppermute | solution.py:387
  14.5 3.9 %all-to-all-start = ((bf16[8,32,1792]{2,1,0:T(8,128)(2,1)}), bf16[8,32,1792]{2,1,0:T(8,128)(2,1)S(1)}, u32[]{:S(2)}, u32[]{:S(2)}) async-start(bf16[8,32,1792]{2,1,0:T(8,128)(2,1)} %get-tuple-element.34.refs_5_), calls=%async_computation | async-start | bytes 1835008 | tf_op jit(solution)/shard_map/all_to_all | solution.py:517
  18.5 9.2 %collective-permute-done.4.refs_6_.refs_2_ = f32[4,128]{1,0:T(4,128)S(1)} collective-permute-done((f32[4,128]{1,0:T(4,128)S(1)}, f32[4,128]{1,0:T(4,128)S(1)}, u32[]{:S(2)}, u32[]{:S(2)}) %collective-permute-start.4) | collective-permute-done | bytes 2080 | tf_op jit(solution)/shard_map/ppermute | solution.py:531
  27.7 2.7 %shard_map.95 = (bf16[64,1792]{1,0:T(8,128)(2,1)}, bf16[64,1792]{1,0:T(8,128)(2,1)}, bf16[64,1792]{1,0:T(8,128)(2,1)}, bf16[64,1792]{1,0:T(8,128)(2,1)}, bf16[12...) custom-call(s32[4]{0:T(128)S(1)} %pad_add_fusion.refs_0_, ...), custom_call_target="tpu_custom_call" | custom-call | tf_op jit(solution)/shard_map/pallas_call | solution.py:34
  34.0 1.5 shard_map.97
  36.7 3.8 %all-to-all-start.1 = ((bf16[8,32,1792]{2,1,0:T(8,128)(2,1)}), bf16[8,32,1792]{2,1,0:T(8,128)(2,1)S(1)}, u32[]{:S(2)}, u32[]{:S(2)}) async-start(bf16[8,32,1792]{2,1,0:T(8,128)(2,1)} %shard_map.98.refs_2_), calls=%async_computation.1 | async-start | bytes 1835008 | tf_op jit(solution)/shard_map/all_to_all | solution.py:517
  40.5 5.1 %shard_map.99.refs_2_.refs_1_.refs_0_ = bf16[256,2048]{1,0:T(8,128)(2,1)} custom-call(bf16[8,32,1792]{2,1,0:T(8,128)(2,1)S(1)} %all-to-all-done.refs_1_.refs_0_, bf16[1,1792,2048]{2,1,0:T(8,128)(2,1)} %refs_6_.1, bf16[8,32,1792]{2,1,0:T(8,128)(2,1)S(1)} %copy-done.1), custom_call_target="tpu_custom_call" | custom-call | tf_op jit(solution)/shard_map/pallas_call | solution.py:34
  45.6 7.8 %collective-permute-done.7.refs_0_ = bf16[128,1792]{1,0:T(8,128)(2,1)} collective-permute-done((bf16[128,1792]{1,0:T(8,128)(2,1)}, bf16[128,1792]{1,0:T(8,128)(2,1)}, u32[]{:S(2)}, u32[]{:S(2)}) %collective-permute-start.7) | collective-permute-done | bytes 458784 | tf_op jit(solution)/shard_map/ppermute | solution.py:387
  53.4 1.5 collective-permute-start.10
  56.9 4.1 %all-to-all-done.1.refs_0_.refs_1_ = bf16[8,32,1792]{2,1,0:T(8,128)(2,1)S(1)} async-done(((bf16[8,32,1792]{2,1,0:T(8,128)(2,1)}), bf16[8,32,1792]{2,1,0:T(8,128)(2,1)S(1)}, u32[]{:S(2)}, u32[]{:S(2)}) %all-to-all-start.1) | async-done | bytes 917536 | tf_op jit(solution)/shard_map/all_to_all | solution.py:517
  61.0 5.1 %shard_map.100.refs_9_.refs_2_.refs_4_ = bf16[256,2048]{1,0:T(8,128)(2,1)} custom-call(bf16[8,32,1792]{2,1,0:T(8,128)(2,1)S(1)} %all-to-all-done.1.refs_0_.refs_1_, bf16[1,1792,2048]{2,1,0:T(8,128)(2,1)} %refs_6_.1, bf16[256,2048]{1,0:T(8,128)(2,1)} %shard_map.99.refs_2_.refs_1_.refs_0_), custom_call_target="tpu_custom_call" | custom-call | tf_op jit(solution)/shard_map/pallas_call | solution.py:34
  67.4 3.2 %shard_map.102 = (bf16[64,1792]{1,0:T(8,128)(2,1)}, bf16[64,1792]{1,0:T(8,128)(2,1)}, bf16[64,1792]{1,0:T(8,128)(2,1)}, bf16[64,1792]{1,0:T(8,128)(2,1)}, bf16[1...) custom-call(s32[4]{0:T(128)S(1)} %pad_add_fusion.refs_0_, ...), custom_call_target="tpu_custom_call", output_to_operand_aliasing={{4}: (5, {}), {5}: (6, {}), {6}: (7, {}), {7}: (8, {})} | custom-call | flops 49999998976 | tf_op jit(solution)/shard_map/pallas_call | solution.py:34
  70.6 1.6 collective-permute-start.12
  72.2 1.9 %collective-permute-start.13 = (bf16[64,1792]{1,0:T(8,128)(2,1)}, bf16[64,1792]{1,0:T(8,128)(2,1)}, u32[]{:S(2)}, u32[]{:S(2)}) collective-permute-start(bf16[64,1792]{1,0:T(8,128)(2,1)} %get-tuple-element.47), channel_id=1, source_target_pairs={{0,2},{1,3},{2,0},{3,1},{4,6},{5,7},{6,4},{7,5},{8,10},{9,11},{10,... | collective-permute-start | bytes 688136 | tf_op jit(solution)/shard_map/ppermute | solution.py:523
  76.0 7.2 %shard_map.103 = (bf16[512,1024]{1,0:T(8,128)(2,1)}, bf16[512,512]{1,0:T(8,128)(2,1)}, bf16[8,64,1792]{2,1,0:T(8,128)(2,1)}) custom-call(bf16[256,2048]{1,0:T(8,128)(2,1)} %shard_map.99.refs_2_.refs_1_.refs_0_, bf16[256,2048]{1,0:T(8,128)(2,1)} %copy-done.27, bf16[256,2048]{1,0:T(8,128)(2,1)} %shard_map.100.refs_9_.refs_2_.refs_4_, ...), custom_call_target="tpu_custom_call" | custom-call | tf_op jit(solution)/shard_map/pallas_call | solution.py:34
  83.3 3.6 %collective-permute-start.16 = (bf16[512,512]{1,0:T(8,128)(2,1)}, bf16[512,512]{1,0:T(8,128)(2,1)S(1)}, u32[]{:S(2)}, u32[]{:S(2)}) collective-permute-start(bf16[512,512]{1,0:T(8,128)(2,1)} %get-tuple-element.50), channel_id=1, source_target_pairs={{0,8},{1,9},{2,10},{3,11},{4,12},{5,13},{6,14},{7,15},{8,0},{9,1},... | collective-permute-start | bytes 1572872 | tf_op jit(solution)/shard_map/ppermute | solution.py:387
  86.8 5.9 %all-to-all-start.2 = ((bf16[8,64,1792]{2,1,0:T(8,128)(2,1)}), bf16[8,64,1792]{2,1,0:T(8,128)(2,1)S(1)}, u32[]{:S(2)}, u32[]{:S(2)}) async-start(bf16[8,64,1792]{2,1,0:T(8,128)(2,1)} %shard_map.104.refs_10_), calls=%async_computation.2 | async-start | bytes 3670016 | tf_op jit(solution)/shard_map/all_to_all | solution.py:517
  93.7 6.3 %shard_map.105 = (bf16[512,1024]{1,0:T(8,128)(2,1)}, bf16[512,1792]{1,0:T(8,128)(2,1)}) custom-call(s32[4]{0:T(128)S(1)} %pad_add_fusion.refs_0_, bf16[64,1792]{1,0:T(8,128)(2,1)S(1)} %copy-done.12, bf16[64,1792]{1,0:T(8,128)(2,1)S(1)} %copy-done.26, bf16[64,1792]{1,0:T(8,128)(2,1)S(1)} %copy-done.22, bf16[64,1792]{1,0:T(8,128)(2,1)S(1)} %copy-done.24, ...), custom_call_target="tpu_custom_call" | custom-call | flops 49999998976 | tf_op jit(solution)/shard_map/pallas_call | solution.py:34
  100.1 8.5 %collective-permute-done.16.refs_0_ = bf16[512,512]{1,0:T(8,128)(2,1)S(1)} collective-permute-done((bf16[512,512]{1,0:T(8,128)(2,1)}, bf16[512,512]{1,0:T(8,128)(2,1)S(1)}, u32[]{:S(2)}, u32[]{:S(2)}) %collective-permute-start.16) | collective-permute-done | bytes 524320 | tf_op jit(solution)/shard_map/ppermute | solution.py:387
  111.4 11.1 %shard_map.107.refs_0_ = bf16[8,64,1792]{2,1,0:T(8,128)(2,1)} custom-call(bf16[512,1024]{1,0:T(8,128)(2,1)S(1)} %copy-done.7, bf16[512,1024]{1,0:T(8,128)(2,1)} %copy-done.28, bf16[256,2048]{1,0:T(8,128)(2,1)} %shard_map.99.refs_2_.refs_1_.refs_0_, bf16[256,2048]{1,0:T(8,128)(2,1)} %copy-done.27, bf16[256,2048]{1,0:T(8,128)(2,1)} %shard_map.100.refs_9_.refs_2_.refs_4_, ...), custom_call_target="tpu_custom_call" | custom-call | tf_op jit(solution)/shard_map/pallas_call | solution.py:34
  122.5 4.6 %all-to-all-start.3 = ((bf16[8,64,1792]{2,1,0:T(8,128)(2,1)}), bf16[8,64,1792]{2,1,0:T(8,128)(2,1)}, u32[]{:S(2)}, u32[]{:S(2)}) async-start(bf16[8,64,1792]{2,1,0:T(8,128)(2,1)} %shard_map.108.refs_3_), calls=%async_computation.3 | async-start | bytes 3670016 | tf_op jit(solution)/shard_map/all_to_all | solution.py:517
  128.6 2.9 %collective-permute-start.17 = (bf16[128,1792]{1,0:T(8,128)(2,1)}, bf16[128,1792]{1,0:T(8,128)(2,1)S(1)}, u32[]{:S(2)}, u32[]{:S(2)}) collective-permute-start(bf16[128,1792]{1,0:T(8,128)(2,1)} %shard_map.109), channel_id=1, source_target_pairs={{0,8},{1,9},{2,10},{3,11},{4,12},{5,13},{6,14},{7,15},{8,0},{9,1},... | collective-permute-start | bytes 1376264 | tf_op jit(solution)/shard_map/ppermute | solution.py:387
  131.5 2.0 %collective-permute-start.20 = (bf16[128,1792]{1,0:T(8,128)(2,1)}, bf16[128,1792]{1,0:T(8,128)(2,1)S(1)}, u32[]{:S(2)}, u32[]{:S(2)}) collective-permute-start(bf16[128,1792]{1,0:T(8,128)(2,1)} %get-tuple-element.60), channel_id=1, source_target_pairs={{0,1},{1,0},{2,3},{3,2},{4,5},{5,4},{6,7},{7,6},{8,9},{9,8},{10,11... | collective-permute-start | bytes 1376264 | tf_op jit(solution)/shard_map/ppermute | solution.py:523
  135.0 21.7 %collective-permute-done.17.refs_2_.refs_5_ = bf16[128,1792]{1,0:T(8,128)(2,1)S(1)} collective-permute-done((bf16[128,1792]{1,0:T(8,128)(2,1)}, bf16[128,1792]{1,0:T(8,128)(2,1)S(1)}, u32[]{:S(2)}, u32[]{:S(2)}) %collective-permute-start.17) | collective-permute-done | bytes 458784 | tf_op jit(solution)/shard_map/ppermute | solution.py:387
  156.7 2.2 %all-to-all-done.3.refs_0_.refs_1_ = bf16[8,64,1792]{2,1,0:T(8,128)(2,1)} async-done(((bf16[8,64,1792]{2,1,0:T(8,128)(2,1)}), bf16[8,64,1792]{2,1,0:T(8,128)(2,1)}, u32[]{:S(2)}, u32[]{:S(2)}) %all-to-all-start.3) | async-done | bytes 1835040 | tf_op jit(solution)/shard_map/all_to_all | solution.py:517
  158.9 2.2 %shard_map.110.refs_7_ = bf16[128,1792]{1,0:T(8,128)(2,1)} custom-call(bf16[8,64,1792]{2,1,0:T(8,128)(2,1)} %all-to-all-done.3.refs_0_.refs_1_, bf16[128,256]{1,0:T(8,128)(2,1)S(1)} %copy-done.20, bf16[128,1792]{1,0:T(8,128)(2,1)S(1)} %collective-permute-done.17.refs_2_.refs_5_), custom_call_target="tpu_custom_call" | custom-call | tf_op jit(solution)/shard_map/pallas_call | solution.py:34
  163.6 7.3 %collective-permute-done.21.refs_5_ = bf16[128,1792]{1,0:T(8,128)(2,1)S(1)} collective-permute-done((bf16[128,1792]{1,0:T(8,128)(2,1)}, bf16[128,1792]{1,0:T(8,128)(2,1)S(1)}, u32[]{:S(2)}, u32[]{:S(2)}) %collective-permute-start.21) | collective-permute-done | bytes 458784 | tf_op jit(solution)/shard_map/ppermute | solution.py:523
  171.0 7.5 %shard_map.111.refs_7_ = bf16[1,1024,1792]{2,1,0:T(8,128)(2,1)} custom-call(s32[3]{0:T(128)S(1)} %pad_add_fusion.1.where_ref, bf16[512,1024]{1,0:T(8,128)(2,1)} %get-tuple-element.57.hidden_ref, bf16[512,512]{1,0:T(8,128)(2,1)} %shard_map.106.refs_7_.refs_0_, bf16[512,512]{1,0:T(8,128)(2,1)} %collective-permute-done.19.refs_1_, ...), custom_call_target="tpu_custom_call" | custom-call | tf_op jit(solution)/shard_map/pallas_call | solution.py:366
  178.4 4.7 %collective-permute-done.18.refs_6_ = bf16[128,1792]{1,0:T(8,128)(2,1)S(1)} collective-permute-done((bf16[128,1792]{1,0:T(8,128)(2,1)}, bf16[128,1792]{1,0:T(8,128)(2,1)S(1)}, u32[]{:S(2)}, u32[]{:S(2)}) %collective-permute-start.18) | collective-permute-done | bytes 458784 | tf_op jit(solution)/shard_map/ppermute | solution.py:387
  183.2 2.7 %shard_map.112 = (bf16[128,1792]{1,0:T(8,128)(2,1)}, bf16[128,1792]{1,0:T(8,128)(2,1)}) custom-call(bf16[8,64,1792]{2,1,0:T(8,128)(2,1)} %copy-done, bf16[8,64,1792]{2,1,0:T(8,128)(2,1)} %all-to-all-done.3.refs_0_.refs_1_, bf16[128,256]{1,0:T(8,128)(2,1)S(1)} %copy-done.16, bf16[128,256]{1,0:T(8,128)(2,1)S(1)} %copy-done.17, ...), custom_call_target="tpu_custom_call" | custom-call | tf_op jit(solution)/shard_map/pallas_call | solution.py:34
  (106 shorter events, 23.4 us)
Async XLA Ops:
  0.6 27.1 %copy-start.6 = (bf16[128,1792]{1,0:T(8,128)(2,1)S(1)}, bf16[128,1792]{1,0:T(8,128)(2,1)}, u32[]{:S(2)}) copy-start(bf16[128,1792]{1,0:T(8,128)(2,1)} %refs_0_.1) | copy-start | bytes 1376260
  0.6 27.1 %collective-permute-start.3 = (bf16[128,1792]{1,0:T(8,128)(2,1)}, bf16[128,1792]{1,0:T(8,128)(2,1)S(1)}, u32[]{:S(2)}, u32[]{:S(2)}) collective-permute-start(bf16[128,1792]{1,0:T(8,128)(2,1)} %refs_0_.1), channel_id=1, source_target_pairs={{0,4},{1,5},{2,6},{3,7},{4,0},{5,1},{6,2},{7,3},{8,12},{9,13},{10,... | collective-permute-start | bytes 1376264 | tf_op jit(solution)/shard_map/ppermute | solution.py:514
  3.7 26.7 %collective-permute-start.1 = (bf16[128,1792]{1,0:T(8,128)(2,1)}, bf16[128,1792]{1,0:T(8,128)(2,1)S(1)}, u32[]{:S(2)}, u32[]{:S(2)}) collective-permute-start(bf16[128,1792]{1,0:T(8,128)(2,1)} %refs_2_.1), channel_id=1, source_target_pairs={{0,8},{1,9},{2,10},{3,11},{4,12},{5,13},{6,14},{7,15},{8,0},{9,1},... | collective-permute-start | bytes 1376264 | tf_op jit(solution)/shard_map/ppermute | solution.py:387
  7.7 20.0 %collective-permute-start.4 = (f32[4,128]{1,0:T(4,128)S(1)}, f32[4,128]{1,0:T(4,128)S(1)}, u32[]{:S(2)}, u32[]{:S(2)}) collective-permute-start(f32[4,128]{1,0:T(4,128)S(1)} %pad_maximum_fusion.refs_1_), channel_id=1, source_target_pairs={{0,12},{1,13},{2,14},{3,15},{4,8},{5,9},{6,10},{7,11},{8,4},{9,5},... | collective-permute-start | bytes 6152 | tf_op jit(solution)/shard_map/ppermute | solution.py:531
  7.7 20.0 %collective-permute-start.2 = (f32[4,128]{1,0:T(4,128)S(1)}, f32[4,128]{1,0:T(4,128)S(1)}, u32[]{:S(2)}, u32[]{:S(2)}) collective-permute-start(f32[4,128]{1,0:T(4,128)S(1)} %pad_maximum_fusion.refs_1_), channel_id=1, source_target_pairs={{0,4},{1,5},{2,6},{3,7},{4,0},{5,1},{6,2},{7,3},{8,12},{9,13},{10,... | collective-permute-start | bytes 6152 | tf_op jit(solution)/shard_map/ppermute | solution.py:514
  8.6 24.4 %collective-permute-start = (f32[4,128]{1,0:T(4,128)S(1)}, f32[4,128]{1,0:T(4,128)S(1)}, u32[]{:S(2)}, u32[]{:S(2)}) collective-permute-start(f32[4,128]{1,0:T(4,128)S(1)} %pad_maximum_fusion.refs_1_), channel_id=1, source_target_pairs={{0,8},{1,9},{2,10},{3,11},{4,12},{5,13},{6,14},{7,15},{8,0},{9,1},... | collective-permute-start | bytes 6152 | tf_op jit(solution)/shard_map/ppermute | solution.py:387
  14.5 13.2 %copy-start.2 = (bf16[8,32,1792]{2,1,0:T(8,128)(2,1)S(1)}, bf16[8,32,1792]{2,1,0:T(8,128)(2,1)}, u32[]{:S(2)}) copy-start(bf16[8,32,1792]{2,1,0:T(8,128)(2,1)} %get-tuple-element.34.refs_5_) | copy-start | bytes 2752516
  14.5 22.2 %all-to-all-start = ((bf16[8,32,1792]{2,1,0:T(8,128)(2,1)}), bf16[8,32,1792]{2,1,0:T(8,128)(2,1)S(1)}, u32[]{:S(2)}, u32[]{:S(2)}) async-start(bf16[8,32,1792]{2,1,0:T(8,128)(2,1)} %get-tuple-element.34.refs_5_), calls=%async_computation | async-start | bytes 1835008 | tf_op jit(solution)/shard_map/all_to_all | solution.py:517
  32.2 21.2 %collective-permute-start.7 = (bf16[128,1792]{1,0:T(8,128)(2,1)}, bf16[128,1792]{1,0:T(8,128)(2,1)}, u32[]{:S(2)}, u32[]{:S(2)}) collective-permute-start(bf16[128,1792]{1,0:T(8,128)(2,1)} %shard_map.96.refs_3_), channel_id=1, source_target_pairs={{0,8},{1,9},{2,10},{3,11},{4,12},{5,13},{6,14},{7,15},{8,0},{9,1},... | collective-permute-start | bytes 1376264 | tf_op jit(solution)/shard_map/ppermute | solution.py:387
  36.7 24.3 %all-to-all-start.1 = ((bf16[8,32,1792]{2,1,0:T(8,128)(2,1)}), bf16[8,32,1792]{2,1,0:T(8,128)(2,1)S(1)}, u32[]{:S(2)}, u32[]{:S(2)}) async-start(bf16[8,32,1792]{2,1,0:T(8,128)(2,1)} %shard_map.98.refs_2_), calls=%async_computation.1 | async-start | bytes 1835008 | tf_op jit(solution)/shard_map/all_to_all | solution.py:517
  53.4 13.9 %collective-permute-start.8 = (bf16[128,1792]{1,0:T(8,128)(2,1)}, bf16[128,1792]{1,0:T(8,128)(2,1)S(1)}, u32[]{:S(2)}, u32[]{:S(2)}) collective-permute-start(bf16[128,1792]{1,0:T(8,128)(2,1)} %shard_map.101.refs_3_), channel_id=1, source_target_pairs={{0,4},{1,5},{2,6},{3,7},{4,0},{5,1},{6,2},{7,3},{8,12},{9,13},{10,... | collective-permute-start | bytes 1376264 | tf_op jit(solution)/shard_map/ppermute | solution.py:514
  53.4 12.6 %collective-permute-start.10 = (bf16[64,1792]{1,0:T(8,128)(2,1)}, bf16[64,1792]{1,0:T(8,128)(2,1)S(1)}, u32[]{:S(2)}, u32[]{:S(2)}) collective-permute-start(bf16[64,1792]{1,0:T(8,128)(2,1)} %get-tuple-element.42), channel_id=1, source_target_pairs={{0,2},{1,3},{2,0},{3,1},{4,6},{5,7},{6,4},{7,5},{8,10},{9,11},{10,... | collective-permute-start | bytes 688136 | tf_op jit(solution)/shard_map/ppermute | solution.py:523
  55.0 11.2 %collective-permute-start.11 = (bf16[64,1792]{1,0:T(8,128)(2,1)}, bf16[64,1792]{1,0:T(8,128)(2,1)S(1)}, u32[]{:S(2)}, u32[]{:S(2)}) collective-permute-start(bf16[64,1792]{1,0:T(8,128)(2,1)} %get-tuple-element.43), channel_id=1, source_target_pairs={{0,3},{1,2},{2,1},{3,0},{4,7},{5,6},{6,5},{7,4},{8,11},{9,10},{10,... | collective-permute-start | bytes 688136 | tf_op jit(solution)/shard_map/ppermute | solution.py:523
  56.4 10.3 %collective-permute-start.9 = (bf16[64,1792]{1,0:T(8,128)(2,1)}, bf16[64,1792]{1,0:T(8,128)(2,1)S(1)}, u32[]{:S(2)}, u32[]{:S(2)}) collective-permute-start(bf16[64,1792]{1,0:T(8,128)(2,1)} %get-tuple-element.41), channel_id=1, source_target_pairs={{0,1},{1,0},{2,3},{3,2},{4,5},{5,4},{6,7},{7,6},{8,9},{9,8},{10,11... | collective-permute-start | bytes 688136 | tf_op jit(solution)/shard_map/ppermute | solution.py:523
  56.9 17.2 %collective-permute-start.5 = (bf16[256,2048]{1,0:T(8,128)(2,1)}, bf16[256,2048]{1,0:T(8,128)(2,1)S(1)}, u32[]{:S(2)}, u32[]{:S(2)}) collective-permute-start(bf16[256,2048]{1,0:T(8,128)(2,1)} %shard_map.99.refs_2_.refs_1_.refs_0_), channel_id=1, source_target_pairs={{0,16},{16,0},{1,17},{17,1},{2,18},{18,2},{3,19},{19,3},{4,20},{20... | collective-permute-start | bytes 3145736 | tf_op jit(solution)/shard_map/ppermute | solution.py:387
  66.1 8.1 %collective-permute-start.6 = (bf16[256,2048]{1,0:T(8,128)(2,1)}, bf16[256,2048]{1,0:T(8,128)(2,1)}, u32[]{:S(2)}, u32[]{:S(2)}) collective-permute-start(bf16[256,2048]{1,0:T(8,128)(2,1)} %shard_map.100.refs_9_.refs_2_.refs_4_), channel_id=1, source_target_pairs={{0,16},{16,0},{1,17},{17,1},{2,18},{18,2},{3,19},{19,3},{4,20},{20... | collective-permute-start | bytes 3145736 | tf_op jit(solution)/shard_map/ppermute | solution.py:387
  70.6 22.1 %collective-permute-start.12 = (bf16[64,1792]{1,0:T(8,128)(2,1)}, bf16[64,1792]{1,0:T(8,128)(2,1)}, u32[]{:S(2)}, u32[]{:S(2)}) collective-permute-start(bf16[64,1792]{1,0:T(8,128)(2,1)} %get-tuple-element.46), channel_id=1, source_target_pairs={{0,1},{1,0},{2,3},{3,2},{4,5},{5,4},{6,7},{7,6},{8,9},{9,8},{10,11... | collective-permute-start | bytes 688136 | tf_op jit(solution)/shard_map/ppermute | solution.py:523
  72.2 20.5 %collective-permute-start.13 = (bf16[64,1792]{1,0:T(8,128)(2,1)}, bf16[64,1792]{1,0:T(8,128)(2,1)}, u32[]{:S(2)}, u32[]{:S(2)}) collective-permute-start(bf16[64,1792]{1,0:T(8,128)(2,1)} %get-tuple-element.47), channel_id=1, source_target_pairs={{0,2},{1,3},{2,0},{3,1},{4,6},{5,7},{6,4},{7,5},{8,10},{9,11},{10,... | collective-permute-start | bytes 688136 | tf_op jit(solution)/shard_map/ppermute | solution.py:523
  74.1 18.6 %collective-permute-start.14 = (bf16[64,1792]{1,0:T(8,128)(2,1)}, bf16[64,1792]{1,0:T(8,128)(2,1)}, u32[]{:S(2)}, u32[]{:S(2)}) collective-permute-start(bf16[64,1792]{1,0:T(8,128)(2,1)} %get-tuple-element.48), channel_id=1, source_target_pairs={{0,3},{1,2},{2,1},{3,0},{4,7},{5,6},{6,5},{7,4},{8,11},{9,10},{10,... | collective-permute-start | bytes 688136 | tf_op jit(solution)/shard_map/ppermute | solution.py:523
  83.3 25.3 %collective-permute-start.16 = (bf16[512,512]{1,0:T(8,128)(2,1)}, bf16[512,512]{1,0:T(8,128)(2,1)S(1)}, u32[]{:S(2)}, u32[]{:S(2)}) collective-permute-start(bf16[512,512]{1,0:T(8,128)(2,1)} %get-tuple-element.50), channel_id=1, source_target_pairs={{0,8},{1,9},{2,10},{3,11},{4,12},{5,13},{6,14},{7,15},{8,0},{9,1},... | collective-permute-start | bytes 1572872 | tf_op jit(solution)/shard_map/ppermute | solution.py:387
  86.8 35.6 %all-to-all-start.2 = ((bf16[8,64,1792]{2,1,0:T(8,128)(2,1)}), bf16[8,64,1792]{2,1,0:T(8,128)(2,1)S(1)}, u32[]{:S(2)}, u32[]{:S(2)}) async-start(bf16[8,64,1792]{2,1,0:T(8,128)(2,1)} %shard_map.104.refs_10_), calls=%async_computation.2 | async-start | bytes 3670016 | tf_op jit(solution)/shard_map/all_to_all | solution.py:517
  100.0 9.3 %collective-permute-start.15 = (bf16[512,1024]{1,0:T(8,128)(2,1)}, bf16[512,1024]{1,0:T(8,128)(2,1)S(1)}, u32[]{:S(2)}, u32[]{:S(2)}) collective-permute-start(bf16[512,1024]{1,0:T(8,128)(2,1)} %get-tuple-element.49.refs_0_), channel_id=1, source_target_pairs={{0,16},{16,0},{1,17},{17,1},{2,18},{18,2},{3,19},{19,3},{4,20},{20... | collective-permute-start | bytes 3145736 | tf_op jit(solution)/shard_map/ppermute | solution.py:387
  122.5 36.4 %all-to-all-start.3 = ((bf16[8,64,1792]{2,1,0:T(8,128)(2,1)}), bf16[8,64,1792]{2,1,0:T(8,128)(2,1)}, u32[]{:S(2)}, u32[]{:S(2)}) async-start(bf16[8,64,1792]{2,1,0:T(8,128)(2,1)} %shard_map.108.refs_3_), calls=%async_computation.3 | async-start | bytes 3670016 | tf_op jit(solution)/shard_map/all_to_all | solution.py:517
  127.2 31.8 %copy-start.20 = (bf16[128,256]{1,0:T(8,128)(2,1)S(1)}, bf16[128,256]{1,0:T(8,128)(2,1)}, u32[]{:S(2)}) copy-start(bf16[128,256]{1,0:T(8,128)(2,1)} %get-tuple-element.56.refs_1_) | copy-start | bytes 196612
  128.6 33.6 %copy-start.29 = (s32[4]{0:T(128)S(1)}, s32[4]{0:T(128)}, u32[]{:S(2)}) copy-start(s32[4]{0:T(128)} %param.13) | copy-start | bytes 52
  128.6 42.3 %copy-start.10 = (bf16[128,1792]{1,0:T(8,128)(2,1)S(1)}, bf16[128,1792]{1,0:T(8,128)(2,1)}, u32[]{:S(2)}) copy-start(bf16[128,1792]{1,0:T(8,128)(2,1)} %get-tuple-element.59.refs_3_) | copy-start | bytes 1376260
  128.6 28.1 %collective-permute-start.17 = (bf16[128,1792]{1,0:T(8,128)(2,1)}, bf16[128,1792]{1,0:T(8,128)(2,1)S(1)}, u32[]{:S(2)}, u32[]{:S(2)}) collective-permute-start(bf16[128,1792]{1,0:T(8,128)(2,1)} %shard_map.109), channel_id=1, source_target_pairs={{0,8},{1,9},{2,10},{3,11},{4,12},{5,13},{6,14},{7,15},{8,0},{9,1},... | collective-permute-start | bytes 1376264 | tf_op jit(solution)/shard_map/ppermute | solution.py:387
  131.5 39.5 %collective-permute-start.19 = (bf16[512,512]{1,0:T(8,128)(2,1)S(1)}, bf16[512,512]{1,0:T(8,128)(2,1)}, u32[]{:S(2)}, u32[]{:S(2)}) collective-permute-start(bf16[512,512]{1,0:T(8,128)(2,1)S(1)} %copy-done.5), channel_id=1, source_target_pairs={{0,16},{16,0},{1,17},{17,1},{2,18},{18,2},{3,19},{19,3},{4,20},{20... | collective-permute-start | bytes 1572872 | tf_op jit(solution)/shard_map/ppermute | solution.py:387
  131.5 32.1 %collective-permute-start.20 = (bf16[128,1792]{1,0:T(8,128)(2,1)}, bf16[128,1792]{1,0:T(8,128)(2,1)S(1)}, u32[]{:S(2)}, u32[]{:S(2)}) collective-permute-start(bf16[128,1792]{1,0:T(8,128)(2,1)} %get-tuple-element.60), channel_id=1, source_target_pairs={{0,1},{1,0},{2,3},{3,2},{4,5},{5,4},{6,7},{7,6},{8,9},{9,8},{10,11... | collective-permute-start | bytes 1376264 | tf_op jit(solution)/shard_map/ppermute | solution.py:523
  133.5 37.4 %collective-permute-start.21 = (bf16[128,1792]{1,0:T(8,128)(2,1)}, bf16[128,1792]{1,0:T(8,128)(2,1)S(1)}, u32[]{:S(2)}, u32[]{:S(2)}) collective-permute-start(bf16[128,1792]{1,0:T(8,128)(2,1)} %get-tuple-element.61), channel_id=1, source_target_pairs={{0,2},{1,3},{2,0},{3,1},{4,6},{5,7},{6,4},{7,5},{8,10},{9,11},{10,... | collective-permute-start | bytes 1376264 | tf_op jit(solution)/shard_map/ppermute | solution.py:523
  134.9 36.0 %collective-permute-start.22 = (bf16[128,1792]{1,0:T(8,128)(2,1)}, bf16[128,1792]{1,0:T(8,128)(2,1)S(1)}, u32[]{:S(2)}, u32[]{:S(2)}) collective-permute-start(bf16[128,1792]{1,0:T(8,128)(2,1)} %get-tuple-element.62), channel_id=1, source_target_pairs={{0,3},{1,2},{2,1},{3,0},{4,7},{5,6},{6,5},{7,4},{8,11},{9,10},{10,... | collective-permute-start | bytes 1376264 | tf_op jit(solution)/shard_map/ppermute | solution.py:523
  161.1 22.0 %collective-permute-start.18 = (bf16[128,1792]{1,0:T(8,128)(2,1)}, bf16[128,1792]{1,0:T(8,128)(2,1)S(1)}, u32[]{:S(2)}, u32[]{:S(2)}) collective-permute-start(bf16[128,1792]{1,0:T(8,128)(2,1)} %shard_map.110.refs_7_), channel_id=1, source_target_pairs={{0,8},{1,9},{2,10},{3,11},{4,12},{5,13},{6,14},{7,15},{8,0},{9,1},... | collective-permute-start | bytes 1376264 | tf_op jit(solution)/shard_map/ppermute | solution.py:387
  (25 other events, 114.3 us)

commit v4 on v3

--- a/solution.py
+++ b/solution.py
@@ -8,6 +8,7 @@
 BF16 = jnp.bfloat16
 F32 = jnp.float32
 LONG = 50_000_000_000
+PARTS = 4
 ANYWHERE = pl.BlockSpec(memory_space=pl.ANY)
 IN_VMEM = pl.BlockSpec(memory_space=pltpu.VMEM)
 
@@ -188,11 +189,13 @@
     width = near[0].shape[1]
     inner = weight.shape[1]
     rows = 2 * peers * slots
+    step = 2 * rows // PARTS
     tile = tile_of(inner)
 
     def body(scalar_ref, *refs):
         near_refs, far_refs = refs[:peers], refs[peers : 2 * peers]
-        w_ref, out, x, *scratch = refs[2 * peers :]
+        w_ref, *outs, x = refs[2 * peers : 2 * peers + PARTS + 2]
+        scratch = refs[2 * peers + PARTS + 2 :]
         piece = piece_of(w_ref, *scratch, 1)
 
         @pl.when(pl.program_id(0) == 0)
@@ -203,19 +206,18 @@
         got = lax.dot_general(
             x[...], piece(), (((1,), (1,)), ((), ())), preferred_element_type=F32
         )
-        out[...] = got.astype(BF16)
+        for p, out in enumerate(outs):
+            out[...] = got[p * step : (p + 1) * step].astype(BF16)
 
     return run(
         body,
-        [
-            jax.ShapeDtypeStruct((2 * rows, inner), BF16),
-            jax.ShapeDtypeStruct((2 * rows, width), BF16),
-        ],
+        [jax.ShapeDtypeStruct((step, inner), BF16)] * PARTS
+        + [jax.ShapeDtypeStruct((2 * rows, width), BF16)],
         (inner // tile,),
         [pl.BlockSpec(memory_space=pltpu.SMEM)]
         + [fixed((2 * slots, width))] * (2 * peers)
         + [ANYWHERE],
-        [pl.BlockSpec((2 * rows, tile), lambda c: (0, c)), fixed((2 * rows, width))],
+        [pl.BlockSpec((step, tile), lambda c: (0, c))] * PARTS + [fixed((2 * rows, width))],
         [scalars, *near, *far, weight],
         streamed(weight.shape, tile, 1),
         deps,
@@ -226,27 +228,30 @@
 def rows_dx(grad_parts, near, far, weight, peers, deps=()):
     n = len(near)
     rows = near[0].shape[0]
-    inner = grad_parts[0].shape[1]
+    inner = grad_parts[0][0].shape[1]
+    step = 2 * rows // PARTS
     width = weight.shape[1]
     slots = rows // peers
     tile = tile_of(width)
     blocks = pl.BlockSpec((peers, 2 * slots, tile), lambda c: (0, 0, c))
 
     def body(*refs):
-        grad_refs, near_refs, far_refs = refs[:n], refs[n : 2 * n], refs[2 * n : 3 * n]
-        w_ref, out, both, *scratch = refs[3 * n :]
+        grad_refs, refs = refs[: PARTS * n], refs[PARTS * n :]
+        near_refs, far_refs = refs[:n], refs[n : 2 * n]
+        w_ref, out, both, *scratch = refs[2 * n :]
         piece = piece_of(w_ref, *scratch, 1)
 
         @pl.when(pl.program_id(0) == 0)
         def _():
-            for at, part_refs in ((0, near_refs), (rows, far_refs)):
-                hidden_grad = total([g.at[at : at + rows, :] for g in grad_refs])
-                gate_up = total(part_refs)
+            for p in range(PARTS):
+                hidden_grad = total(grad_refs[p * n : (p + 1) * n])
+                part_refs, at = (near_refs, p * step) if p * step < rows else (far_refs, p * step - rows)
+                gate_up = total([ref.at[at : at + step, :] for ref in part_refs])
                 gate, up = gate_up[:, :inner], gate_up[:, inner:]
                 sig = jax.nn.sigmoid(gate)
                 gate_grad = hidden_grad * up * sig * (1.0 + gate * (1.0 - sig))
-                both[at : at + rows, :inner] = gate_grad.astype(BF16)
-                both[at : at + rows, inner:] = (hidden_grad * (gate * sig)).astype(BF16)
+                both[p * step : (p + 1) * step, :inner] = gate_grad.astype(BF16)
+                both[p * step : (p + 1) * step, inner:] = (hidden_grad * (gate * sig)).astype(BF16)
 
         got = lax.dot_general(
             both[...],
@@ -261,9 +266,9 @@
         body,
         jax.ShapeDtypeStruct((peers, 2 * slots, width), BF16),
         (width // tile,),
-        [fixed(p.shape) for p in (*grad_parts, *near, *far)] + [ANYWHERE],
+        [fixed(p.shape) for p in (*sum(grad_parts, []), *near, *far)] + [ANYWHERE],
         blocks,
-        [*grad_parts, *near, *far, weight],
+        [*sum(grad_parts, []), *near, *far, weight],
         [pltpu.VMEM((2 * rows, 2 * inner), BF16)] + streamed(weight.shape, tile, 1),
         deps,
     )
@@ -576,13 +581,12 @@
     send_4 = tied(send_4, second)
     fourth = exchange(send_4)
 
-    grad_part, grads = hidden_grad_part(
+    *grad_part, grads = hidden_grad_part(
         scalars, grads_near, grads_far, slots, down_weight, deps=(send_4,), flops=LONG
     )
-    grad_parts = over_dp(grad_part)
-    far_share = tied(far_share, flops=LONG)
-    send_5 = rows_dx(grad_parts, parts_n, parts_f, gate_up_weight, half, deps=(far_share,))
-    send_5 = tied(send_5, fourth)
+    grad_parts = [over_dp(part) for part in grad_part]
+    send_5 = rows_dx(grad_parts, parts_n, parts_f, gate_up_weight, half)
+    send_5 = tied(send_5, fourth, far_share)
     fifth = exchange(send_5)
     far_shares = [far_share] + [crossed(far_share, "dp", d) for d in range(1, n_dp)]
     give_out = give(fourth, 0, slots, back_wt_f, deps=(send_5,))

time: 187 us -> 184 us (0.984)
  waiting for transfers between devices: 68 us -> 60.4 us
  local copies, waits for them, and re-layouts: 8.72 us -> 10.7 us
  starting transfers between devices: 47.2 us -> 49.1 us
    ppermute x10 -> x13, waiting for transfers between devices: 42.7 us -> 35.4 us  [crossed(): lax.ppermute(block, axis, [(i, (i + distance) % size) for i in range(size)])]
    unnamed x60, local copies, waits for them, and re-layouts: 8.72 us -> 10.7 us
    pallas_call x18 -> x17, Pallas kernels: 50.7 us -> 51.1 us  [run(): pl.pallas_call(whole, out_shape=out_shape, grid=grid, in_specs=list(in_sp...]
    ppermute x10 -> x13, starting transfers between devices: 14.4 us -> 14.7 us  [crossed(): lax.ppermute(block, axis, [(i, (i + distance) % size) for i in range(size)])]
  transfers between devices with their start and end apart: 27 -> 30, of which waited for: 11 -> 15; matrix products, arithmetic and copies ran while one was open for 1% -> 1% of each run, Pallas kernels for 30% -> 31%
where the time goes in v4:
time: 184 us; the launch traced here: 183 us
  waiting for transfers between devices  60.4 us (33%)
  Pallas kernels  58.6 us (32%)
  starting transfers between devices  49.1 us (27%)
  local copies, waits for them, and re-layouts  10.7 us (6%)
  other arithmetic  2.15 us (1%)
    pallas_call x17, Pallas kernels, run(): pl.pallas_call(whole, out_shape=out_shape, grid=grid, in_specs=list(in_sp...  51.1 us
    ppermute x13, waiting for transfers between devices, crossed(): lax.ppermute(block, axis, [(i, (i + distance) % size) for i in range(size)])  35.4 us
    all_to_all x4, starting transfers between devices, exchange(): lax.all_to_all(x, 'expert', split_axis=0, concat_axis=0, tiled=True, axis...  19.9 us
    ppermute x13, starting transfers between devices, crossed(): lax.ppermute(block, axis, [(i, (i + distance) % size) for i in range(size)])  14.7 us
    unnamed x60, local copies, waits for them, and re-layouts  10.7 us
    ppermute x9, starting transfers between devices, over_plane(): lax.ppermute(pieces[d], 'expert', [(i, i ^ d) for i in range(experts)])  10.5 us
    ppermute x1, waiting for transfers between devices, on_device(): lax.ppermute(table, 'expert', [(i, i ^ plane ^ half) for i in range(exper...  9.25 us
    all_to_all x4, waiting for transfers between devices, exchange(): lax.all_to_all(x, 'expert', split_axis=0, concat_axis=0, tiled=True, axis...  7.93 us
  transfers between devices with their start and end apart: 30, of which 15 were waited for; matrix products, arithmetic and copies ran while one was open for 1% of the time, Pallas kernels for 31%

profile of v4, /device:TPU:0, one launch (start us, length us, event | category | flops | bytes accessed | tf_op | source)
XLA Modules:
  0.0 182.6 jit_solution(16445676020586738748)
XLA Ops:
  0.6 3.1 %collective-permute-start.3 = (bf16[128,1792]{1,0:T(8,128)(2,1)}, bf16[128,1792]{1,0:T(8,128)(2,1)S(1)}, u32[]{:S(2)}, u32[]{:S(2)}) collective-permute-start(bf16[128,1792]{1,0:T(8,128)(2,1)} %refs_0_.1), channel_id=1, source_target_pairs={{0,4},{1,5},{2,6},{3,7},{4,0},{5,1},{6,2},{7,3},{8,12},{9,13},{10,... | collective-permute-start | bytes 1376264 | tf_op jit(solution)/shard_map/ppermute | solution.py:519
  3.7 2.6 %collective-permute-start.1 = (bf16[128,1792]{1,0:T(8,128)(2,1)}, bf16[128,1792]{1,0:T(8,128)(2,1)S(1)}, u32[]{:S(2)}, u32[]{:S(2)}) collective-permute-start(bf16[128,1792]{1,0:T(8,128)(2,1)} %refs_2_.1), channel_id=1, source_target_pairs={{0,8},{1,9},{2,10},{3,11},{4,12},{5,13},{6,14},{7,15},{8,0},{9,1},... | collective-permute-start | bytes 1376264 | tf_op jit(solution)/shard_map/ppermute | solution.py:392
  8.6 3.5 %collective-permute-start = (f32[4,128]{1,0:T(4,128)S(1)}, f32[4,128]{1,0:T(4,128)S(1)}, u32[]{:S(2)}, u32[]{:S(2)}) collective-permute-start(f32[4,128]{1,0:T(4,128)S(1)} %pad_maximum_fusion.refs_1_), channel_id=1, source_target_pairs={{0,8},{1,9},{2,10},{3,11},{4,12},{5,13},{6,14},{7,15},{8,0},{9,1},... | collective-permute-start | bytes 6152 | tf_op jit(solution)/shard_map/ppermute | solution.py:392
  13.1 1.4 shard_map.94
  14.5 3.9 %all-to-all-start = ((bf16[8,32,1792]{2,1,0:T(8,128)(2,1)}), bf16[8,32,1792]{2,1,0:T(8,128)(2,1)S(1)}, u32[]{:S(2)}, u32[]{:S(2)}) async-start(bf16[8,32,1792]{2,1,0:T(8,128)(2,1)} %get-tuple-element.37.refs_5_), calls=%async_computation | async-start | bytes 1835008 | tf_op jit(solution)/shard_map/all_to_all | solution.py:522
  18.5 9.2 %collective-permute-done.4.refs_6_.refs_2_ = f32[4,128]{1,0:T(4,128)S(1)} collective-permute-done((f32[4,128]{1,0:T(4,128)S(1)}, f32[4,128]{1,0:T(4,128)S(1)}, u32[]{:S(2)}, u32[]{:S(2)}) %collective-permute-start.4) | collective-permute-done | bytes 2080 | tf_op jit(solution)/shard_map/ppermute | solution.py:536
  27.7 2.7 %shard_map.95 = (bf16[64,1792]{1,0:T(8,128)(2,1)}, bf16[64,1792]{1,0:T(8,128)(2,1)}, bf16[64,1792]{1,0:T(8,128)(2,1)}, bf16[64,1792]{1,0:T(8,128)(2,1)}, bf16[12...) custom-call(s32[4]{0:T(128)S(1)} %pad_add_fusion.refs_0_, ...), custom_call_target="tpu_custom_call" | custom-call | tf_op jit(solution)/shard_map/pallas_call | solution.py:35
  34.0 1.5 shard_map.97
  36.7 3.8 %all-to-all-start.1 = ((bf16[8,32,1792]{2,1,0:T(8,128)(2,1)}), bf16[8,32,1792]{2,1,0:T(8,128)(2,1)S(1)}, u32[]{:S(2)}, u32[]{:S(2)}) async-start(bf16[8,32,1792]{2,1,0:T(8,128)(2,1)} %shard_map.98.refs_2_), calls=%async_computation.1 | async-start | bytes 1835008 | tf_op jit(solution)/shard_map/all_to_all | solution.py:522
  40.5 5.1 %shard_map.99.refs_2_.refs_1_.refs_0_.refs_8_ = bf16[256,2048]{1,0:T(8,128)(2,1)} custom-call(bf16[8,32,1792]{2,1,0:T(8,128)(2,1)S(1)} %all-to-all-done.refs_1_.refs_0_, bf16[1,1792,2048]{2,1,0:T(8,128)(2,1)} %refs_12_.1, bf16[8,32,1792]{2,1,0:T(8,128)(2,1)S(1)} %copy-done.2), custom_call_target="tpu_custom_call" | custom-call | tf_op jit(solution)/shard_map/pallas_call | solution.py:35
  45.6 7.8 %collective-permute-done.7.refs_0_ = bf16[128,1792]{1,0:T(8,128)(2,1)} collective-permute-done((bf16[128,1792]{1,0:T(8,128)(2,1)}, bf16[128,1792]{1,0:T(8,128)(2,1)}, u32[]{:S(2)}, u32[]{:S(2)}) %collective-permute-start.7) | collective-permute-done | bytes 458784 | tf_op jit(solution)/shard_map/ppermute | solution.py:392
  53.5 1.5 collective-permute-start.10
  57.0 4.1 %all-to-all-done.1.refs_0_.refs_1_ = bf16[8,32,1792]{2,1,0:T(8,128)(2,1)S(1)} async-done(((bf16[8,32,1792]{2,1,0:T(8,128)(2,1)}), bf16[8,32,1792]{2,1,0:T(8,128)(2,1)S(1)}, u32[]{:S(2)}, u32[]{:S(2)}) %all-to-all-start.1) | async-done | bytes 917536 | tf_op jit(solution)/shard_map/all_to_all | solution.py:522
  61.0 5.1 %shard_map.100.refs_9_.refs_2_.refs_10_ = bf16[256,2048]{1,0:T(8,128)(2,1)} custom-call(bf16[8,32,1792]{2,1,0:T(8,128)(2,1)S(1)} %all-to-all-done.1.refs_0_.refs_1_, bf16[1,1792,2048]{2,1,0:T(8,128)(2,1)} %refs_12_.1, bf16[256,2048]{1,0:T(8,128)(2,1)} %shard_map.99.refs_2_.refs_1_.refs_0_.refs_8_), custom_call_target="tpu_custom_call" | custom-call | tf_op jit(solution)/shard_map/pallas_call | solution.py:35
  67.4 3.2 %shard_map.102 = (bf16[64,1792]{1,0:T(8,128)(2,1)}, bf16[64,1792]{1,0:T(8,128)(2,1)}, bf16[64,1792]{1,0:T(8,128)(2,1)}, bf16[64,1792]{1,0:T(8,128)(2,1)}, bf16[1...) custom-call(s32[4]{0:T(128)S(1)} %pad_add_fusion.refs_0_, ...), custom_call_target="tpu_custom_call", output_to_operand_aliasing={{4}: (5, {}), {5}: (6, {}), {6}: (7, {}), {7}: (8, {})} | custom-call | flops 49999998976 | tf_op jit(solution)/shard_map/pallas_call | solution.py:35
  70.6 1.6 collective-permute-start.12
  72.1 1.9 %collective-permute-start.13 = (bf16[64,1792]{1,0:T(8,128)(2,1)}, bf16[64,1792]{1,0:T(8,128)(2,1)}, u32[]{:S(2)}, u32[]{:S(2)}) collective-permute-start(bf16[64,1792]{1,0:T(8,128)(2,1)} %get-tuple-element.50), channel_id=1, source_target_pairs={{0,2},{1,3},{2,0},{3,1},{4,6},{5,7},{6,4},{7,5},{8,10},{9,11},{10,... | collective-permute-start | bytes 688136 | tf_op jit(solution)/shard_map/ppermute | solution.py:528
  75.0 7.2 %shard_map.103 = (bf16[512,1024]{1,0:T(8,128)(2,1)}, bf16[512,512]{1,0:T(8,128)(2,1)}, bf16[8,64,1792]{2,1,0:T(8,128)(2,1)}) custom-call(bf16[256,2048]{1,0:T(8,128)(2,1)} %shard_map.99.refs_2_.refs_1_.refs_0_.refs_8_, bf16[256,2048]{1,0:T(8,128)(2,1)} %collective-permute-done.5.refs_1_.refs_9_, bf16[256,2048]{1,0:T(8,128)(2,1)} %shard_map.100.refs_9_.refs_2_.refs_10_, ...), custom_call_target="tpu_custom_call" | custom-call | tf_op jit(solution)/shard_map/pallas_call | solution.py:35
  82.3 4.3 %all-to-all-start.2 = ((bf16[8,64,1792]{2,1,0:T(8,128)(2,1)}), bf16[8,64,1792]{2,1,0:T(8,128)(2,1)S(1)}, u32[]{:S(2)}, u32[]{:S(2)}) async-start(bf16[8,64,1792]{2,1,0:T(8,128)(2,1)} %shard_map.104.refs_10_), calls=%async_computation.2 | async-start | bytes 3670016 | tf_op jit(solution)/shard_map/all_to_all | solution.py:522
  86.6 5.1 %collective-permute-start.19 = (bf16[512,512]{1,0:T(8,128)(2,1)}, bf16[512,512]{1,0:T(8,128)(2,1)S(1)}, u32[]{:S(2)}, u32[]{:S(2)}) collective-permute-start(bf16[512,512]{1,0:T(8,128)(2,1)} %get-tuple-element.56), channel_id=1, source_target_pairs={{0,8},{1,9},{2,10},{3,11},{4,12},{5,13},{6,14},{7,15},{8,0},{9,1},... | collective-permute-start | bytes 1572872 | tf_op jit(solution)/shard_map/ppermute | solution.py:392
  92.6 6.8 %shard_map.105 = (bf16[128,1024]{1,0:T(8,128)(2,1)}, bf16[128,1024]{1,0:T(8,128)(2,1)}, bf16[128,1024]{1,0:T(8,128)(2,1)}, bf16[128,1024]{1,0:T(8,128)(2,1)}, bf16[512,1792]{1,0:T(8,128)(2,1)}) custom-call(s32[4]{0:T(128)S(1)} %pad_add_fusion.refs_0_, bf16[64,1792]{1,0:T(8,128)(2,1)S(1)} %copy-done.14, bf16[64,1792]{1,0:T(8,128)(2,1)S(1)} %copy-done.24, ...), custom_call_target="tpu_custom_call" | custom-call | flops 49999998976 | tf_op jit(solution)/shard_map/pallas_call | solution.py:35
  106.9 10.8 %shard_map.106.refs_0_ = bf16[8,64,1792]{2,1,0:T(8,128)(2,1)} custom-call(bf16[128,1024]{1,0:T(8,128)(2,1)S(1)} %copy-done.9, bf16[128,1024]{1,0:T(8,128)(2,1)S(1)} %collective-permute-done.15.refs_1_, bf16[128,1024]{1,0:T(8,128)(2,1)S(1)} %copy-done.10, bf16[128,1024]{1,0:T(8,128)(2,1)S(1)} %collective-permute-done.16.refs_3_, ...), custom_call_target="tpu_custom_call" | custom-call | tf_op jit(solution)/shard_map/pallas_call | solution.py:35
  119.6 8.0 %all-to-all-start.3 = ((bf16[8,64,1792]{2,1,0:T(8,128)(2,1)}), bf16[8,64,1792]{2,1,0:T(8,128)(2,1)}, u32[]{:S(2)}, u32[]{:S(2)}) async-start(bf16[8,64,1792]{2,1,0:T(8,128)(2,1)} %shard_map.107.refs_3_), calls=%async_computation.3 | async-start | bytes 3670016 | tf_op jit(solution)/shard_map/all_to_all | solution.py:522
  129.6 2.0 %collective-permute-start.23 = (bf16[128,1792]{1,0:T(8,128)(2,1)}, bf16[128,1792]{1,0:T(8,128)(2,1)S(1)}, u32[]{:S(2)}, u32[]{:S(2)}) collective-permute-start(bf16[128,1792]{1,0:T(8,128)(2,1)} %get-tuple-element.66), channel_id=1, source_target_pairs={{0,1},{1,0},{2,3},{3,2},{4,5},{5,4},{6,7},{7,6},{8,9},{9,8},{10,11... | collective-permute-start | bytes 1376264 | tf_op jit(solution)/shard_map/ppermute | solution.py:528
  131.6 1.5 collective-permute-start.24
  133.1 21.5 %collective-permute-done.20.refs_2_.refs_5_ = bf16[128,1792]{1,0:T(8,128)(2,1)S(1)} collective-permute-done((bf16[128,1792]{1,0:T(8,128)(2,1)}, bf16[128,1792]{1,0:T(8,128)(2,1)S(1)}, u32[]{:S(2)}, u32[]{:S(2)}) %collective-permute-start.20) | collective-permute-done | bytes 458784 | tf_op jit(solution)/shard_map/ppermute | solution.py:392
  154.6 2.1 %all-to-all-done.3.refs_0_.refs_1_ = bf16[8,64,1792]{2,1,0:T(8,128)(2,1)} async-done(((bf16[8,64,1792]{2,1,0:T(8,128)(2,1)}), bf16[8,64,1792]{2,1,0:T(8,128)(2,1)}, u32[]{:S(2)}, u32[]{:S(2)}) %all-to-all-start.3) | async-done | bytes 1835040 | tf_op jit(solution)/shard_map/all_to_all | solution.py:522
  156.7 2.2 %shard_map.109.refs_7_ = bf16[128,1792]{1,0:T(8,128)(2,1)} custom-call(bf16[8,64,1792]{2,1,0:T(8,128)(2,1)} %all-to-all-done.3.refs_0_.refs_1_, bf16[128,256]{1,0:T(8,128)(2,1)S(1)} %copy-done.22, bf16[128,1792]{1,0:T(8,128)(2,1)S(1)} %collective-permute-done.20.refs_2_.refs_5_), custom_call_target="tpu_custom_call" | custom-call | tf_op jit(solution)/shard_map/pallas_call | solution.py:35
  161.5 6.7 %collective-permute-done.24.refs_5_ = bf16[128,1792]{1,0:T(8,128)(2,1)S(1)} collective-permute-done((bf16[128,1792]{1,0:T(8,128)(2,1)}, bf16[128,1792]{1,0:T(8,128)(2,1)S(1)}, u32[]{:S(2)}, u32[]{:S(2)}) %collective-permute-start.24) | collective-permute-done | bytes 458784 | tf_op jit(solution)/shard_map/ppermute | solution.py:528
  168.2 7.5 %shard_map.110.refs_7_ = bf16[1,1024,1792]{2,1,0:T(8,128)(2,1)} custom-call(s32[3]{0:T(128)S(1)} %pad_add_fusion.1.where_ref, bf16[512,1024]{1,0:T(8,128)(2,1)} %get-tuple-element.63.hidden_ref, bf16[512,512]{1,0:T(8,128)(2,1)} %copy-done.4, bf16[512,512]{1,0:T(8,128)(2,1)} %collective-permute-done.22.refs_1_, bf16[512,1792]{1,0:T(8,128)(2,1)} %get-tuple-element.64.refs_2_, ...), custom_call_target="tpu_custom_call" | custom-call | tf_op jit(solution)/shard_map/pallas_call | solution.py:371
  175.6 4.2 %collective-permute-done.21.refs_6_ = bf16[128,1792]{1,0:T(8,128)(2,1)S(1)} collective-permute-done((bf16[128,1792]{1,0:T(8,128)(2,1)}, bf16[128,1792]{1,0:T(8,128)(2,1)S(1)}, u32[]{:S(2)}, u32[]{:S(2)}) %collective-permute-start.21) | collective-permute-done | bytes 458784 | tf_op jit(solution)/shard_map/ppermute | solution.py:392
  179.9 2.7 %shard_map.111 = (bf16[128,1792]{1,0:T(8,128)(2,1)}, bf16[128,1792]{1,0:T(8,128)(2,1)}) custom-call(bf16[8,64,1792]{2,1,0:T(8,128)(2,1)} %copy-done, bf16[8,64,1792]{2,1,0:T(8,128)(2,1)} %all-to-all-done.3.refs_0_.refs_1_, bf16[128,256]{1,0:T(8,128)(2,1)S(1)} %copy-done.18, bf16[128,256]{1,0:T(8,128)(2,1)S(1)} %copy-done.19, ...), custom_call_target="tpu_custom_call" | custom-call | tf_op jit(solution)/shard_map/pallas_call | solution.py:35
  (111 shorter events, 26.6 us)
Async XLA Ops:
  0.6 27.1 %collective-permute-start.3 = (bf16[128,1792]{1,0:T(8,128)(2,1)}, bf16[128,1792]{1,0:T(8,128)(2,1)S(1)}, u32[]{:S(2)}, u32[]{:S(2)}) collective-permute-start(bf16[128,1792]{1,0:T(8,128)(2,1)} %refs_0_.1), channel_id=1, source_target_pairs={{0,4},{1,5},{2,6},{3,7},{4,0},{5,1},{6,2},{7,3},{8,12},{9,13},{10,... | collective-permute-start | bytes 1376264 | tf_op jit(solution)/shard_map/ppermute | solution.py:519
  3.7 26.7 %collective-permute-start.1 = (bf16[128,1792]{1,0:T(8,128)(2,1)}, bf16[128,1792]{1,0:T(8,128)(2,1)S(1)}, u32[]{:S(2)}, u32[]{:S(2)}) collective-permute-start(bf16[128,1792]{1,0:T(8,128)(2,1)} %refs_2_.1), channel_id=1, source_target_pairs={{0,8},{1,9},{2,10},{3,11},{4,12},{5,13},{6,14},{7,15},{8,0},{9,1},... | collective-permute-start | bytes 1376264 | tf_op jit(solution)/shard_map/ppermute | solution.py:392
  7.7 20.0 %collective-permute-start.4 = (f32[4,128]{1,0:T(4,128)S(1)}, f32[4,128]{1,0:T(4,128)S(1)}, u32[]{:S(2)}, u32[]{:S(2)}) collective-permute-start(f32[4,128]{1,0:T(4,128)S(1)} %pad_maximum_fusion.refs_1_), channel_id=1, source_target_pairs={{0,12},{1,13},{2,14},{3,15},{4,8},{5,9},{6,10},{7,11},{8,4},{9,5},... | collective-permute-start | bytes 6152 | tf_op jit(solution)/shard_map/ppermute | solution.py:536
  7.7 20.0 %collective-permute-start.2 = (f32[4,128]{1,0:T(4,128)S(1)}, f32[4,128]{1,0:T(4,128)S(1)}, u32[]{:S(2)}, u32[]{:S(2)}) collective-permute-start(f32[4,128]{1,0:T(4,128)S(1)} %pad_maximum_fusion.refs_1_), channel_id=1, source_target_pairs={{0,4},{1,5},{2,6},{3,7},{4,0},{5,1},{6,2},{7,3},{8,12},{9,13},{10,... | collective-permute-start | bytes 6152 | tf_op jit(solution)/shard_map/ppermute | solution.py:519
  8.6 24.4 %collective-permute-start = (f32[4,128]{1,0:T(4,128)S(1)}, f32[4,128]{1,0:T(4,128)S(1)}, u32[]{:S(2)}, u32[]{:S(2)}) collective-permute-start(f32[4,128]{1,0:T(4,128)S(1)} %pad_maximum_fusion.refs_1_), channel_id=1, source_target_pairs={{0,8},{1,9},{2,10},{3,11},{4,12},{5,13},{6,14},{7,15},{8,0},{9,1},... | collective-permute-start | bytes 6152 | tf_op jit(solution)/shard_map/ppermute | solution.py:392
  14.5 22.1 %all-to-all-start = ((bf16[8,32,1792]{2,1,0:T(8,128)(2,1)}), bf16[8,32,1792]{2,1,0:T(8,128)(2,1)S(1)}, u32[]{:S(2)}, u32[]{:S(2)}) async-start(bf16[8,32,1792]{2,1,0:T(8,128)(2,1)} %get-tuple-element.37.refs_5_), calls=%async_computation | async-start | bytes 1835008 | tf_op jit(solution)/shard_map/all_to_all | solution.py:522
  32.2 21.2 %collective-permute-start.7 = (bf16[128,1792]{1,0:T(8,128)(2,1)}, bf16[128,1792]{1,0:T(8,128)(2,1)}, u32[]{:S(2)}, u32[]{:S(2)}) collective-permute-start(bf16[128,1792]{1,0:T(8,128)(2,1)} %shard_map.96.refs_3_), channel_id=1, source_target_pairs={{0,8},{1,9},{2,10},{3,11},{4,12},{5,13},{6,14},{7,15},{8,0},{9,1},... | collective-permute-start | bytes 1376264 | tf_op jit(solution)/shard_map/ppermute | solution.py:392
  36.7 24.3 %all-to-all-start.1 = ((bf16[8,32,1792]{2,1,0:T(8,128)(2,1)}), bf16[8,32,1792]{2,1,0:T(8,128)(2,1)S(1)}, u32[]{:S(2)}, u32[]{:S(2)}) async-start(bf16[8,32,1792]{2,1,0:T(8,128)(2,1)} %shard_map.98.refs_2_), calls=%async_computation.1 | async-start | bytes 1835008 | tf_op jit(solution)/shard_map/all_to_all | solution.py:522
  53.4 13.9 %collective-permute-start.8 = (bf16[128,1792]{1,0:T(8,128)(2,1)}, bf16[128,1792]{1,0:T(8,128)(2,1)S(1)}, u32[]{:S(2)}, u32[]{:S(2)}) collective-permute-start(bf16[128,1792]{1,0:T(8,128)(2,1)} %shard_map.101.refs_3_), channel_id=1, source_target_pairs={{0,4},{1,5},{2,6},{3,7},{4,0},{5,1},{6,2},{7,3},{8,12},{9,13},{10,... | collective-permute-start | bytes 1376264 | tf_op jit(solution)/shard_map/ppermute | solution.py:519
  53.5 12.7 %collective-permute-start.10 = (bf16[64,1792]{1,0:T(8,128)(2,1)S(1)}, bf16[64,1792]{1,0:T(8,128)(2,1)S(1)}, u32[]{:S(2)}, u32[]{:S(2)}) collective-permute-start(bf16[64,1792]{1,0:T(8,128)(2,1)S(1)} %copy-done.28), channel_id=1, source_target_pairs={{0,2},{1,3},{2,0},{3,1},{4,6},{5,7},{6,4},{7,5},{8,10},{9,11},{10,... | collective-permute-start | bytes 688136 | tf_op jit(solution)/shard_map/ppermute | solution.py:528
  55.0 11.2 %collective-permute-start.11 = (bf16[64,1792]{1,0:T(8,128)(2,1)S(1)}, bf16[64,1792]{1,0:T(8,128)(2,1)S(1)}, u32[]{:S(2)}, u32[]{:S(2)}) collective-permute-start(bf16[64,1792]{1,0:T(8,128)(2,1)S(1)} %copy-done.27), channel_id=1, source_target_pairs={{0,3},{1,2},{2,1},{3,0},{4,7},{5,6},{6,5},{7,4},{8,11},{9,10},{10,... | collective-permute-start | bytes 688136 | tf_op jit(solution)/shard_map/ppermute | solution.py:528
  56.4 10.2 %collective-permute-start.9 = (bf16[64,1792]{1,0:T(8,128)(2,1)S(1)}, bf16[64,1792]{1,0:T(8,128)(2,1)S(1)}, u32[]{:S(2)}, u32[]{:S(2)}) collective-permute-start(bf16[64,1792]{1,0:T(8,128)(2,1)S(1)} %copy-done.26), channel_id=1, source_target_pairs={{0,1},{1,0},{2,3},{3,2},{4,5},{5,4},{6,7},{7,6},{8,9},{9,8},{10,11... | collective-permute-start | bytes 688136 | tf_op jit(solution)/shard_map/ppermute | solution.py:528
  56.9 17.1 %collective-permute-start.5 = (bf16[256,2048]{1,0:T(8,128)(2,1)}, bf16[256,2048]{1,0:T(8,128)(2,1)}, u32[]{:S(2)}, u32[]{:S(2)}) collective-permute-start(bf16[256,2048]{1,0:T(8,128)(2,1)} %shard_map.99.refs_2_.refs_1_.refs_0_.refs_8_), channel_id=1, source_target_pairs={{0,16},{16,0},{1,17},{17,1},{2,18},{18,2},{3,19},{19,3},{4,20},{20... | collective-permute-start | bytes 3145736 | tf_op jit(solution)/shard_map/ppermute | solution.py:392
  66.1 7.9 %collective-permute-start.6 = (bf16[256,2048]{1,0:T(8,128)(2,1)}, bf16[256,2048]{1,0:T(8,128)(2,1)}, u32[]{:S(2)}, u32[]{:S(2)}) collective-permute-start(bf16[256,2048]{1,0:T(8,128)(2,1)} %shard_map.100.refs_9_.refs_2_.refs_10_), channel_id=1, source_target_pairs={{0,16},{16,0},{1,17},{17,1},{2,18},{18,2},{3,19},{19,3},{4,20},{20... | collective-permute-start | bytes 3145736 | tf_op jit(solution)/shard_map/ppermute | solution.py:392
  70.6 21.1 %collective-permute-start.12 = (bf16[64,1792]{1,0:T(8,128)(2,1)}, bf16[64,1792]{1,0:T(8,128)(2,1)}, u32[]{:S(2)}, u32[]{:S(2)}) collective-permute-start(bf16[64,1792]{1,0:T(8,128)(2,1)} %get-tuple-element.49), channel_id=1, source_target_pairs={{0,1},{1,0},{2,3},{3,2},{4,5},{5,4},{6,7},{7,6},{8,9},{9,8},{10,11... | collective-permute-start | bytes 688136 | tf_op jit(solution)/shard_map/ppermute | solution.py:528
  72.1 19.5 %collective-permute-start.13 = (bf16[64,1792]{1,0:T(8,128)(2,1)}, bf16[64,1792]{1,0:T(8,128)(2,1)}, u32[]{:S(2)}, u32[]{:S(2)}) collective-permute-start(bf16[64,1792]{1,0:T(8,128)(2,1)} %get-tuple-element.50), channel_id=1, source_target_pairs={{0,2},{1,3},{2,0},{3,1},{4,6},{5,7},{6,4},{7,5},{8,10},{9,11},{10,... | collective-permute-start | bytes 688136 | tf_op jit(solution)/shard_map/ppermute | solution.py:528
  74.0 17.6 %collective-permute-start.14 = (bf16[64,1792]{1,0:T(8,128)(2,1)}, bf16[64,1792]{1,0:T(8,128)(2,1)}, u32[]{:S(2)}, u32[]{:S(2)}) collective-permute-start(bf16[64,1792]{1,0:T(8,128)(2,1)} %get-tuple-element.51), channel_id=1, source_target_pairs={{0,3},{1,2},{2,1},{3,0},{4,7},{5,6},{6,5},{7,4},{8,11},{9,10},{10,... | collective-permute-start | bytes 688136 | tf_op jit(solution)/shard_map/ppermute | solution.py:528
  82.3 36.1 %all-to-all-start.2 = ((bf16[8,64,1792]{2,1,0:T(8,128)(2,1)}), bf16[8,64,1792]{2,1,0:T(8,128)(2,1)S(1)}, u32[]{:S(2)}, u32[]{:S(2)}) async-start(bf16[8,64,1792]{2,1,0:T(8,128)(2,1)} %shard_map.104.refs_10_), calls=%async_computation.2 | async-start | bytes 3670016 | tf_op jit(solution)/shard_map/all_to_all | solution.py:522
  86.6 31.2 %collective-permute-start.19 = (bf16[512,512]{1,0:T(8,128)(2,1)}, bf16[512,512]{1,0:T(8,128)(2,1)S(1)}, u32[]{:S(2)}, u32[]{:S(2)}) collective-permute-start(bf16[512,512]{1,0:T(8,128)(2,1)} %get-tuple-element.56), channel_id=1, source_target_pairs={{0,8},{1,9},{2,10},{3,11},{4,12},{5,13},{6,14},{7,15},{8,0},{9,1},... | collective-permute-start | bytes 1572872 | tf_op jit(solution)/shard_map/ppermute | solution.py:392
  99.4 1.8 collective-permute-start.15
  99.5 2.1 %collective-permute-start.16 = (bf16[128,1024]{1,0:T(8,128)(2,1)}, bf16[128,1024]{1,0:T(8,128)(2,1)S(1)}, u32[]{:S(2)}, u32[]{:S(2)}) collective-permute-start(bf16[128,1024]{1,0:T(8,128)(2,1)} %get-tuple-element.53.refs_2_), channel_id=1, source_target_pairs={{0,16},{16,0},{1,17},{17,1},{2,18},{18,2},{3,19},{19,3},{4,20},{20... | collective-permute-start | bytes 786440 | tf_op jit(solution)/shard_map/ppermute | solution.py:392
  100.0 2.0 %collective-permute-start.17 = (bf16[128,1024]{1,0:T(8,128)(2,1)}, bf16[128,1024]{1,0:T(8,128)(2,1)S(1)}, u32[]{:S(2)}, u32[]{:S(2)}) collective-permute-start(bf16[128,1024]{1,0:T(8,128)(2,1)} %get-tuple-element.54.refs_4_), channel_id=1, source_target_pairs={{0,16},{16,0},{1,17},{17,1},{2,18},{18,2},{3,19},{19,3},{4,20},{20... | collective-permute-start | bytes 786440 | tf_op jit(solution)/shard_map/ppermute | solution.py:392
  100.1 2.3 %collective-permute-start.18 = (bf16[128,1024]{1,0:T(8,128)(2,1)}, bf16[128,1024]{1,0:T(8,128)(2,1)S(1)}, u32[]{:S(2)}, u32[]{:S(2)}) collective-permute-start(bf16[128,1024]{1,0:T(8,128)(2,1)} %get-tuple-element.55.refs_6_), channel_id=1, source_target_pairs={{0,16},{16,0},{1,17},{17,1},{2,18},{18,2},{3,19},{19,3},{4,20},{20... | collective-permute-start | bytes 786440 | tf_op jit(solution)/shard_map/ppermute | solution.py:392
  119.6 37.0 %all-to-all-start.3 = ((bf16[8,64,1792]{2,1,0:T(8,128)(2,1)}), bf16[8,64,1792]{2,1,0:T(8,128)(2,1)}, u32[]{:S(2)}, u32[]{:S(2)}) async-start(bf16[8,64,1792]{2,1,0:T(8,128)(2,1)} %shard_map.107.refs_3_), calls=%async_computation.3 | async-start | bytes 3670016 | tf_op jit(solution)/shard_map/all_to_all | solution.py:522
  129.1 31.0 %copy-start.29 = (s32[4]{0:T(128)S(1)}, s32[4]{0:T(128)}, u32[]{:S(2)}) copy-start(s32[4]{0:T(128)} %param.13) | copy-start | bytes 52
  129.1 39.0 %copy-start.8 = (bf16[128,1792]{1,0:T(8,128)(2,1)S(1)}, bf16[128,1792]{1,0:T(8,128)(2,1)}, u32[]{:S(2)}) copy-start(bf16[128,1792]{1,0:T(8,128)(2,1)} %get-tuple-element.65.refs_3_) | copy-start | bytes 1376260
  129.1 25.5 %collective-permute-start.20 = (bf16[128,1792]{1,0:T(8,128)(2,1)}, bf16[128,1792]{1,0:T(8,128)(2,1)S(1)}, u32[]{:S(2)}, u32[]{:S(2)}) collective-permute-start(bf16[128,1792]{1,0:T(8,128)(2,1)} %shard_map.108), channel_id=1, source_target_pairs={{0,8},{1,9},{2,10},{3,11},{4,12},{5,13},{6,14},{7,15},{8,0},{9,1},... | collective-permute-start | bytes 1376264 | tf_op jit(solution)/shard_map/ppermute | solution.py:392
  129.6 38.5 %collective-permute-start.22 = (bf16[512,512]{1,0:T(8,128)(2,1)S(1)}, bf16[512,512]{1,0:T(8,128)(2,1)}, u32[]{:S(2)}, u32[]{:S(2)}) collective-permute-start(bf16[512,512]{1,0:T(8,128)(2,1)S(1)} %collective-permute-done.19.refs_2_.refs_0_), channel_id=1, source_target_pairs={{0,16},{16,0},{1,17},{17,1},{2,18},{18,2},{3,19},{19,3},{4,20},{20... | collective-permute-start | bytes 1572872 | tf_op jit(solution)/shard_map/ppermute | solution.py:392
  129.6 31.9 %collective-permute-start.23 = (bf16[128,1792]{1,0:T(8,128)(2,1)}, bf16[128,1792]{1,0:T(8,128)(2,1)S(1)}, u32[]{:S(2)}, u32[]{:S(2)}) collective-permute-start(bf16[128,1792]{1,0:T(8,128)(2,1)} %get-tuple-element.66), channel_id=1, source_target_pairs={{0,1},{1,0},{2,3},{3,2},{4,5},{5,4},{6,7},{7,6},{8,9},{9,8},{10,11... | collective-permute-start | bytes 1376264 | tf_op jit(solution)/shard_map/ppermute | solution.py:528
  131.6 36.5 %collective-permute-start.24 = (bf16[128,1792]{1,0:T(8,128)(2,1)}, bf16[128,1792]{1,0:T(8,128)(2,1)S(1)}, u32[]{:S(2)}, u32[]{:S(2)}) collective-permute-start(bf16[128,1792]{1,0:T(8,128)(2,1)} %get-tuple-element.67), channel_id=1, source_target_pairs={{0,2},{1,3},{2,0},{3,1},{4,6},{5,7},{6,4},{7,5},{8,10},{9,11},{10,... | collective-permute-start | bytes 1376264 | tf_op jit(solution)/shard_map/ppermute | solution.py:528
  133.1 35.1 %collective-permute-start.25 = (bf16[128,1792]{1,0:T(8,128)(2,1)}, bf16[128,1792]{1,0:T(8,128)(2,1)S(1)}, u32[]{:S(2)}, u32[]{:S(2)}) collective-permute-start(bf16[128,1792]{1,0:T(8,128)(2,1)} %get-tuple-element.68), channel_id=1, source_target_pairs={{0,3},{1,2},{2,1},{3,0},{4,7},{5,6},{6,5},{7,4},{8,11},{9,10},{10,... | collective-permute-start | bytes 1376264 | tf_op jit(solution)/shard_map/ppermute | solution.py:528
  158.9 21.0 %collective-permute-start.21 = (bf16[128,1792]{1,0:T(8,128)(2,1)}, bf16[128,1792]{1,0:T(8,128)(2,1)S(1)}, u32[]{:S(2)}, u32[]{:S(2)}) collective-permute-start(bf16[128,1792]{1,0:T(8,128)(2,1)} %shard_map.109.refs_7_), channel_id=1, source_target_pairs={{0,8},{1,9},{2,10},{3,11},{4,12},{5,13},{6,14},{7,15},{8,0},{9,1},... | collective-permute-start | bytes 1376264 | tf_op jit(solution)/shard_map/ppermute | solution.py:392
  (28 other events, 205.5 us)

commit v5 on v4

--- a/solution.py
+++ b/solution.py
@@ -41,7 +41,7 @@
         scratch_shapes=list(scratch),
         input_output_aliases=aliases or {},
         cost_estimate=pl.CostEstimate(flops=flops, bytes_accessed=0, transcendentals=0),
-        compiler_params=pltpu.CompilerParams(vmem_limit_bytes=52 * 1024 * 1024),
+        compiler_params=pltpu.CompilerParams(vmem_limit_bytes=50 * 1024 * 1024),
     )(*operands, *deps)
 
 
@@ -383,7 +383,7 @@
             scratch_shapes=[pltpu.VMEM((n, share, rows), BF16), pltpu.VMEM((rows, tile), BF16)],
         ),
         cost_estimate=pl.CostEstimate(flops=flops, bytes_accessed=0, transcendentals=0),
-        compiler_params=pltpu.CompilerParams(vmem_limit_bytes=52 * 1024 * 1024),
+        compiler_params=pltpu.CompilerParams(vmem_limit_bytes=50 * 1024 * 1024),
     )(where, hidden, *far_shares, own, *there, *deps)
 
 

time: 184 us -> 183 us (level)
  local copies, waits for them, and re-layouts: 10.7 us -> 17.4 us
  waiting for transfers between devices: 60.4 us -> 55.9 us
    unnamed x60 -> x68, local copies, waits for them, and re-layouts: 10.7 us -> 17.4 us
    ppermute x13, waiting for transfers between devices: 35.4 us -> 32 us  [crossed(): lax.ppermute(block, axis, [(i, (i + distance) % size) for i in range(size)])]
  transfers between devices with their start and end apart: 30 -> 30, of which waited for: 15 -> 15; matrix products, arithmetic and copies ran while one was open for 1% -> 1% of each run, Pallas kernels for 31% -> 30%
where the time goes in v5:
time: 183 us; the launch traced here: 182 us
  Pallas kernels  57.5 us (31%)
  waiting for transfers between devices  55.9 us (31%)
  starting transfers between devices  47.7 us (26%)
  local copies, waits for them, and re-layouts  17.4 us (10%)
  other arithmetic  2.15 us (1%)
    pallas_call x17, Pallas kernels, run(): pl.pallas_call(whole, out_shape=out_shape, grid=grid, in_specs=list(in_sp...  50.1 us
    ppermute x13, waiting for transfers between devices, crossed(): lax.ppermute(block, axis, [(i, (i + distance) % size) for i in range(size)])  32 us
    all_to_all x4, starting transfers between devices, exchange(): lax.all_to_all(x, 'expert', split_axis=0, concat_axis=0, tiled=True, axis...  19 us
    unnamed x68, local copies, waits for them, and re-layouts  17.4 us
    ppermute x13, starting transfers between devices, crossed(): lax.ppermute(block, axis, [(i, (i + distance) % size) for i in range(size)])  14.3 us
    ppermute x9, starting transfers between devices, over_plane(): lax.ppermute(pieces[d], 'expert', [(i, i ^ d) for i in range(experts)])  10.5 us
    ppermute x1, waiting for transfers between devices, on_device(): lax.ppermute(table, 'expert', [(i, i ^ plane ^ half) for i in range(exper...  9.25 us
    pallas_call x1, Pallas kernels, expert_grad(): pl.pallas_call(body, out_shape=pltpu.HBM((1, hidden.shape[1], width), BF1...  7.44 us
  transfers between devices with their start and end apart: 30, of which 15 were waited for; matrix products, arithmetic and copies ran while one was open for 1% of the time, Pallas kernels for 30%

profile of v5, /device:TPU:0, one launch (start us, length us, event | category | flops | bytes accessed | tf_op | source)
XLA Modules:
  0.0 182.3 jit_solution(2040981327441573939)
XLA Ops:
  0.6 3.1 %collective-permute-start.3 = (bf16[128,1792]{1,0:T(8,128)(2,1)}, bf16[128,1792]{1,0:T(8,128)(2,1)S(1)}, u32[]{:S(2)}, u32[]{:S(2)}) collective-permute-start(bf16[128,1792]{1,0:T(8,128)(2,1)} %refs_0_.1), channel_id=1, source_target_pairs={{0,4},{1,5},{2,6},{3,7},{4,0},{5,1},{6,2},{7,3},{8,12},{9,13},{10,... | collective-permute-start | bytes 1376264 | tf_op jit(solution)/shard_map/ppermute | solution.py:519
  3.7 2.6 %collective-permute-start.1 = (bf16[128,1792]{1,0:T(8,128)(2,1)}, bf16[128,1792]{1,0:T(8,128)(2,1)S(1)}, u32[]{:S(2)}, u32[]{:S(2)}) collective-permute-start(bf16[128,1792]{1,0:T(8,128)(2,1)} %refs_2_.1), channel_id=1, source_target_pairs={{0,8},{1,9},{2,10},{3,11},{4,12},{5,13},{6,14},{7,15},{8,0},{9,1},... | collective-permute-start | bytes 1376264 | tf_op jit(solution)/shard_map/ppermute | solution.py:392
  8.6 3.5 %collective-permute-start = (f32[4,128]{1,0:T(4,128)S(1)}, f32[4,128]{1,0:T(4,128)S(1)}, u32[]{:S(2)}, u32[]{:S(2)}) collective-permute-start(f32[4,128]{1,0:T(4,128)S(1)} %pad_maximum_fusion.refs_1_), channel_id=1, source_target_pairs={{0,8},{1,9},{2,10},{3,11},{4,12},{5,13},{6,14},{7,15},{8,0},{9,1},... | collective-permute-start | bytes 6152 | tf_op jit(solution)/shard_map/ppermute | solution.py:392
  14.5 3.9 %all-to-all-start = ((bf16[8,32,1792]{2,1,0:T(8,128)(2,1)}), bf16[8,32,1792]{2,1,0:T(8,128)(2,1)S(1)}, u32[]{:S(2)}, u32[]{:S(2)}) async-start(bf16[8,32,1792]{2,1,0:T(8,128)(2,1)} %get-tuple-element.37.refs_5_), calls=%async_computation | async-start | bytes 1835008 | tf_op jit(solution)/shard_map/all_to_all | solution.py:522
  18.5 9.2 %collective-permute-done.4.refs_6_.refs_2_ = f32[4,128]{1,0:T(4,128)S(1)} collective-permute-done((f32[4,128]{1,0:T(4,128)S(1)}, f32[4,128]{1,0:T(4,128)S(1)}, u32[]{:S(2)}, u32[]{:S(2)}) %collective-permute-start.4) | collective-permute-done | bytes 2080 | tf_op jit(solution)/shard_map/ppermute | solution.py:536
  27.7 2.7 %shard_map.95 = (bf16[64,1792]{1,0:T(8,128)(2,1)}, bf16[64,1792]{1,0:T(8,128)(2,1)}, bf16[64,1792]{1,0:T(8,128)(2,1)}, bf16[64,1792]{1,0:T(8,128)(2,1)}, bf16[12...) custom-call(s32[4]{0:T(128)S(1)} %pad_add_fusion.refs_0_, ...), custom_call_target="tpu_custom_call" | custom-call | tf_op jit(solution)/shard_map/pallas_call | solution.py:35
  34.0 1.5 shard_map.97
  36.7 3.8 %all-to-all-start.1 = ((bf16[8,32,1792]{2,1,0:T(8,128)(2,1)}), bf16[8,32,1792]{2,1,0:T(8,128)(2,1)S(1)}, u32[]{:S(2)}, u32[]{:S(2)}) async-start(bf16[8,32,1792]{2,1,0:T(8,128)(2,1)} %shard_map.98.refs_2_), calls=%async_computation.1 | async-start | bytes 1835008 | tf_op jit(solution)/shard_map/all_to_all | solution.py:522
  40.5 5.1 %shard_map.99.refs_2_.refs_1_.refs_0_.refs_8_ = bf16[256,2048]{1,0:T(8,128)(2,1)} custom-call(bf16[8,32,1792]{2,1,0:T(8,128)(2,1)S(1)} %all-to-all-done.refs_1_.refs_0_, bf16[1,1792,2048]{2,1,0:T(8,128)(2,1)} %refs_12_.1, bf16[8,32,1792]{2,1,0:T(8,128)(2,1)S(1)} %copy-done.3), custom_call_target="tpu_custom_call" | custom-call | tf_op jit(solution)/shard_map/pallas_call | solution.py:35
  45.6 7.7 %collective-permute-done.7.refs_0_ = bf16[128,1792]{1,0:T(8,128)(2,1)S(1)} collective-permute-done((bf16[128,1792]{1,0:T(8,128)(2,1)}, bf16[128,1792]{1,0:T(8,128)(2,1)S(1)}, u32[]{:S(2)}, u32[]{:S(2)}) %collective-permute-start.7) | collective-permute-done | bytes 458784 | tf_op jit(solution)/shard_map/ppermute | solution.py:392
  54.1 1.5 collective-permute-start.10
  57.6 3.1 %all-to-all-done.1.refs_0_.refs_1_ = bf16[8,32,1792]{2,1,0:T(8,128)(2,1)S(1)} async-done(((bf16[8,32,1792]{2,1,0:T(8,128)(2,1)}), bf16[8,32,1792]{2,1,0:T(8,128)(2,1)S(1)}, u32[]{:S(2)}, u32[]{:S(2)}) %all-to-all-start.1) | async-done | bytes 917536 | tf_op jit(solution)/shard_map/all_to_all | solution.py:522
  60.7 5.1 %shard_map.100.refs_9_.refs_2_.refs_10_ = bf16[256,2048]{1,0:T(8,128)(2,1)} custom-call(bf16[8,32,1792]{2,1,0:T(8,128)(2,1)S(1)} %all-to-all-done.1.refs_0_.refs_1_, bf16[1,1792,2048]{2,1,0:T(8,128)(2,1)} %refs_12_.1, bf16[256,2048]{1,0:T(8,128)(2,1)} %shard_map.99.refs_2_.refs_1_.refs_0_.refs_8_), custom_call_target="tpu_custom_call" | custom-call | tf_op jit(solution)/shard_map/pallas_call | solution.py:35
  69.6 2.7 %shard_map.102 = (bf16[64,1792]{1,0:T(8,128)(2,1)}, bf16[64,1792]{1,0:T(8,128)(2,1)}, bf16[64,1792]{1,0:T(8,128)(2,1)}, bf16[64,1792]{1,0:T(8,128)(2,1)}, bf16[1...) custom-call(s32[4]{0:T(128)S(1)} %pad_add_fusion.refs_0_, ...), custom_call_target="tpu_custom_call", output_to_operand_aliasing={{4}: (5, {}), {5}: (6, {}), {6}: (7, {}), {7}: (8, {})} | custom-call | flops 49999998976 | tf_op jit(solution)/shard_map/pallas_call | solution.py:35
  72.3 1.5 collective-permute-start.12
  73.8 1.9 %collective-permute-start.13 = (bf16[64,1792]{1,0:T(8,128)(2,1)}, bf16[64,1792]{1,0:T(8,128)(2,1)}, u32[]{:S(2)}, u32[]{:S(2)}) collective-permute-start(bf16[64,1792]{1,0:T(8,128)(2,1)} %get-tuple-element.50), channel_id=1, source_target_pairs={{0,2},{1,3},{2,0},{3,1},{4,6},{5,7},{6,4},{7,5},{8,10},{9,11},{10,... | collective-permute-start | bytes 688136 | tf_op jit(solution)/shard_map/ppermute | solution.py:528
  76.7 6.9 %shard_map.103 = (bf16[512,1024]{1,0:T(8,128)(2,1)}, bf16[512,512]{1,0:T(8,128)(2,1)}, bf16[8,64,1792]{2,1,0:T(8,128)(2,1)}) custom-call(bf16[256,2048]{1,0:T(8,128)(2,1)} %shard_map.99.refs_2_.refs_1_.refs_0_.refs_8_, bf16[256,2048]{1,0:T(8,128)(2,1)} %collective-permute-done.5.refs_1_.refs_9_, bf16[256,2048]{1,0:T(8,128)(2,1)S(1)} %copy-done.2, ...), custom_call_target="tpu_custom_call" | custom-call | tf_op jit(solution)/shard_map/pallas_call | solution.py:35
  83.6 4.3 %all-to-all-start.2 = ((bf16[8,64,1792]{2,1,0:T(8,128)(2,1)}), bf16[8,64,1792]{2,1,0:T(8,128)(2,1)S(1)}, u32[]{:S(2)}, u32[]{:S(2)}) async-start(bf16[8,64,1792]{2,1,0:T(8,128)(2,1)} %shard_map.104.refs_10_), calls=%async_computation.2 | async-start | bytes 3670016 | tf_op jit(solution)/shard_map/all_to_all | solution.py:522
  87.9 5.0 %collective-permute-start.19 = (bf16[512,512]{1,0:T(8,128)(2,1)}, bf16[512,512]{1,0:T(8,128)(2,1)S(1)}, u32[]{:S(2)}, u32[]{:S(2)}) collective-permute-start(bf16[512,512]{1,0:T(8,128)(2,1)} %get-tuple-element.56), channel_id=1, source_target_pairs={{0,8},{1,9},{2,10},{3,11},{4,12},{5,13},{6,14},{7,15},{8,0},{9,1},... | collective-permute-start | bytes 1572872 | tf_op jit(solution)/shard_map/ppermute | solution.py:392
  92.9 1.5 copy-done.4
  95.4 6.9 %shard_map.105 = (bf16[128,1024]{1,0:T(8,128)(2,1)}, bf16[128,1024]{1,0:T(8,128)(2,1)}, bf16[128,1024]{1,0:T(8,128)(2,1)}, bf16[128,1024]{1,0:T(8,128)(2,1)}, bf16[512,1792]{1,0:T(8,128)(2,1)}) custom-call(s32[4]{0:T(128)S(1)} %pad_add_fusion.refs_0_, bf16[64,1792]{1,0:T(8,128)(2,1)S(1)} %copy-done.16, bf16[64,1792]{1,0:T(8,128)(2,1)S(1)} %copy-done.29, ...), custom_call_target="tpu_custom_call" | custom-call | flops 49999998976 | tf_op jit(solution)/shard_map/pallas_call | solution.py:35
  109.0 10.7 %shard_map.106.refs_0_ = bf16[8,64,1792]{2,1,0:T(8,128)(2,1)} custom-call(bf16[128,1024]{1,0:T(8,128)(2,1)S(1)} %copy-done.11, bf16[128,1024]{1,0:T(8,128)(2,1)S(1)} %collective-permute-done.15.refs_1_, bf16[128,1024]{1,0:T(8,128)(2,1)S(1)} %copy-done.12, bf16[128,1024]{1,0:T(8,128)(2,1)S(1)} %collective-permute-done.16.refs_3_, ...), custom_call_target="tpu_custom_call" | custom-call | tf_op jit(solution)/shard_map/pallas_call | solution.py:35
  120.5 7.1 %all-to-all-start.3 = ((bf16[8,64,1792]{2,1,0:T(8,128)(2,1)}), bf16[8,64,1792]{2,1,0:T(8,128)(2,1)}, u32[]{:S(2)}, u32[]{:S(2)}) async-start(bf16[8,64,1792]{2,1,0:T(8,128)(2,1)} %shard_map.107.refs_3_), calls=%async_computation.3 | async-start | bytes 3670016 | tf_op jit(solution)/shard_map/all_to_all | solution.py:522
  127.6 1.5 copy-done
  131.0 2.0 %collective-permute-start.23 = (bf16[128,1792]{1,0:T(8,128)(2,1)}, bf16[128,1792]{1,0:T(8,128)(2,1)}, u32[]{:S(2)}, u32[]{:S(2)}) collective-permute-start(bf16[128,1792]{1,0:T(8,128)(2,1)} %get-tuple-element.66), channel_id=1, source_target_pairs={{0,1},{1,0},{2,3},{3,2},{4,5},{5,4},{6,7},{7,6},{8,9},{9,8},{10,11... | collective-permute-start | bytes 1376264 | tf_op jit(solution)/shard_map/ppermute | solution.py:528
  134.5 20.8 %collective-permute-done.20.refs_2_.refs_5_ = bf16[128,1792]{1,0:T(8,128)(2,1)S(1)} collective-permute-done((bf16[128,1792]{1,0:T(8,128)(2,1)}, bf16[128,1792]{1,0:T(8,128)(2,1)S(1)}, u32[]{:S(2)}, u32[]{:S(2)}) %collective-permute-start.20) | collective-permute-done | bytes 458784 | tf_op jit(solution)/shard_map/ppermute | solution.py:392
  155.2 2.2 %all-to-all-done.3.refs_0_.refs_1_ = bf16[8,64,1792]{2,1,0:T(8,128)(2,1)} async-done(((bf16[8,64,1792]{2,1,0:T(8,128)(2,1)}), bf16[8,64,1792]{2,1,0:T(8,128)(2,1)}, u32[]{:S(2)}, u32[]{:S(2)}) %all-to-all-start.3) | async-done | bytes 1835040 | tf_op jit(solution)/shard_map/all_to_all | solution.py:522
  157.5 2.2 %shard_map.109.refs_7_ = bf16[128,1792]{1,0:T(8,128)(2,1)} custom-call(bf16[8,64,1792]{2,1,0:T(8,128)(2,1)} %all-to-all-done.3.refs_0_.refs_1_, bf16[128,256]{1,0:T(8,128)(2,1)S(1)} %copy-done.24, bf16[128,1792]{1,0:T(8,128)(2,1)S(1)} %collective-permute-done.20.refs_2_.refs_5_), custom_call_target="tpu_custom_call" | custom-call | tf_op jit(solution)/shard_map/pallas_call | solution.py:35
  162.1 6.4 %collective-permute-done.24.refs_5_ = bf16[128,1792]{1,0:T(8,128)(2,1)} collective-permute-done((bf16[128,1792]{1,0:T(8,128)(2,1)}, bf16[128,1792]{1,0:T(8,128)(2,1)}, u32[]{:S(2)}, u32[]{:S(2)}) %collective-permute-start.24) | collective-permute-done | bytes 458784 | tf_op jit(solution)/shard_map/ppermute | solution.py:528
  170.6 7.4 %shard_map.110.refs_7_ = bf16[1,1024,1792]{2,1,0:T(8,128)(2,1)} custom-call(s32[3]{0:T(128)S(1)} %pad_add_fusion.1.where_ref, bf16[512,1024]{1,0:T(8,128)(2,1)} %get-tuple-element.63.hidden_ref, bf16[512,512]{1,0:T(8,128)(2,1)S(1)} %collective-permute-done.19.refs_2_.refs_0_, bf16[512,512]{1,0:T(8,128)(2,1)S(1)} %collective-permute-done.22.refs_1_, ...), custom_call_target="tpu_custom_call" | custom-call | tf_op jit(solution)/shard_map/pallas_call | solution.py:371
  178.0 1.6 collective-permute-done.21.refs_6_
  179.6 2.6 %shard_map.111 = (bf16[128,1792]{1,0:T(8,128)(2,1)}, bf16[128,1792]{1,0:T(8,128)(2,1)}) custom-call(bf16[8,64,1792]{2,1,0:T(8,128)(2,1)S(1)} %all-to-all-done.2.refs_1_.refs_0_, bf16[8,64,1792]{2,1,0:T(8,128)(2,1)} %all-to-all-done.3.refs_0_.refs_1_, bf16[128,256]{1,0:T(8,128)(2,1)S(1)} %copy-done.20, bf16[128,256]{1,0:T(8,128)(2,1)S(1)} %copy-done.21, ...), custom_call_target="tpu_custom_call" | custom-call | tf_op jit(solution)/shard_map/pallas_call | solution.py:35
  (119 shorter events, 32.8 us)
Async XLA Ops:
  0.6 27.1 %collective-permute-start.3 = (bf16[128,1792]{1,0:T(8,128)(2,1)}, bf16[128,1792]{1,0:T(8,128)(2,1)S(1)}, u32[]{:S(2)}, u32[]{:S(2)}) collective-permute-start(bf16[128,1792]{1,0:T(8,128)(2,1)} %refs_0_.1), channel_id=1, source_target_pairs={{0,4},{1,5},{2,6},{3,7},{4,0},{5,1},{6,2},{7,3},{8,12},{9,13},{10,... | collective-permute-start | bytes 1376264 | tf_op jit(solution)/shard_map/ppermute | solution.py:519
  3.7 26.7 %collective-permute-start.1 = (bf16[128,1792]{1,0:T(8,128)(2,1)}, bf16[128,1792]{1,0:T(8,128)(2,1)S(1)}, u32[]{:S(2)}, u32[]{:S(2)}) collective-permute-start(bf16[128,1792]{1,0:T(8,128)(2,1)} %refs_2_.1), channel_id=1, source_target_pairs={{0,8},{1,9},{2,10},{3,11},{4,12},{5,13},{6,14},{7,15},{8,0},{9,1},... | collective-permute-start | bytes 1376264 | tf_op jit(solution)/shard_map/ppermute | solution.py:392
  7.7 20.0 %collective-permute-start.4 = (f32[4,128]{1,0:T(4,128)S(1)}, f32[4,128]{1,0:T(4,128)S(1)}, u32[]{:S(2)}, u32[]{:S(2)}) collective-permute-start(f32[4,128]{1,0:T(4,128)S(1)} %pad_maximum_fusion.refs_1_), channel_id=1, source_target_pairs={{0,12},{1,13},{2,14},{3,15},{4,8},{5,9},{6,10},{7,11},{8,4},{9,5},... | collective-permute-start | bytes 6152 | tf_op jit(solution)/shard_map/ppermute | solution.py:536
  7.7 20.0 %collective-permute-start.2 = (f32[4,128]{1,0:T(4,128)S(1)}, f32[4,128]{1,0:T(4,128)S(1)}, u32[]{:S(2)}, u32[]{:S(2)}) collective-permute-start(f32[4,128]{1,0:T(4,128)S(1)} %pad_maximum_fusion.refs_1_), channel_id=1, source_target_pairs={{0,4},{1,5},{2,6},{3,7},{4,0},{5,1},{6,2},{7,3},{8,12},{9,13},{10,... | collective-permute-start | bytes 6152 | tf_op jit(solution)/shard_map/ppermute | solution.py:519
  8.6 24.4 %collective-permute-start = (f32[4,128]{1,0:T(4,128)S(1)}, f32[4,128]{1,0:T(4,128)S(1)}, u32[]{:S(2)}, u32[]{:S(2)}) collective-permute-start(f32[4,128]{1,0:T(4,128)S(1)} %pad_maximum_fusion.refs_1_), channel_id=1, source_target_pairs={{0,8},{1,9},{2,10},{3,11},{4,12},{5,13},{6,14},{7,15},{8,0},{9,1},... | collective-permute-start | bytes 6152 | tf_op jit(solution)/shard_map/ppermute | solution.py:392
  14.5 22.2 %all-to-all-start = ((bf16[8,32,1792]{2,1,0:T(8,128)(2,1)}), bf16[8,32,1792]{2,1,0:T(8,128)(2,1)S(1)}, u32[]{:S(2)}, u32[]{:S(2)}) async-start(bf16[8,32,1792]{2,1,0:T(8,128)(2,1)} %get-tuple-element.37.refs_5_), calls=%async_computation | async-start | bytes 1835008 | tf_op jit(solution)/shard_map/all_to_all | solution.py:522
  32.2 21.1 %collective-permute-start.7 = (bf16[128,1792]{1,0:T(8,128)(2,1)}, bf16[128,1792]{1,0:T(8,128)(2,1)S(1)}, u32[]{:S(2)}, u32[]{:S(2)}) collective-permute-start(bf16[128,1792]{1,0:T(8,128)(2,1)} %shard_map.96.refs_3_), channel_id=1, source_target_pairs={{0,8},{1,9},{2,10},{3,11},{4,12},{5,13},{6,14},{7,15},{8,0},{9,1},... | collective-permute-start | bytes 1376264 | tf_op jit(solution)/shard_map/ppermute | solution.py:392
  36.7 24.0 %all-to-all-start.1 = ((bf16[8,32,1792]{2,1,0:T(8,128)(2,1)}), bf16[8,32,1792]{2,1,0:T(8,128)(2,1)S(1)}, u32[]{:S(2)}, u32[]{:S(2)}) async-start(bf16[8,32,1792]{2,1,0:T(8,128)(2,1)} %shard_map.98.refs_2_), calls=%async_computation.1 | async-start | bytes 1835008 | tf_op jit(solution)/shard_map/all_to_all | solution.py:522
  54.1 13.3 %collective-permute-start.8 = (bf16[128,1792]{1,0:T(8,128)(2,1)}, bf16[128,1792]{1,0:T(8,128)(2,1)S(1)}, u32[]{:S(2)}, u32[]{:S(2)}) collective-permute-start(bf16[128,1792]{1,0:T(8,128)(2,1)} %shard_map.101.refs_3_), channel_id=1, source_target_pairs={{0,4},{1,5},{2,6},{3,7},{4,0},{5,1},{6,2},{7,3},{8,12},{9,13},{10,... | collective-permute-start | bytes 1376264 | tf_op jit(solution)/shard_map/ppermute | solution.py:519
  54.1 12.3 %collective-permute-start.10 = (bf16[64,1792]{1,0:T(8,128)(2,1)S(1)}, bf16[64,1792]{1,0:T(8,128)(2,1)S(1)}, u32[]{:S(2)}, u32[]{:S(2)}) collective-permute-start(bf16[64,1792]{1,0:T(8,128)(2,1)S(1)} %copy-done.32), channel_id=1, source_target_pairs={{0,2},{1,3},{2,0},{3,1},{4,6},{5,7},{6,4},{7,5},{8,10},{9,11},{10,... | collective-permute-start | bytes 688136 | tf_op jit(solution)/shard_map/ppermute | solution.py:528
  55.6 10.8 %collective-permute-start.11 = (bf16[64,1792]{1,0:T(8,128)(2,1)S(1)}, bf16[64,1792]{1,0:T(8,128)(2,1)S(1)}, u32[]{:S(2)}, u32[]{:S(2)}) collective-permute-start(bf16[64,1792]{1,0:T(8,128)(2,1)S(1)} %copy-done.31), channel_id=1, source_target_pairs={{0,3},{1,2},{2,1},{3,0},{4,7},{5,6},{6,5},{7,4},{8,11},{9,10},{10,... | collective-permute-start | bytes 688136 | tf_op jit(solution)/shard_map/ppermute | solution.py:528
  57.1 9.6 %collective-permute-start.9 = (bf16[64,1792]{1,0:T(8,128)(2,1)S(1)}, bf16[64,1792]{1,0:T(8,128)(2,1)S(1)}, u32[]{:S(2)}, u32[]{:S(2)}) collective-permute-start(bf16[64,1792]{1,0:T(8,128)(2,1)S(1)} %copy-done.30), channel_id=1, source_target_pairs={{0,1},{1,0},{2,3},{3,2},{4,5},{5,4},{6,7},{7,6},{8,9},{9,8},{10,11... | collective-permute-start | bytes 688136 | tf_op jit(solution)/shard_map/ppermute | solution.py:528
  57.6 18.2 %collective-permute-start.5 = (bf16[256,2048]{1,0:T(8,128)(2,1)}, bf16[256,2048]{1,0:T(8,128)(2,1)}, u32[]{:S(2)}, u32[]{:S(2)}) collective-permute-start(bf16[256,2048]{1,0:T(8,128)(2,1)} %shard_map.99.refs_2_.refs_1_.refs_0_.refs_8_), channel_id=1, source_target_pairs={{0,16},{16,0},{1,17},{17,1},{2,18},{18,2},{3,19},{19,3},{4,20},{20... | collective-permute-start | bytes 3145736 | tf_op jit(solution)/shard_map/ppermute | solution.py:392
  66.4 9.4 %collective-permute-start.6 = (bf16[256,2048]{1,0:T(8,128)(2,1)}, bf16[256,2048]{1,0:T(8,128)(2,1)}, u32[]{:S(2)}, u32[]{:S(2)}) collective-permute-start(bf16[256,2048]{1,0:T(8,128)(2,1)} %shard_map.100.refs_9_.refs_2_.refs_10_), channel_id=1, source_target_pairs={{0,16},{16,0},{1,17},{17,1},{2,18},{18,2},{3,19},{19,3},{4,20},{20... | collective-permute-start | bytes 3145736 | tf_op jit(solution)/shard_map/ppermute | solution.py:392
  72.3 20.6 %collective-permute-start.12 = (bf16[64,1792]{1,0:T(8,128)(2,1)}, bf16[64,1792]{1,0:T(8,128)(2,1)}, u32[]{:S(2)}, u32[]{:S(2)}) collective-permute-start(bf16[64,1792]{1,0:T(8,128)(2,1)} %get-tuple-element.49), channel_id=1, source_target_pairs={{0,1},{1,0},{2,3},{3,2},{4,5},{5,4},{6,7},{7,6},{8,9},{9,8},{10,11... | collective-permute-start | bytes 688136 | tf_op jit(solution)/shard_map/ppermute | solution.py:528
  73.8 19.1 %collective-permute-start.13 = (bf16[64,1792]{1,0:T(8,128)(2,1)}, bf16[64,1792]{1,0:T(8,128)(2,1)}, u32[]{:S(2)}, u32[]{:S(2)}) collective-permute-start(bf16[64,1792]{1,0:T(8,128)(2,1)} %get-tuple-element.50), channel_id=1, source_target_pairs={{0,2},{1,3},{2,0},{3,1},{4,6},{5,7},{6,4},{7,5},{8,10},{9,11},{10,... | collective-permute-start | bytes 688136 | tf_op jit(solution)/shard_map/ppermute | solution.py:528
  75.7 17.2 %collective-permute-start.14 = (bf16[64,1792]{1,0:T(8,128)(2,1)}, bf16[64,1792]{1,0:T(8,128)(2,1)}, u32[]{:S(2)}, u32[]{:S(2)}) collective-permute-start(bf16[64,1792]{1,0:T(8,128)(2,1)} %get-tuple-element.51), channel_id=1, source_target_pairs={{0,3},{1,2},{2,1},{3,0},{4,7},{5,6},{6,5},{7,4},{8,11},{9,10},{10,... | collective-permute-start | bytes 688136 | tf_op jit(solution)/shard_map/ppermute | solution.py:528
  83.6 36.8 %all-to-all-start.2 = ((bf16[8,64,1792]{2,1,0:T(8,128)(2,1)}), bf16[8,64,1792]{2,1,0:T(8,128)(2,1)S(1)}, u32[]{:S(2)}, u32[]{:S(2)}) async-start(bf16[8,64,1792]{2,1,0:T(8,128)(2,1)} %shard_map.104.refs_10_), calls=%async_computation.2 | async-start | bytes 3670016 | tf_op jit(solution)/shard_map/all_to_all | solution.py:522
  87.9 31.8 %collective-permute-start.19 = (bf16[512,512]{1,0:T(8,128)(2,1)}, bf16[512,512]{1,0:T(8,128)(2,1)S(1)}, u32[]{:S(2)}, u32[]{:S(2)}) collective-permute-start(bf16[512,512]{1,0:T(8,128)(2,1)} %get-tuple-element.56), channel_id=1, source_target_pairs={{0,8},{1,9},{2,10},{3,11},{4,12},{5,13},{6,14},{7,15},{8,0},{9,1},... | collective-permute-start | bytes 1572872 | tf_op jit(solution)/shard_map/ppermute | solution.py:392
  102.2 1.8 collective-permute-start.15
  102.3 2.1 %collective-permute-start.16 = (bf16[128,1024]{1,0:T(8,128)(2,1)}, bf16[128,1024]{1,0:T(8,128)(2,1)S(1)}, u32[]{:S(2)}, u32[]{:S(2)}) collective-permute-start(bf16[128,1024]{1,0:T(8,128)(2,1)} %get-tuple-element.53.refs_2_), channel_id=1, source_target_pairs={{0,16},{16,0},{1,17},{17,1},{2,18},{18,2},{3,19},{19,3},{4,20},{20... | collective-permute-start | bytes 786440 | tf_op jit(solution)/shard_map/ppermute | solution.py:392
  102.8 2.0 %collective-permute-start.17 = (bf16[128,1024]{1,0:T(8,128)(2,1)}, bf16[128,1024]{1,0:T(8,128)(2,1)S(1)}, u32[]{:S(2)}, u32[]{:S(2)}) collective-permute-start(bf16[128,1024]{1,0:T(8,128)(2,1)} %get-tuple-element.54.refs_4_), channel_id=1, source_target_pairs={{0,16},{16,0},{1,17},{17,1},{2,18},{18,2},{3,19},{19,3},{4,20},{20... | collective-permute-start | bytes 786440 | tf_op jit(solution)/shard_map/ppermute | solution.py:392
  102.9 2.3 %collective-permute-start.18 = (bf16[128,1024]{1,0:T(8,128)(2,1)}, bf16[128,1024]{1,0:T(8,128)(2,1)S(1)}, u32[]{:S(2)}, u32[]{:S(2)}) collective-permute-start(bf16[128,1024]{1,0:T(8,128)(2,1)} %get-tuple-element.55.refs_6_), channel_id=1, source_target_pairs={{0,16},{16,0},{1,17},{17,1},{2,18},{18,2},{3,19},{19,3},{4,20},{20... | collective-permute-start | bytes 786440 | tf_op jit(solution)/shard_map/ppermute | solution.py:392
  120.5 37.0 %all-to-all-start.3 = ((bf16[8,64,1792]{2,1,0:T(8,128)(2,1)}), bf16[8,64,1792]{2,1,0:T(8,128)(2,1)}, u32[]{:S(2)}, u32[]{:S(2)}) async-start(bf16[8,64,1792]{2,1,0:T(8,128)(2,1)} %shard_map.107.refs_3_), calls=%async_computation.3 | async-start | bytes 3670016 | tf_op jit(solution)/shard_map/all_to_all | solution.py:522
  129.1 28.4 %copy-start.24 = (bf16[128,256]{1,0:T(8,128)(2,1)S(1)}, bf16[128,256]{1,0:T(8,128)(2,1)}, u32[]{:S(2)}) copy-start(bf16[128,256]{1,0:T(8,128)(2,1)} %get-tuple-element.62.refs_1_) | copy-start | bytes 196612
  130.5 30.2 %copy-start.33 = (s32[4]{0:T(128)S(1)}, s32[4]{0:T(128)}, u32[]{:S(2)}) copy-start(s32[4]{0:T(128)} %param.13) | copy-start | bytes 52
  130.5 24.7 %collective-permute-start.20 = (bf16[128,1792]{1,0:T(8,128)(2,1)}, bf16[128,1792]{1,0:T(8,128)(2,1)S(1)}, u32[]{:S(2)}, u32[]{:S(2)}) collective-permute-start(bf16[128,1792]{1,0:T(8,128)(2,1)} %shard_map.108), channel_id=1, source_target_pairs={{0,8},{1,9},{2,10},{3,11},{4,12},{5,13},{6,14},{7,15},{8,0},{9,1},... | collective-permute-start | bytes 1376264 | tf_op jit(solution)/shard_map/ppermute | solution.py:392
  131.0 37.6 %collective-permute-start.22 = (bf16[512,512]{1,0:T(8,128)(2,1)S(1)}, bf16[512,512]{1,0:T(8,128)(2,1)S(1)}, u32[]{:S(2)}, u32[]{:S(2)}) collective-permute-start(bf16[512,512]{1,0:T(8,128)(2,1)S(1)} %collective-permute-done.19.refs_2_.refs_0_), channel_id=1, source_target_pairs={{0,16},{16,0},{1,17},{17,1},{2,18},{18,2},{3,19},{19,3},{4,20},{20... | collective-permute-start | bytes 1572872 | tf_op jit(solution)/shard_map/ppermute | solution.py:392
  131.0 31.1 %collective-permute-start.23 = (bf16[128,1792]{1,0:T(8,128)(2,1)}, bf16[128,1792]{1,0:T(8,128)(2,1)}, u32[]{:S(2)}, u32[]{:S(2)}) collective-permute-start(bf16[128,1792]{1,0:T(8,128)(2,1)} %get-tuple-element.66), channel_id=1, source_target_pairs={{0,1},{1,0},{2,3},{3,2},{4,5},{5,4},{6,7},{7,6},{8,9},{9,8},{10,11... | collective-permute-start | bytes 1376264 | tf_op jit(solution)/shard_map/ppermute | solution.py:528
  133.0 35.5 %collective-permute-start.24 = (bf16[128,1792]{1,0:T(8,128)(2,1)}, bf16[128,1792]{1,0:T(8,128)(2,1)}, u32[]{:S(2)}, u32[]{:S(2)}) collective-permute-start(bf16[128,1792]{1,0:T(8,128)(2,1)} %get-tuple-element.67), channel_id=1, source_target_pairs={{0,2},{1,3},{2,0},{3,1},{4,6},{5,7},{6,4},{7,5},{8,10},{9,11},{10,... | collective-permute-start | bytes 1376264 | tf_op jit(solution)/shard_map/ppermute | solution.py:528
  134.4 34.1 %collective-permute-start.25 = (bf16[128,1792]{1,0:T(8,128)(2,1)}, bf16[128,1792]{1,0:T(8,128)(2,1)}, u32[]{:S(2)}, u32[]{:S(2)}) collective-permute-start(bf16[128,1792]{1,0:T(8,128)(2,1)} %get-tuple-element.68), channel_id=1, source_target_pairs={{0,3},{1,2},{2,1},{3,0},{4,7},{5,6},{6,5},{7,4},{8,11},{9,10},{10,... | collective-permute-start | bytes 1376264 | tf_op jit(solution)/shard_map/ppermute | solution.py:528
  159.7 19.9 %collective-permute-start.21 = (bf16[128,1792]{1,0:T(8,128)(2,1)}, bf16[128,1792]{1,0:T(8,128)(2,1)}, u32[]{:S(2)}, u32[]{:S(2)}) collective-permute-start(bf16[128,1792]{1,0:T(8,128)(2,1)} %shard_map.109.refs_7_), channel_id=1, source_target_pairs={{0,8},{1,9},{2,10},{3,11},{4,12},{5,13},{6,14},{7,15},{8,0},{9,1},... | collective-permute-start | bytes 1376264 | tf_op jit(solution)/shard_map/ppermute | solution.py:392
  (32 other events, 168.0 us)
